TPU v7x, 32 devices: a whole 2x2x4 slice. The times are simulated.
32 devices in a mesh: expert: 4 (over y, x), fsdp: 8 (over z, core).
Axes of the slice: x: 2, y: 2, z: 4, core: 2. Of those that a mesh axis runs over, the one named last changes fastest.
Arguments:
- branch_wo: bfloat16 [4, 4096, 4096], P('expert', 'fsdp'), may hold values from -3 to 3
- context: bfloat16 [1024, 4096], P('fsdp', 'expert'), may hold values from -6 to 6
- residual: bfloat16 [1024, 4096], P('fsdp', 'expert'), may hold values from -160 to 160
- norm_gain: bfloat16 [4096], P('expert'), may hold values from 0.25 to 1.75
- router_w: bfloat16 [4096, 4], P('expert'), may hold values from -0.1875 to 0.1875
- gate_w: bfloat16 [4, 4096, 8192], P('expert', None, 'fsdp'), may hold values from -0.09375 to 0.09375
- up_w: bfloat16 [4, 4096, 8192], P('expert', None, 'fsdp'), may hold values from -0.09375 to 0.09375
- expert_ids: int32 [1024, 2], P('fsdp'), may hold values from 0 to 3, as said below
- slot_ids: int32 [1024, 2], P('fsdp'), may hold values from 0 to 95, as said below
- cot_hidden: bfloat16 [4, 768, 8192], P('expert', None, 'fsdp'), may hold values from -1.1953125 to 1.1953125
Outputs:
- merged_wo: bfloat16 [4096, 4096], P('fsdp', 'expert')
- hidden: bfloat16 [4, 768, 8192], P('expert', None, 'fsdp')
- grad_gate: bfloat16 [4, 4096, 8192], P('expert', None, 'fsdp')
- grad_up: bfloat16 [4, 4096, 8192], P('expert', None, 'fsdp')
Inputs may be any that keep to these rules, and one draw needn't show every extreme that they name: expert_ids[t, 0] and expert_ids[t, 1] differ. Within each aligned block of 128 tokens (the tokens of one index of fsdp) no expert is named more than 96 times, and some expert is named exactly 96 times in every block. Within each aligned block of 128 tokens the pairs (expert_ids[t, k], slot_ids[t, k]) are all different, and an expert named c times in the block uses exactly the slots 0 to c - 1.
All inputs are finite; a program needn't handle non-finite values.
Results may differ from a plain program's by a relative error of at most 0.015.
Values may be sent and summed in bfloat16 or wider, within the bound.
No kernel may reach another device: no remote copies, remote signals or barrier semaphores. Data moves between devices by JAX's collectives and lax.ppermute only.
A program may use at most 128 MiB of HBM per device.

v0:
```python
import functools

import jax
import jax.numpy as jnp
from jax import lax
from jax.experimental import pallas as pl
from jax.experimental.pallas import tpu as pltpu
from jax.sharding import PartitionSpec as P

CHUNKS = 2
VMEM_LIMIT = 56 * 1024 * 1024


def exchange(value, axis, offset):
    size = lax.axis_size(axis)
    return lax.ppermute(value, axis, [(i, i ^ offset) for i in range(size)])


def pick(value, index, axis):
    return lax.dynamic_index_in_dim(value, index, axis, keepdims=False)


def after(value, *others):
    return lax.optimization_barrier((value, others))[0]


def bits_of(size):
    return size.bit_length() - 1


def whole(shape):
    return pl.BlockSpec(shape, lambda *_: (0,) * len(shape))


def smem():
    return pl.BlockSpec(memory_space=pltpu.SMEM)


def params():
    return pltpu.CompilerParams(vmem_limit_bytes=VMEM_LIMIT)


def signs_kernel(experts, position_ref, ids_ref, out_ref):
    blocks, capacity, lanes = out_ref.shape
    tokens = ids_ref.shape[2]
    expert = position_ref[0]
    slots = lax.broadcasted_iota(jnp.int32, (capacity, tokens), 0)
    rows = lax.broadcasted_iota(jnp.int32, (lanes, tokens), 0)
    last = lax.broadcasted_iota(jnp.int32, (capacity, lanes), 1) == lanes - 1
    for b in range(blocks):
        ids = ids_ref[b]
        e0, e1, s0, s1 = ids[0:1], ids[1:2], ids[2:3], ids[3:4]
        hit0 = jnp.where((e0 == expert) & (s0 == slots), 1.0, 0.0)
        hit1 = jnp.where((e1 == expert) & (s1 == slots), 1.0, 0.0)
        table = jnp.where(e0 == rows - 1, 1.0, 0.0) - jnp.where(e1 == rows - 1, 1.0, 0.0)
        signs = lax.dot_general(
            (hit0 - hit1).astype(jnp.bfloat16),
            table.astype(jnp.bfloat16),
            (((1,), (1,)), ((), ())),
            preferred_element_type=jnp.float32,
        )
        filled = jnp.sum(hit0 + hit1, axis=1, keepdims=True)
        out_ref[b] = jnp.where(last, filled, signs)


def pack_kernel(position_ref, low_ref, high_ref, low_out, high_out):
    low_out[0] = low_ref[...]
    high_out[0] = high_ref[...]


def pack(position, branch, c, experts):
    half = branch.shape[0] // 2
    part = branch.shape[1] // experts // CHUNKS
    others = experts // 2

    def low(j, position_ref):
        return (0, (2 * j + 1 - position_ref[0] % 2) * CHUNKS + c)

    def high(j, position_ref):
        return (1, (j + others * (1 - position_ref[0] // others)) * CHUNKS + c)

    block = pl.BlockSpec((1, half, part), lambda j, position_ref: (j, 0, 0))
    shape = jax.ShapeDtypeStruct((others, half, part), jnp.bfloat16)
    return pl.pallas_call(
        pack_kernel,
        out_shape=(shape, shape),
        grid_spec=pltpu.PrefetchScalarGridSpec(
            num_scalar_prefetch=1,
            grid=(others,),
            in_specs=[pl.BlockSpec((half, part), low), pl.BlockSpec((half, part), high)],
            out_specs=(block, block),
        ),
        compiler_params=params(),
        name="pack",
    )(position, branch, branch)


def join_kernel(*refs):
    *part_refs, out_ref = refs
    part = part_refs[0].shape[1]
    for c, part_ref in enumerate(part_refs):
        out_ref[:, c * part : (c + 1) * part] = part_ref[...]


def spread_kernel(shares_ref, ids_ref, out_ref):
    experts, quarter, columns = shares_ref.shape
    blocks, _, features = out_ref.shape
    per_expert = blocks // experts
    for f in range(blocks):
        start = (f % per_expert) * features
        out_ref[f, :quarter] = shares_ref[f // per_expert, :, start : start + features]
        out_ref[f, quarter:] = ids_ref[...]


def sides_kernel(position_ref, *refs):
    *share_refs, own_ref, other_ref = refs
    for k, share_ref in enumerate(share_refs):
        place = position_ref[0] ^ k
        for side, out_ref in enumerate((own_ref, other_ref)):
            out_ref[:, place] = share_ref[:, position_ref[2] ^ side]


def dispatch_kernel(position_ref, ids_ref, extra_ref, *refs):
    *token_refs, out_ref = refs
    planes = len(token_refs)
    experts, _, part = out_ref.shape
    lanes = extra_ref.shape[0]
    count = out_ref.shape[1] - lanes
    capacity = count // planes
    tokens = ids_ref.shape[2]
    plane, core = position_ref[1], position_ref[2]
    slots = lax.broadcasted_iota(jnp.int32, (experts * capacity, tokens), 0)
    for k in range(planes):
        source = plane ^ k
        ids = ids_ref[source * 2 + core]
        code0 = ids[0:1] * capacity + ids[2:3]
        code1 = ids[1:2] * capacity + ids[3:4]
        one_hot = jnp.where((code0 == slots) | (code1 == slots), 1.0, 0.0).astype(jnp.bfloat16)
        picked = jnp.dot(one_hot, token_refs[k][...], preferred_element_type=jnp.float32)
        rows = pl.ds(pl.multiple_of(source * capacity, 16), capacity)
        out_ref[:, rows] = picked.reshape(experts, capacity, part).astype(jnp.bfloat16)
    for e in range(experts):
        out_ref[e, count:] = extra_ref[...]


def row_stats(flat_ref, side, aux_ref):
    count = flat_ref.shape[0] // 2
    experts, lanes, part = aux_ref.shape
    squares = jnp.zeros((count, part), jnp.float32)
    logits = jnp.zeros((count, lanes), jnp.float32)
    for e in range(experts):
        rows = flat_ref[side * count : (side + 1) * count, e * part : (e + 1) * part]
        aux = aux_ref[e]
        ratio = rows.astype(jnp.float32) * (1.0 / aux[0:1].astype(jnp.float32))
        squares = squares + ratio * ratio
        logits = logits + lax.dot_general(
            rows, aux, (((1,), (1,)), ((), ())), preferred_element_type=jnp.float32
        )
    total = jnp.sum(squares, axis=1, keepdims=True)
    return jnp.where(lax.broadcasted_iota(jnp.int32, logits.shape, 1) == 0, total, logits)


def row_copies(sides, flat_ref, aux_ref, sems):
    count = flat_ref.shape[0] // 2
    experts, _, part = aux_ref.shape
    copies = [
        pltpu.make_async_copy(sides[0].at[:, pl.ds(count, aux_ref.shape[1])], aux_ref, sems.at[0])
    ]
    for side, rows_ref in enumerate(sides):
        for e in range(experts):
            copies.append(
                pltpu.make_async_copy(
                    rows_ref.at[e, pl.ds(0, count)],
                    flat_ref.at[pl.ds(side * count, count), pl.ds(e * part, part)],
                    sems.at[1 + side * experts + e],
                )
            )
    return copies


def turned(flat_ref, e, part):
    return flat_ref[:, e * part : (e + 1) * part].T


def product(flat_ref, weight_ref):
    weight = weight_ref[...].reshape(flat_ref.shape[1], weight_ref.shape[3])
    return jnp.dot(flat_ref[...], weight, preferred_element_type=jnp.float32)


def shares_of(experts, tiles, t):
    return range(t * experts // tiles, (t + 1) * experts // tiles)


def early_kernel(
    tiles,
    own_ref,
    other_ref,
    gate_ref,
    up_ref,
    gate_out,
    up_out,
    stats_out,
    turned_out,
    flat_scratch,
    aux_scratch,
    sems,
):
    count = flat_scratch.shape[0] // 2
    experts, _, part = aux_scratch.shape

    for t in range(tiles):

        @pl.when(pl.program_id(0) == t)
        def _():
            if t == 0:
                copies = row_copies((own_ref, other_ref), flat_scratch, aux_scratch, sems)
                for copy in copies:
                    copy.start()
                for copy in copies:
                    copy.wait()
            gate_out[...] = product(flat_scratch, gate_ref)
            up_out[...] = product(flat_scratch, up_ref)
            for e in shares_of(experts, tiles, t):
                turned_out[e] = turned(flat_scratch, e, part)
            if t == tiles - 1:
                for side in range(2):
                    stats_out[side * count : (side + 1) * count] = row_stats(
                        flat_scratch, side, aux_scratch
                    )


def late_kernel(
    width,
    tiles,
    position_ref,
    own_ref,
    other_ref,
    turned_ref,
    gate_ref,
    up_ref,
    gate_acc,
    up_acc,
    stats_ref,
    signs_ref,
    cot_ref,
    hidden_out,
    grad_gate_out,
    grad_up_out,
    flat_scratch,
    aux_scratch,
    scale_scratch,
    weight_scratch,
    gate_scratch,
    up_scratch,
    d_gate_scratch,
    d_up_scratch,
    turned_scratch,
    sems,
):
    step = pl.program_id(0)
    core = position_ref[2]
    planes, _, capacity, tile = hidden_out.shape
    count = planes * capacity
    experts, _, part = aux_scratch.shape
    lanes = stats_ref.shape[1]
    turn_copy = pltpu.make_async_copy(
        turned_ref, turned_scratch.at[0], sems.at[1 + 2 * experts]
    )

    def scales():
        for side in range(2):
            span = slice(side * count, (side + 1) * count)
            stats = stats_ref[span] + row_stats(flat_scratch, side, aux_scratch)
            inverse = lax.rsqrt(stats[:, 0:1] / width + 1e-05)
            signs = signs_ref[:, pl.ds(core ^ side, 1)].reshape(count, lanes)
            filled = signs[:, lanes - 1 :]
            column = lax.broadcasted_iota(jnp.int32, stats.shape, 1)
            router = (column >= 1) & (column <= experts)
            margin = jnp.sum(jnp.where(router, stats * signs, 0.0), axis=1, keepdims=True)
            prob = jax.nn.sigmoid(margin * inverse).astype(jnp.bfloat16).astype(jnp.float32)
            scale_scratch[span] = inverse
            weight_scratch[span] = jnp.where(filled > 0.0, prob, 0.0)

    def units_of(t):
        for side in range(2):
            span = slice(side * count, (side + 1) * count)
            inverse = scale_scratch[span]
            weight = weight_scratch[span]
            gate_pre = inverse * gate_scratch[t % 2, span]
            up_pre = inverse * up_scratch[t % 2, span]
            sig_gate = jax.nn.sigmoid(gate_pre)
            act_gate = gate_pre * sig_gate
            hidden = (weight * act_gate * up_pre).astype(jnp.bfloat16)
            hidden_out[:, pl.ds(core ^ side, 1)] = hidden.reshape(planes, 1, capacity, tile)
            cot = cot_ref[:, pl.ds(core ^ side, 1)].reshape(count, tile)
            d_pre = cot.astype(jnp.float32) * (weight * inverse)
            d_gate = d_pre * up_pre * sig_gate * (1.0 + gate_pre * (1.0 - sig_gate))
            columns = slice(t * tile, (t + 1) * tile)
            d_gate_scratch[span, columns] = d_gate.astype(jnp.bfloat16)
            d_up_scratch[span, columns] = (d_pre * act_gate).astype(jnp.bfloat16)

    def gradients(stretch):
        e = (step - tiles) % experts
        stretch_units = grad_gate_out.shape[2]
        span = slice(stretch * stretch_units, (stretch + 1) * stretch_units)
        for c in range(CHUNKS):
            for scratch, out in ((d_gate_scratch, grad_gate_out), (d_up_scratch, grad_up_out)):
                out[0, c * part : (c + 1) * part] = jnp.dot(
                    turned_scratch[c, e], scratch[:, span], preferred_element_type=jnp.float32
                ).astype(jnp.bfloat16)

    for t in range(tiles):

        @pl.when(step == t)
        def _():
            if t == 0:
                copies = row_copies((own_ref, other_ref), flat_scratch, aux_scratch, sems)
                for copy in copies:
                    copy.start()
                turn_copy.start()
                for copy in copies:
                    copy.wait()
            gate_scratch[t % 2] = gate_acc[...] + product(flat_scratch, gate_ref)
            up_scratch[t % 2] = up_acc[...] + product(flat_scratch, up_ref)
            for e in shares_of(experts, tiles, t):
                turned_scratch[1, e] = turned(flat_scratch, e, part)
            if t == 0:
                scales()
            else:
                units_of(t - 1)

    @pl.when(step == tiles)
    def _():
        turn_copy.wait()
        units_of(tiles - 1)
        gradients(0)

    for stretch in range(tiles * tile // grad_gate_out.shape[2]):
        first = tiles + stretch * experts

        @pl.when((step >= first) & (step < first + experts) & (step > tiles))
        def _():
            gradients(stretch)


def per_device(
    branch_wo,
    context,
    residual,
    norm_gain,
    router_w,
    gate_w,
    up_w,
    expert_ids,
    slot_ids,
    cot_hidden,
):
    experts = lax.axis_size("expert")
    blocks = lax.axis_size("fsdp")
    planes = blocks // 2
    expert = lax.axis_index("expert")
    block = lax.axis_index("fsdp")
    plane, core = block // 2, block % 2
    tokens, columns = context.shape
    width = columns * experts
    features = width // blocks
    capacity = cot_hidden.shape[1] // blocks
    units = cot_hidden.shape[2]
    part = columns // CHUNKS
    quarter = tokens // experts
    count = planes * capacity
    position = jnp.stack([expert, plane, core]).astype(jnp.int32)
    bits = bits_of(experts)

    lanes = experts + 2 + (-(experts + 2)) % 16
    extra = jnp.concatenate([norm_gain[None], router_w.T])
    extra = jnp.pad(extra, ((0, lanes - extra.shape[0]), (0, 0)))
    ids = jnp.concatenate([expert_ids, slot_ids], axis=1).T.astype(jnp.bfloat16)
    id_rows = ids.size // features
    ids = jnp.pad(ids.reshape(id_rows, features), ((0, -id_rows % 16), (0, 0)))

    branch = branch_wo[0]
    half = branch.shape[0] // 2
    weights = [1 << (bits - 1 - i) for i in range(bits)]
    own_bits = [(expert // weight) % 2 for weight in weights]

    def start_sum(c, h):
        def value(chosen):
            place = sum(weight * bit for weight, bit in zip(weights, chosen))
            corner = (h * half, (place * CHUNKS + c) * part)
            return lax.dynamic_slice(branch, corner, (half, part)).astype(jnp.float32)

        return value

    def joined(value, got, axis, rest):
        def total(chosen):
            chosen = [own_bits[axis] if i == axis else bit for i, bit in enumerate(chosen)]
            place = 0
            for i in rest:
                place = 2 * place + chosen[i]
            return value(chosen) + pick(got, place, 0).astype(jnp.float32)

        return total

    held = {(c, h): start_sum(c, h) for c in range(CHUNKS) for h in range(2)}
    orders = (list(range(bits))[::-1], list(range(bits)))

    def branch_sends(phase, c):
        if phase == 0:
            return pack(position, branch, c, experts)
        sends = []
        for h, order in enumerate(orders):
            rest = sorted(order[phase + 1 :])
            stacked = []
            for code in range(1 << len(rest)):
                chosen = list(own_bits)
                chosen[order[phase]] = 1 - own_bits[order[phase]]
                for at, i in enumerate(rest):
                    chosen[i] = (code >> (len(rest) - 1 - at)) & 1
                stacked.append(held[c, h](chosen).astype(jnp.bfloat16))
            sends.append(stacked[0][None] if len(stacked) == 1 else jnp.stack(stacked))
        return tuple(sends)

    def branch_exchange(phase, sends):
        return tuple(
            exchange(sends[h], "expert", weights[order[phase]]) for h, order in enumerate(orders)
        )

    def branch_add(phase, c, got):
        for h, order in enumerate(orders):
            held[c, h] = joined(held[c, h], got[h], order[phase], sorted(order[phase + 1 :]))

    def merged_of(c):
        total = jnp.concatenate([held[c, 0](own_bits), held[c, 1](own_bits)])
        return (total / experts).astype(jnp.bfloat16)

    shares = lax.all_to_all(
        context.reshape(experts, quarter, columns), "expert", split_axis=0, concat_axis=0, tiled=True
    )
    got = branch_exchange(0, branch_sends(0, 0))
    shares, got = lax.optimization_barrier((shares, got))
    branch_add(0, 0, got)

    spread_shape = (blocks, quarter + ids.shape[0], features)
    to_blocks = pl.pallas_call(
        spread_kernel,
        out_shape=jax.ShapeDtypeStruct(spread_shape, jnp.bfloat16),
        in_specs=[whole(shares.shape), whole(ids.shape)],
        out_specs=whole(spread_shape),
        grid=(1,),
        compiler_params=params(),
        name="spread",
    )(shares, ids)
    from_blocks = lax.all_to_all(to_blocks, "fsdp", split_axis=0, concat_axis=0, tiled=True)
    for phase in range(1, bits):
        got = branch_exchange(phase, branch_sends(phase, 0))
        if phase == bits - 1:
            from_blocks, got = lax.optimization_barrier((from_blocks, got))
        branch_add(phase, 0, got)

    ids_all = from_blocks[:, quarter : quarter + id_rows].astype(jnp.int32)
    ids_all = ids_all.reshape(blocks, 4, tokens)
    own_share = from_blocks[:, :quarter]
    pieces = [exchange(own_share, "expert", k) if k else own_share for k in range(experts)]
    side_shape = (planes, experts, quarter, features)
    sides = pl.pallas_call(
        sides_kernel,
        out_shape=(jax.ShapeDtypeStruct(side_shape, jnp.bfloat16),) * 2,
        in_specs=[smem()] + [whole((planes, 2, quarter, features))] * experts,
        out_specs=(whole(side_shape),) * 2,
        grid=(1,),
        compiler_params=params(),
        name="sides",
    )(position, *[piece.reshape(planes, 2, quarter, features) for piece in pieces])
    sides = [side.reshape(planes * tokens, features) for side in sides]
    signs = pl.pallas_call(
        functools.partial(signs_kernel, experts),
        out_shape=jax.ShapeDtypeStruct((blocks, capacity, lanes), jnp.float32),
        in_specs=[smem(), whole(ids_all.shape)],
        out_specs=whole((blocks, capacity, lanes)),
        grid=(1,),
        compiler_params=params(),
        name="signs",
    )(position, ids_all).reshape(planes, 2, capacity, lanes)

    gate_view = gate_w.reshape(experts, CHUNKS, part, units)
    up_view = up_w.reshape(experts, CHUNKS, part, units)
    tile = min(256, units)
    stretch = min(512, units)
    tiles = units // tile
    def pair_of(merged):
        def attend(rows):
            out = jnp.dot(rows, merged, preferred_element_type=jnp.float32)
            return out.reshape(planes, tokens, part)

        swapped = exchange(attend(sides[1]).astype(jnp.bfloat16), "fsdp", 1)
        return attend(sides[0]) + swapped.astype(jnp.float32)

    def plane_sends(pair):
        return [pick(pair, plane ^ k, 0).astype(jnp.bfloat16) for k in range(1, planes)]

    def plane_exchange(sends):
        return [exchange(send, "fsdp", 2 * k) for k, send in enumerate(sends, 1)]

    def scaled_of(c, pair, arrived):
        span = slice(c * part, (c + 1) * part)
        hstate = residual[:, span].astype(jnp.float32) + pick(pair, plane, 0)
        for value in arrived:
            hstate = hstate + value.astype(jnp.float32)
        return (hstate * norm_gain[span].astype(jnp.float32)).astype(jnp.bfloat16)

    height = count + lanes

    def slots_of(c, own_tokens):
        return pl.pallas_call(
            dispatch_kernel,
            out_shape=jax.ShapeDtypeStruct((experts, height, part), jnp.bfloat16),
            in_specs=[smem(), whole(ids_all.shape)]
            + [pl.BlockSpec((lanes, part), lambda i, c=c: (0, c))]
            + [whole((tokens, part))] * planes,
            out_specs=whole((experts, height, part)),
            grid=(1,),
            compiler_params=params(),
            name="dispatch",
        )(position, ids_all, extra, *own_tokens)

    merged0 = merged_of(0)
    got = branch_exchange(0, after(branch_sends(0, 1), pieces))
    pair0 = pair_of(merged0)
    sends0 = plane_sends(pair0)
    branch_add(0, 1, after(got, sends0))
    arrived0 = plane_exchange(sends0)
    for phase in range(1, bits):
        got = branch_exchange(phase, branch_sends(phase, 1))
        if phase < bits - 1:
            branch_add(phase, 1, got)

    scaled0 = scaled_of(0, pair0, arrived0)
    tokens0 = [scaled0] + plane_exchange([scaled0] * (planes - 1))
    if bits > 1:
        branch_add(bits - 1, 1, after(got, scaled0))
    merged1 = merged_of(1)
    merged_out = pl.pallas_call(
        join_kernel,
        out_shape=jax.ShapeDtypeStruct((features, columns), jnp.bfloat16),
        in_specs=[whole((features, part))] * CHUNKS,
        out_specs=whole((features, columns)),
        grid=(1,),
        compiler_params=params(),
        name="join",
    )(merged0, merged1)
    pair1 = pair_of(merged1)
    arrived1 = plane_exchange(plane_sends(pair1))

    slots0 = slots_of(0, tokens0)
    scaled1 = scaled_of(1, pair1, after(arrived1, slots0))
    tokens1 = [scaled1] + plane_exchange([scaled1] * (planes - 1))
    slots1 = slots_of(1, tokens1)
    slots = (slots0, slots1)

    def to_experts(c):
        return lax.all_to_all(slots[c], "expert", split_axis=0, concat_axis=0, tiled=True)

    rows = after(to_experts(0), slots[-1], merged_out, signs)
    other = exchange(rows, "fsdp", 1)
    weight_spec = pl.BlockSpec((experts, 1, part, tile), lambda n: (0, 0, 0, n))
    sums = jax.ShapeDtypeStruct((2 * count, units), jnp.float32)
    sum_spec = pl.BlockSpec((2 * count, tile), lambda n: (0, n))
    any_spec = pl.BlockSpec(memory_space=pl.ANY)
    row_scratch = [
        pltpu.VMEM((2 * count, experts * part), jnp.bfloat16),
        pltpu.VMEM((experts, lanes, part), jnp.bfloat16),
    ]
    partial = pl.pallas_call(
        functools.partial(early_kernel, tiles),
        out_shape=(
            sums,
            sums,
            jax.ShapeDtypeStruct((2 * count, lanes), jnp.float32),
            jax.ShapeDtypeStruct((experts, part, 2 * count), jnp.bfloat16),
        ),
        in_specs=[any_spec, any_spec, weight_spec, weight_spec],
        out_specs=(
            sum_spec,
            sum_spec,
            whole((2 * count, lanes)),
            whole((experts, part, 2 * count)),
        ),
        grid=(tiles,),
        scratch_shapes=row_scratch + [pltpu.SemaphoreType.DMA((1 + 2 * experts,))],
        compiler_params=params(),
        cost_estimate=pl.CostEstimate(
            flops=8 * count * experts * part * units,
            bytes_accessed=4 * experts * part * units,
            transcendentals=0,
        ),
        name="early",
    )(rows, other, gate_view, up_view)
    rows = after(to_experts(1), partial)
    other = exchange(rows, "fsdp", 1)

    tile_of = lambda i: jnp.minimum(i, tiles - 1)
    behind = lambda i: jnp.clip(i - 1, 0, tiles - 1)
    place_of = lambda i: jnp.maximum(i - tiles, 0)
    weight_spec = pl.BlockSpec((experts, 1, part, tile), lambda i: (0, 1, 0, tile_of(i)))
    sum_spec = pl.BlockSpec((2 * count, tile), lambda i: (0, tile_of(i)))
    unit_spec = pl.BlockSpec((planes, 2, capacity, tile), lambda i: (0, 0, 0, behind(i)))
    grad_spec = pl.BlockSpec(
        (1, columns, stretch), lambda i: (place_of(i) % experts, 0, place_of(i) // experts)
    )
    grad_shape = jax.ShapeDtypeStruct((experts, columns, units), jnp.bfloat16)
    gate_sums, up_sums, stats, turned_rows = partial
    hidden, grad_gate, grad_up = pl.pallas_call(
        functools.partial(late_kernel, float(width), tiles),
        out_shape=(
            jax.ShapeDtypeStruct((planes, 2, capacity, units), jnp.bfloat16),
            grad_shape,
            grad_shape,
        ),
        in_specs=[smem(), any_spec, any_spec, any_spec]
        + [weight_spec, weight_spec, sum_spec, sum_spec]
        + [whole(stats.shape), whole(signs.shape), unit_spec],
        out_specs=(unit_spec, grad_spec, grad_spec),
        grid=(tiles + experts * (units // stretch),),
        scratch_shapes=row_scratch
        + [
            pltpu.VMEM((2 * count, 1), jnp.float32),
            pltpu.VMEM((2 * count, 1), jnp.float32),
            pltpu.VMEM((2, 2 * count, tile), jnp.float32),
            pltpu.VMEM((2, 2 * count, tile), jnp.float32),
            pltpu.VMEM((2 * count, units), jnp.bfloat16),
            pltpu.VMEM((2 * count, units), jnp.bfloat16),
            pltpu.VMEM((CHUNKS, experts, part, 2 * count), jnp.bfloat16),
            pltpu.SemaphoreType.DMA((2 + 2 * experts,)),
        ],
        compiler_params=params(),
        name="late",
    )(
        position,
        rows,
        other,
        turned_rows,
        gate_view,
        up_view,
        gate_sums,
        up_sums,
        stats,
        signs,
        cot_hidden.reshape(planes, 2, capacity, units),
    )
    return (
        merged_out,
        hidden.reshape(1, -1, units),
        grad_gate.reshape(1, width, units),
        grad_up.reshape(1, width, units),
    )


def solution(mesh):
    placed = (
        P("expert", "fsdp", None),
        P("fsdp", "expert"),
        P("fsdp", "expert"),
        P("expert"),
        P("expert", None),
        P("expert", None, "fsdp"),
        P("expert", None, "fsdp"),
        P("fsdp", None),
        P("fsdp", None),
        P("expert", None, "fsdp"),
    )
    return jax.shard_map(
        per_device,
        mesh=mesh,
        in_specs=placed,
        out_specs=(
            P("fsdp", "expert"),
            P("expert", None, "fsdp"),
            P("expert", None, "fsdp"),
            P("expert", None, "fsdp"),
        ),
        check_vma=False,
    )
```

profile of v0, /device:TPU:0, one launch (start us, length us, event | category | flops | bytes accessed | tf_op | source)
XLA Modules:
  0.0 199.2 jit_solution(15475682407200667673)
XLA Ops:
  1.3 2.8 %pack.2 = (bf16[2,256,512]{2,1,0:T(8,128)(2,1)}, bf16[2,256,512]{2,1,0:T(8,128)(2,1)}) custom-call(s32[3]{0:T(128)} %pad_add_fusion.position_ref, bf16[512,4096]{1,0:T(8,128)(2,1)} %bitcast.85, bf16[512,4096]{1,0:T(8,128)(2,1)} %bitcast.86), custom_call_target="tpu_custom_call" | custom-call | tf_op jit(solution)/shard_map/pack/pallas_call | solution.py:84
  4.1 2.9 %collective-permute-start = (bf16[2,256,512]{2,1,0:T(8,128)(2,1)}, bf16[2,256,512]{2,1,0:T(8,128)(2,1)S(1)}, u32[]{:S(2)}, u32[]{:S(2)}) collective-permute-start(bf16[2,256,512]{2,1,0:T(8,128)(2,1)} %get-tuple-element.34), channel_id=1, source_target_pairs={{0,8},{8,0},{16,24},{24,16},{1,9},{9,1},{17,25},{25,17},{2,10},{10... | collective-permute-start | bytes 1572872 | tf_op jit(solution)/shard_map/ppermute | solution.py:16
  7.1 1.5 collective-permute-start.1
  8.6 3.4 %all-to-all-start = ((bf16[4,32,1024]{2,1,0:T(8,128)(2,1)}), bf16[4,32,1024]{2,1,0:T(8,128)(2,1)S(1)}, u32[]{:S(2)}, u32[]{:S(2)}) async-start(bf16[4,32,1024]{2,1,0:T(8,128)(2,1)} %bitcast), calls=%async_computation | async-start | bytes 524288 | tf_op jit(solution)/shard_map/all_to_all | solution.py:437
  12.1 0.6 pad.8.ids_ref
  12.7 10.8 %all-to-all-done.shares_ref = bf16[4,32,1024]{2,1,0:T(8,128)(2,1)S(1)} async-done(((bf16[4,32,1024]{2,1,0:T(8,128)(2,1)}), bf16[4,32,1024]{2,1,0:T(8,128)(2,1)S(1)}, u32[]{:S(2)}, u32[]{:S(2)}) %all-to-all-start) | async-done | bytes 262176 | tf_op jit(solution)/shard_map/all_to_all | solution.py:437
  23.5 0.7 copy-done.7
  24.2 1.7 spread.1
  25.9 4.9 %all-to-all-start.1 = ((bf16[8,48,512]{2,1,0:T(8,128)(2,1)}), bf16[8,48,512]{2,1,0:T(8,128)(2,1)S(1)}, u32[]{:S(2)}, u32[]{:S(2)}) async-start(bf16[8,48,512]{2,1,0:T(8,128)(2,1)} %spread.1), calls=%async_computation.1 | async-start | bytes 786432 | tf_op jit(solution)/shard_map/all_to_all | solution.py:454
  30.8 1.2 add_convert_fusion.2
  31.9 1.3 collective-permute-start.3
  33.2 0.8 collective-permute-start.2
  34.0 6.7 %collective-permute-done.3 = bf16[1,256,512]{2,1,0:T(8,128)(2,1)S(1)} collective-permute-done((bf16[1,256,512]{2,1,0:T(8,128)(2,1)S(1)}, bf16[1,256,512]{2,1,0:T(8,128)(2,1)S(1)}, u32[]{:S(2)}, u32[]{:S(2)}) %collective-permute-start.3) | collective-permute-done | bytes 262176 | tf_op jit(solution)/shard_map/ppermute | solution.py:16
  40.7 0.9 collective-permute-done.2
  41.7 1.7 all-to-all-done.1
  43.4 1.5 collective-permute-start.6
  44.9 1.2 collective-permute-start.5
  46.1 0.8 collective-permute-start.4
  46.9 1.2 add_bitcast_fusion.3
  48.3 5.3 %collective-permute-done.6 = bf16[8,32,512]{2,1,0:T(8,128)(2,1)S(1)} collective-permute-done((bf16[8,32,512]{2,1,0:T(8,128)(2,1)S(1)}, bf16[8,32,512]{2,1,0:T(8,128)(2,1)S(1)}, u32[]{:S(2)}, u32[]{:S(2)}) %collective-permute-start.6) | collective-permute-done | bytes 262176 | tf_op jit(solution)/shard_map/ppermute | solution.py:16
  53.6 4.2 %collective-permute-done.5 = bf16[8,32,512]{2,1,0:T(8,128)(2,1)S(1)} collective-permute-done((bf16[8,32,512]{2,1,0:T(8,128)(2,1)S(1)}, bf16[8,32,512]{2,1,0:T(8,128)(2,1)S(1)}, u32[]{:S(2)}, u32[]{:S(2)}) %collective-permute-start.5) | collective-permute-done | bytes 262176 | tf_op jit(solution)/shard_map/ppermute | solution.py:16
  58.6 2.2 %sides.1 = (bf16[4,4,32,512]{3,2,1,0:T(8,128)(2,1)}, bf16[4,4,32,512]{3,2,1,0:T(8,128)(2,1)}) custom-call(s32[3]{0:T(128)} %pad_add_fusion.position_ref, bf16[4,2,32,512]{3,2,1,0:T(8,128)(2,1)} %bitcast.99, bf16[4,2,32,512]{3,2,1,0:T(8,128)(2,1)} %bitcast.105, bf16[4,2,32,512]{3,2,1,0:T(8,128)(2,1)} %bitcast.104, bf16[4,2,32,512]{3,2,1,0:T(8,128)(2,1)} %bitcast.103), custom_call_target="tpu_custom_call" | custom-call | tf_op jit(solution)/shard_map/sides/pallas_call | solution.py:466
  60.8 1.5 convolution_convert_fusion.1
  62.4 2.9 %pack.3 = (bf16[2,256,512]{2,1,0:T(8,128)(2,1)}, bf16[2,256,512]{2,1,0:T(8,128)(2,1)}) custom-call(s32[3]{0:T(128)} %pad_add_fusion.position_ref, bf16[512,4096]{1,0:T(8,128)(2,1)} %bitcast.87, bf16[512,4096]{1,0:T(8,128)(2,1)} %bitcast.88), custom_call_target="tpu_custom_call" | custom-call | tf_op jit(solution)/shard_map/pack/pallas_call | solution.py:84
  65.3 1.2 collective-permute-start.7
  66.5 0.8 collective-permute-start.8
  67.8 0.8 fusion.18
  68.6 1.7 collective-permute-start.14
  70.3 2.7 %collective-permute-start.12 = (bf16[128,512]{1,0:T(8,128)(2,1)}, bf16[128,512]{1,0:T(8,128)(2,1)}, u32[]{:S(2)}, u32[]{:S(2)}) collective-permute-start(bf16[128,512]{1,0:T(8,128)(2,1)} %get-tuple-element.77), channel_id=1, source_target_pairs={{0,2},{1,3},{2,0},{3,1},{4,6},{5,7},{6,4},{7,5},{8,10},{9,11},{10,... | collective-permute-start | bytes 393224 | tf_op jit(solution)/shard_map/ppermute | solution.py:16
  73.0 6.7 %collective-permute-done.7 = bf16[2,256,512]{2,1,0:T(8,128)(2,1)S(1)} collective-permute-done((bf16[2,256,512]{2,1,0:T(8,128)(2,1)}, bf16[2,256,512]{2,1,0:T(8,128)(2,1)S(1)}, u32[]{:S(2)}, u32[]{:S(2)}) %collective-permute-start.7) | collective-permute-done | bytes 524320 | tf_op jit(solution)/shard_map/ppermute | solution.py:16
  79.7 1.0 collective-permute-done.8
  80.7 1.2 add_convert_fusion
  81.9 0.9 collective-permute-start.11
  82.8 1.5 collective-permute-start.10
  84.3 1.3 fusion.24.extra_ref
  85.7 1.2 fusion.15.refs_0_
  86.9 1.8 collective-permute-start.21
  88.6 2.7 %collective-permute-start.19 = (bf16[128,512]{1,0:T(8,128)(2,1)S(1)}, bf16[128,512]{1,0:T(8,128)(2,1)S(1)}, u32[]{:S(2)}, u32[]{:S(2)}) collective-permute-start(bf16[128,512]{1,0:T(8,128)(2,1)S(1)} %fusion.15.refs_0_), channel_id=1, source_target_pairs={{0,2},{1,3},{2,0},{3,1},{4,6},{5,7},{6,4},{7,5},{8,10},{9,11},{10,... | collective-permute-start | bytes 393224 | tf_op jit(solution)/shard_map/ppermute | solution.py:16
  91.3 1.5 add_bitcast_fusion.1
  93.5 0.6 slice_convert_fusion
  94.1 1.1 collective-permute-done.21.refs_3_
  95.2 4.0 %collective-permute-done.20.refs_2_ = bf16[128,512]{1,0:T(8,128)(2,1)S(1)} collective-permute-done((bf16[128,512]{1,0:T(8,128)(2,1)S(1)}, bf16[128,512]{1,0:T(8,128)(2,1)S(1)}, u32[]{:S(2)}, u32[]{:S(2)}) %collective-permute-start.20) | collective-permute-done | bytes 131104 | tf_op jit(solution)/shard_map/ppermute | solution.py:16
  99.2 0.6 copy-done.15
  99.9 2.9 %dispatch.2 = bf16[4,400,512]{2,1,0:T(8,128)(2,1)} custom-call(s32[3]{0:T(128)} %pad_add_fusion.position_ref, s32[8,4,128]{2,1,0:T(4,128)} %bitcast.100, bf16[16,1024]{1,0:T(8,128)(2,1)} %fusion.24.extra_ref, bf16[128,512]{1,0:T(8,128)(2,1)} %copy-done.8, bf16[128,512]{1,0:T(8,128)(2,1)} %copy-done.16, bf16[128,512]{1,0:T(8,128)(2,1)} %copy-done.15, ...), custom_call_target="tpu_custom_call" | custom-call | tf_op jit(solution)/shard_map/dispatch/pallas_call | solution.py:515
  102.8 4.5 %all-to-all-start.3 = ((bf16[4,400,512]{2,1,0:T(8,128)(2,1)}), bf16[4,400,512]{2,1,0:T(8,128)(2,1)}, u32[]{:S(2)}, u32[]{:S(2)}) async-start(bf16[4,400,512]{2,1,0:T(8,128)(2,1)} %dispatch.2), calls=%async_computation.3 | async-start | bytes 3276800 | tf_op jit(solution)/shard_map/all_to_all | solution.py:562
  107.8 1.8 collective-permute-start.18
  109.6 2.7 %collective-permute-start.16 = (bf16[128,512]{1,0:T(8,128)(2,1)S(1)}, bf16[128,512]{1,0:T(8,128)(2,1)S(1)}, u32[]{:S(2)}, u32[]{:S(2)}) collective-permute-start(bf16[128,512]{1,0:T(8,128)(2,1)S(1)} %get-tuple-element.74), channel_id=1, source_target_pairs={{0,2},{1,3},{2,0},{3,1},{4,6},{5,7},{6,4},{7,5},{8,10},{9,11},{10,... | collective-permute-start | bytes 393224 | tf_op jit(solution)/shard_map/ppermute | solution.py:16
  112.3 3.9 %collective-permute-done.18 = bf16[128,512]{1,0:T(8,128)(2,1)S(1)} collective-permute-done((bf16[128,512]{1,0:T(8,128)(2,1)S(1)}, bf16[128,512]{1,0:T(8,128)(2,1)S(1)}, u32[]{:S(2)}, u32[]{:S(2)}) %collective-permute-start.18) | collective-permute-done | bytes 131104 | tf_op jit(solution)/shard_map/ppermute | solution.py:16
  116.2 3.9 %collective-permute-done.17 = bf16[128,512]{1,0:T(8,128)(2,1)S(1)} collective-permute-done((bf16[128,512]{1,0:T(8,128)(2,1)S(1)}, bf16[128,512]{1,0:T(8,128)(2,1)S(1)}, u32[]{:S(2)}, u32[]{:S(2)}) %collective-permute-start.17) | collective-permute-done | bytes 131104 | tf_op jit(solution)/shard_map/ppermute | solution.py:16
  120.3 1.9 collective-permute-start.24
  122.1 2.6 %collective-permute-start.22 = (bf16[128,512]{1,0:T(8,128)(2,1)S(1)}, bf16[128,512]{1,0:T(8,128)(2,1)S(1)}, u32[]{:S(2)}, u32[]{:S(2)}) collective-permute-start(bf16[128,512]{1,0:T(8,128)(2,1)S(1)} %fusion.10.refs_0_), channel_id=1, source_target_pairs={{0,2},{1,3},{2,0},{3,1},{4,6},{5,7},{6,4},{7,5},{8,10},{9,11},{10,... | collective-permute-start | bytes 393224 | tf_op jit(solution)/shard_map/ppermute | solution.py:16
  124.7 1.7 signs.1
  126.5 2.2 %join.1 = bf16[512,1024]{1,0:T(8,128)(2,1)} custom-call(bf16[512,512]{1,0:T(8,128)(2,1)} %copy-done, bf16[512,512]{1,0:T(8,128)(2,1)} %copy-done.1), custom_call_target="tpu_custom_call" | custom-call | tf_op jit(solution)/shard_map/join/pallas_call | solution.py:543
  128.7 4.6 %collective-permute-done.23.refs_2_ = bf16[128,512]{1,0:T(8,128)(2,1)S(1)} collective-permute-done((bf16[128,512]{1,0:T(8,128)(2,1)S(1)}, bf16[128,512]{1,0:T(8,128)(2,1)S(1)}, u32[]{:S(2)}, u32[]{:S(2)}) %collective-permute-start.23) | collective-permute-done | bytes 131104 | tf_op jit(solution)/shard_map/ppermute | solution.py:16
  133.3 0.6 copy-done.18
  134.0 0.7 copy-done.19
  134.6 2.9 %dispatch.3 = bf16[4,400,512]{2,1,0:T(8,128)(2,1)} custom-call(s32[3]{0:T(128)} %pad_add_fusion.position_ref, s32[8,4,128]{2,1,0:T(4,128)} %bitcast.102, bf16[16,1024]{1,0:T(8,128)(2,1)} %fusion.24.extra_ref, bf16[128,512]{1,0:T(8,128)(2,1)} %copy-done.9, bf16[128,512]{1,0:T(8,128)(2,1)} %copy-done.19, bf16[128,512]{1,0:T(8,128)(2,1)} %copy-done.18, ...), custom_call_target="tpu_custom_call" | custom-call | tf_op jit(solution)/shard_map/dispatch/pallas_call | solution.py:515
  137.5 3.9 %all-to-all-start.2 = ((bf16[4,400,512]{2,1,0:T(8,128)(2,1)}), bf16[4,400,512]{2,1,0:T(8,128)(2,1)S(1)}, u32[]{:S(2)}, u32[]{:S(2)}) async-start(bf16[4,400,512]{2,1,0:T(8,128)(2,1)} %dispatch.3), calls=%async_computation.2 | async-start | bytes 3276800 | tf_op jit(solution)/shard_map/all_to_all | solution.py:562
  141.4 1.2 copy-done.21
  142.5 14.9 %early.1 = (f32[768,1024]{1,0:T(8,128)}, f32[768,1024]{1,0:T(8,128)}, f32[768,16]{1,0:T(8,128)}, bf16[4,512,768]{2,1,0:T(8,128)(2,1)}) custom-call(bf16[4,400,512]{2,1,0:T(8,128)(2,1)} %all-to-all-done.3.own_ref, bf16[4,400,512]{2,1,0:T(8,128)(2,1)} %copy-done.21, bf16[4,2,512,1024]{3,2,1,0:T(8,128)(2,1)} %bitcast.89, bf16[4,2,512,1024]{3,2,1,0:T(8,128)(2,1)} %bitcast.91), custom_call_target="tpu_custom_call" | custom-call | flops 6442450944 | bytes 8388608 | tf_op jit(solution)/shard_map/early/pallas_call | solution.py:574
  157.5 4.6 %all-to-all-done.2.own_ref = bf16[4,400,512]{2,1,0:T(8,128)(2,1)S(1)} async-done(((bf16[4,400,512]{2,1,0:T(8,128)(2,1)}), bf16[4,400,512]{2,1,0:T(8,128)(2,1)S(1)}, u32[]{:S(2)}, u32[]{:S(2)}) %all-to-all-start.2) | async-done | bytes 1638432 | tf_op jit(solution)/shard_map/all_to_all | solution.py:562
  162.1 3.5 %collective-permute-done.26.other_ref = bf16[4,400,512]{2,1,0:T(8,128)(2,1)S(1)} collective-permute-done((bf16[4,400,512]{2,1,0:T(8,128)(2,1)S(1)}, bf16[4,400,512]{2,1,0:T(8,128)(2,1)S(1)}, u32[]{:S(2)}, u32[]{:S(2)}) %collective-permute-start.26) | collective-permute-done | bytes 1638432 | tf_op jit(solution)/shard_map/ppermute | solution.py:16
  165.6 1.3 copy-done.5
  166.8 32.2 %late.1 = (bf16[4,2,96,1024]{3,2,1,0:T(8,128)(2,1)}, bf16[4,1024,1024]{2,1,0:T(8,128)(2,1)}, bf16[4,1024,1024]{2,1,0:T(8,128)(2,1)}) custom-call(s32[3]{0:T(128)} %pad_add_fusion.position_ref, bf16[4,400,512]{2,1,0:T(8,128)(2,1)} %copy-done.2, bf16[4,400,512]{2,1,0:T(8,128)(2,1)} %copy-done.5, bf16[4,512,768]{2,1,0:T(8,128)(2,1)} %get-tuple-element.59.turned_ref, ...), custom_call_target="tpu_custom_call" | custom-call | tf_op jit(solution)/shard_map/late/pallas_call | solution.py:613
  (81 shorter events, 3.5 us)
Async XLA Ops:
  1.3 10.7 %copy-start.22 = (s32[128,2]{0,1:T(2,128)S(1)}, s32[128,2]{0,1:T(2,128)}, u32[]{:S(2)}) copy-start(s32[128,2]{0,1:T(2,128)} %param.17) | copy-start | bytes 3076
  1.3 10.7 %copy-start.23 = (s32[128,2]{0,1:T(2,128)S(1)}, s32[128,2]{0,1:T(2,128)}, u32[]{:S(2)}) copy-start(s32[128,2]{0,1:T(2,128)} %param.18) | copy-start | bytes 3076
  4.1 19.4 %collective-permute-start = (bf16[2,256,512]{2,1,0:T(8,128)(2,1)}, bf16[2,256,512]{2,1,0:T(8,128)(2,1)S(1)}, u32[]{:S(2)}, u32[]{:S(2)}) collective-permute-start(bf16[2,256,512]{2,1,0:T(8,128)(2,1)} %get-tuple-element.34), channel_id=1, source_target_pairs={{0,8},{8,0},{16,24},{24,16},{1,9},{9,1},{17,25},{25,17},{2,10},{10... | collective-permute-start | bytes 1572872 | tf_op jit(solution)/shard_map/ppermute | solution.py:16
  7.1 16.4 %collective-permute-start.1 = (bf16[2,256,512]{2,1,0:T(8,128)(2,1)}, bf16[2,256,512]{2,1,0:T(8,128)(2,1)S(1)}, u32[]{:S(2)}, u32[]{:S(2)}) collective-permute-start(bf16[2,256,512]{2,1,0:T(8,128)(2,1)} %get-tuple-element.35), channel_id=1, source_target_pairs={{0,16},{8,24},{16,0},{24,8},{1,17},{9,25},{17,1},{25,9},{2,18},{10... | collective-permute-start | bytes 1572872 | tf_op jit(solution)/shard_map/ppermute | solution.py:16
  8.6 14.9 %all-to-all-start = ((bf16[4,32,1024]{2,1,0:T(8,128)(2,1)}), bf16[4,32,1024]{2,1,0:T(8,128)(2,1)S(1)}, u32[]{:S(2)}, u32[]{:S(2)}) async-start(bf16[4,32,1024]{2,1,0:T(8,128)(2,1)} %bitcast), calls=%async_computation | async-start | bytes 524288 | tf_op jit(solution)/shard_map/all_to_all | solution.py:437
  23.5 0.7 copy-start.7
  25.9 17.4 %all-to-all-start.1 = ((bf16[8,48,512]{2,1,0:T(8,128)(2,1)}), bf16[8,48,512]{2,1,0:T(8,128)(2,1)S(1)}, u32[]{:S(2)}, u32[]{:S(2)}) async-start(bf16[8,48,512]{2,1,0:T(8,128)(2,1)} %spread.1), calls=%async_computation.1 | async-start | bytes 786432 | tf_op jit(solution)/shard_map/all_to_all | solution.py:454
  31.9 8.8 %collective-permute-start.3 = (bf16[1,256,512]{2,1,0:T(8,128)(2,1)S(1)}, bf16[1,256,512]{2,1,0:T(8,128)(2,1)S(1)}, u32[]{:S(2)}, u32[]{:S(2)}) collective-permute-start(bf16[1,256,512]{2,1,0:T(8,128)(2,1)S(1)} %get-tuple-element.70), channel_id=1, source_target_pairs={{0,8},{8,0},{16,24},{24,16},{1,9},{9,1},{17,25},{25,17},{2,10},{10... | collective-permute-start | bytes 786440 | tf_op jit(solution)/shard_map/ppermute | solution.py:16
  33.2 8.4 %collective-permute-start.2 = (bf16[1,256,512]{2,1,0:T(8,128)(2,1)S(1)}, bf16[1,256,512]{2,1,0:T(8,128)(2,1)S(1)}, u32[]{:S(2)}, u32[]{:S(2)}) collective-permute-start(bf16[1,256,512]{2,1,0:T(8,128)(2,1)S(1)} %get-tuple-element.71), channel_id=1, source_target_pairs={{0,16},{8,24},{16,0},{24,8},{1,17},{9,25},{17,1},{25,9},{2,18},{10... | collective-permute-start | bytes 786440 | tf_op jit(solution)/shard_map/ppermute | solution.py:16
  43.3 14.5 %copy-start.6 = (bf16[8,32,512]{2,1,0:T(8,128)(2,1)}, bf16[8,32,512]{2,1,0:T(8,128)(2,1)S(1)}, u32[]{:S(2)}) copy-start(bf16[8,32,512]{2,1,0:T(8,128)(2,1)S(1)} %slice.18) | copy-start | bytes 786436
  43.4 10.2 %collective-permute-start.6 = (bf16[8,32,512]{2,1,0:T(8,128)(2,1)S(1)}, bf16[8,32,512]{2,1,0:T(8,128)(2,1)S(1)}, u32[]{:S(2)}, u32[]{:S(2)}) collective-permute-start(bf16[8,32,512]{2,1,0:T(8,128)(2,1)S(1)} %slice.18), channel_id=1, source_target_pairs={{0,24},{8,16},{16,8},{24,0},{1,25},{9,17},{17,9},{25,1},{2,26},{10... | collective-permute-start | bytes 786440 | tf_op jit(solution)/shard_map/ppermute | solution.py:16
  44.9 12.9 %collective-permute-start.5 = (bf16[8,32,512]{2,1,0:T(8,128)(2,1)S(1)}, bf16[8,32,512]{2,1,0:T(8,128)(2,1)S(1)}, u32[]{:S(2)}, u32[]{:S(2)}) collective-permute-start(bf16[8,32,512]{2,1,0:T(8,128)(2,1)S(1)} %slice.18), channel_id=1, source_target_pairs={{0,16},{8,24},{16,0},{24,8},{1,17},{9,25},{17,1},{25,9},{2,18},{10... | collective-permute-start | bytes 786440 | tf_op jit(solution)/shard_map/ppermute | solution.py:16
  46.1 11.8 %collective-permute-start.4 = (bf16[8,32,512]{2,1,0:T(8,128)(2,1)S(1)}, bf16[8,32,512]{2,1,0:T(8,128)(2,1)S(1)}, u32[]{:S(2)}, u32[]{:S(2)}) collective-permute-start(bf16[8,32,512]{2,1,0:T(8,128)(2,1)S(1)} %slice.18), channel_id=1, source_target_pairs={{0,8},{8,0},{16,24},{24,16},{1,9},{9,1},{17,25},{25,17},{2,10},{10... | collective-permute-start | bytes 786440 | tf_op jit(solution)/shard_map/ppermute | solution.py:16
  48.3 19.1 %copy-start = (bf16[512,512]{1,0:T(8,128)(2,1)}, bf16[512,512]{1,0:T(8,128)(2,1)S(1)}, u32[]{:S(2)}) copy-start(bf16[512,512]{1,0:T(8,128)(2,1)S(1)} %fusion.refs_0_) | copy-start | bytes 1572868
  53.6 4.3 %copy-start.11 = (bf16[8,32,512]{2,1,0:T(8,128)(2,1)}, bf16[8,32,512]{2,1,0:T(8,128)(2,1)S(1)}, u32[]{:S(2)}) copy-start(bf16[8,32,512]{2,1,0:T(8,128)(2,1)S(1)} %collective-permute-done.6) | copy-start | bytes 786436
  57.8 0.7 copy-start.12
  57.9 0.7 copy-start.13
  62.3 5.0 %copy-start.20 = (bf16[1024]{0:T(1024)(128)(2,1)S(1)}, bf16[1024]{0:T(1024)(128)(2,1)}, u32[]{:S(2)}) copy-start(bf16[1024]{0:T(1024)(128)(2,1)} %param.13) | copy-start | bytes 6148
  62.3 5.1 %copy-start.3 = (bf16[4,4,32,512]{3,2,1,0:T(8,128)(2,1)S(1)}, bf16[4,4,32,512]{3,2,1,0:T(8,128)(2,1)}, u32[]{:S(2)}) copy-start(bf16[4,4,32,512]{3,2,1,0:T(8,128)(2,1)} %get-tuple-element.46) | copy-start | bytes 1572868
  62.3 5.0 %collective-permute-start.9 = (bf16[4,128,512]{2,1,0:T(8,128)(2,1)S(1)}, bf16[4,128,512]{2,1,0:T(8,128)(2,1)S(1)}, u32[]{:S(2)}, u32[]{:S(2)}) collective-permute-start(bf16[4,128,512]{2,1,0:T(8,128)(2,1)S(1)} %convolution_convert_fusion.1), channel_id=1, source_target_pairs={{0,1},{1,0},{2,3},{3,2},{4,5},{5,4},{6,7},{7,6},{8,9},{9,8},{10,11... | collective-permute-start | bytes 1572872 | tf_op jit(solution)/shard_map/ppermute | solution.py:16
  65.3 14.4 %collective-permute-start.7 = (bf16[2,256,512]{2,1,0:T(8,128)(2,1)}, bf16[2,256,512]{2,1,0:T(8,128)(2,1)S(1)}, u32[]{:S(2)}, u32[]{:S(2)}) collective-permute-start(bf16[2,256,512]{2,1,0:T(8,128)(2,1)} %get-tuple-element.44), channel_id=1, source_target_pairs={{0,8},{8,0},{16,24},{24,16},{1,9},{9,1},{17,25},{25,17},{2,10},{10... | collective-permute-start | bytes 1572872 | tf_op jit(solution)/shard_map/ppermute | solution.py:16
  66.5 14.2 %collective-permute-start.8 = (bf16[2,256,512]{2,1,0:T(8,128)(2,1)}, bf16[2,256,512]{2,1,0:T(8,128)(2,1)}, u32[]{:S(2)}, u32[]{:S(2)}) collective-permute-start(bf16[2,256,512]{2,1,0:T(8,128)(2,1)} %get-tuple-element.45), channel_id=1, source_target_pairs={{0,16},{8,24},{16,0},{24,8},{1,17},{9,25},{17,1},{25,9},{2,18},{10... | collective-permute-start | bytes 1572872 | tf_op jit(solution)/shard_map/ppermute | solution.py:16
  68.6 17.1 %collective-permute-start.14 = (bf16[128,512]{1,0:T(8,128)(2,1)}, bf16[128,512]{1,0:T(8,128)(2,1)}, u32[]{:S(2)}, u32[]{:S(2)}) collective-permute-start(bf16[128,512]{1,0:T(8,128)(2,1)} %get-tuple-element.75), channel_id=1, source_target_pairs={{0,6},{1,7},{2,4},{3,5},{4,2},{5,3},{6,0},{7,1},{8,14},{9,15},{10,... | collective-permute-start | bytes 393224 | tf_op jit(solution)/shard_map/ppermute | solution.py:16
  70.3 15.4 %collective-permute-start.13 = (bf16[128,512]{1,0:T(8,128)(2,1)}, bf16[128,512]{1,0:T(8,128)(2,1)}, u32[]{:S(2)}, u32[]{:S(2)}) collective-permute-start(bf16[128,512]{1,0:T(8,128)(2,1)} %get-tuple-element.76), channel_id=1, source_target_pairs={{0,4},{1,5},{2,6},{3,7},{4,0},{5,1},{6,2},{7,3},{8,12},{9,13},{10,... | collective-permute-start | bytes 393224 | tf_op jit(solution)/shard_map/ppermute | solution.py:16
  70.3 22.6 %copy-start.4 = (bf16[4,4,32,512]{3,2,1,0:T(8,128)(2,1)S(1)}, bf16[4,4,32,512]{3,2,1,0:T(8,128)(2,1)}, u32[]{:S(2)}) copy-start(bf16[4,4,32,512]{3,2,1,0:T(8,128)(2,1)} %get-tuple-element.47) | copy-start | bytes 1572868
  70.3 15.4 %collective-permute-start.12 = (bf16[128,512]{1,0:T(8,128)(2,1)}, bf16[128,512]{1,0:T(8,128)(2,1)}, u32[]{:S(2)}, u32[]{:S(2)}) collective-permute-start(bf16[128,512]{1,0:T(8,128)(2,1)} %get-tuple-element.77), channel_id=1, source_target_pairs={{0,2},{1,3},{2,0},{3,1},{4,6},{5,7},{6,4},{7,5},{8,10},{9,11},{10,... | collective-permute-start | bytes 393224 | tf_op jit(solution)/shard_map/ppermute | solution.py:16
  81.9 9.4 %collective-permute-start.11 = (bf16[1,256,512]{2,1,0:T(8,128)(2,1)S(1)}, bf16[1,256,512]{2,1,0:T(8,128)(2,1)}, u32[]{:S(2)}, u32[]{:S(2)}) collective-permute-start(bf16[1,256,512]{2,1,0:T(8,128)(2,1)S(1)} %get-tuple-element.66), channel_id=1, source_target_pairs={{0,8},{8,0},{16,24},{24,16},{1,9},{9,1},{17,25},{25,17},{2,10},{10... | collective-permute-start | bytes 786440 | tf_op jit(solution)/shard_map/ppermute | solution.py:16
  82.8 8.5 %collective-permute-start.10 = (bf16[1,256,512]{2,1,0:T(8,128)(2,1)S(1)}, bf16[1,256,512]{2,1,0:T(8,128)(2,1)}, u32[]{:S(2)}, u32[]{:S(2)}) collective-permute-start(bf16[1,256,512]{2,1,0:T(8,128)(2,1)S(1)} %get-tuple-element.67), channel_id=1, source_target_pairs={{0,16},{8,24},{16,0},{24,8},{1,17},{9,25},{17,1},{25,9},{2,18},{10... | collective-permute-start | bytes 786440 | tf_op jit(solution)/shard_map/ppermute | solution.py:16
  86.9 12.4 %copy-start.8 = (bf16[128,512]{1,0:T(8,128)(2,1)}, bf16[128,512]{1,0:T(8,128)(2,1)S(1)}, u32[]{:S(2)}) copy-start(bf16[128,512]{1,0:T(8,128)(2,1)S(1)} %fusion.15.refs_0_) | copy-start | bytes 393220
  86.9 8.3 %collective-permute-start.21 = (bf16[128,512]{1,0:T(8,128)(2,1)S(1)}, bf16[128,512]{1,0:T(8,128)(2,1)S(1)}, u32[]{:S(2)}, u32[]{:S(2)}) collective-permute-start(bf16[128,512]{1,0:T(8,128)(2,1)S(1)} %fusion.15.refs_0_), channel_id=1, source_target_pairs={{0,6},{1,7},{2,4},{3,5},{4,2},{5,3},{6,0},{7,1},{8,14},{9,15},{10,... | collective-permute-start | bytes 393224 | tf_op jit(solution)/shard_map/ppermute | solution.py:16
  88.6 10.6 %collective-permute-start.20 = (bf16[128,512]{1,0:T(8,128)(2,1)S(1)}, bf16[128,512]{1,0:T(8,128)(2,1)S(1)}, u32[]{:S(2)}, u32[]{:S(2)}) collective-permute-start(bf16[128,512]{1,0:T(8,128)(2,1)S(1)} %fusion.15.refs_0_), channel_id=1, source_target_pairs={{0,4},{1,5},{2,6},{3,7},{4,0},{5,1},{6,2},{7,3},{8,12},{9,13},{10,... | collective-permute-start | bytes 393224 | tf_op jit(solution)/shard_map/ppermute | solution.py:16
  88.6 10.6 %collective-permute-start.19 = (bf16[128,512]{1,0:T(8,128)(2,1)S(1)}, bf16[128,512]{1,0:T(8,128)(2,1)S(1)}, u32[]{:S(2)}, u32[]{:S(2)}) collective-permute-start(bf16[128,512]{1,0:T(8,128)(2,1)S(1)} %fusion.15.refs_0_), channel_id=1, source_target_pairs={{0,2},{1,3},{2,0},{3,1},{4,6},{5,7},{6,4},{7,5},{8,10},{9,11},{10,... | collective-permute-start | bytes 393224 | tf_op jit(solution)/shard_map/ppermute | solution.py:16
  92.9 14.4 %copy-start.1 = (bf16[512,512]{1,0:T(8,128)(2,1)}, bf16[512,512]{1,0:T(8,128)(2,1)S(1)}, u32[]{:S(2)}) copy-start(bf16[512,512]{1,0:T(8,128)(2,1)S(1)} %fusion.1.refs_1_) | copy-start | bytes 1572868
  93.4 13.9 %collective-permute-start.15 = (bf16[4,128,512]{2,1,0:T(8,128)(2,1)S(1)}, bf16[4,128,512]{2,1,0:T(8,128)(2,1)S(1)}, u32[]{:S(2)}, u32[]{:S(2)}) collective-permute-start(bf16[4,128,512]{2,1,0:T(8,128)(2,1)S(1)} %convolution_convert_fusion), channel_id=1, source_target_pairs={{0,1},{1,0},{2,3},{3,2},{4,5},{5,4},{6,7},{7,6},{8,9},{9,8},{10,11... | collective-permute-start | bytes 1572872 | tf_op jit(solution)/shard_map/ppermute | solution.py:16
  95.2 4.0 %copy-start.14 = (bf16[128,512]{1,0:T(8,128)(2,1)}, bf16[128,512]{1,0:T(8,128)(2,1)S(1)}, u32[]{:S(2)}) copy-start(bf16[128,512]{1,0:T(8,128)(2,1)S(1)} %collective-permute-done.21.refs_3_) | copy-start | bytes 393220
  99.2 0.7 copy-start.15
  99.2 0.7 copy-start.16
  102.8 17.4 %copy-start.10 = (bf16[128,1024]{1,0:T(8,128)(2,1)S(1)}, bf16[128,1024]{1,0:T(8,128)(2,1)}, u32[]{:S(2)}) copy-start(bf16[128,1024]{1,0:T(8,128)(2,1)} %param.12) | copy-start | bytes 786436
  102.8 34.7 %all-to-all-start.3 = ((bf16[4,400,512]{2,1,0:T(8,128)(2,1)}), bf16[4,400,512]{2,1,0:T(8,128)(2,1)}, u32[]{:S(2)}, u32[]{:S(2)}) async-start(bf16[4,400,512]{2,1,0:T(8,128)(2,1)} %dispatch.2), calls=%async_computation.3 | async-start | bytes 3276800 | tf_op jit(solution)/shard_map/all_to_all | solution.py:562
  107.8 8.4 %collective-permute-start.18 = (bf16[128,512]{1,0:T(8,128)(2,1)S(1)}, bf16[128,512]{1,0:T(8,128)(2,1)S(1)}, u32[]{:S(2)}, u32[]{:S(2)}) collective-permute-start(bf16[128,512]{1,0:T(8,128)(2,1)S(1)} %get-tuple-element.72), channel_id=1, source_target_pairs={{0,6},{1,7},{2,4},{3,5},{4,2},{5,3},{6,0},{7,1},{8,14},{9,15},{10,... | collective-permute-start | bytes 393224 | tf_op jit(solution)/shard_map/ppermute | solution.py:16
  109.6 10.6 %collective-permute-start.17 = (bf16[128,512]{1,0:T(8,128)(2,1)S(1)}, bf16[128,512]{1,0:T(8,128)(2,1)S(1)}, u32[]{:S(2)}, u32[]{:S(2)}) collective-permute-start(bf16[128,512]{1,0:T(8,128)(2,1)S(1)} %get-tuple-element.73), channel_id=1, source_target_pairs={{0,4},{1,5},{2,6},{3,7},{4,0},{5,1},{6,2},{7,3},{8,12},{9,13},{10,... | collective-permute-start | bytes 393224 | tf_op jit(solution)/shard_map/ppermute | solution.py:16
  109.6 10.6 %collective-permute-start.16 = (bf16[128,512]{1,0:T(8,128)(2,1)S(1)}, bf16[128,512]{1,0:T(8,128)(2,1)S(1)}, u32[]{:S(2)}, u32[]{:S(2)}) collective-permute-start(bf16[128,512]{1,0:T(8,128)(2,1)S(1)} %get-tuple-element.74), channel_id=1, source_target_pairs={{0,2},{1,3},{2,0},{3,1},{4,6},{5,7},{6,4},{7,5},{8,10},{9,11},{10,... | collective-permute-start | bytes 393224 | tf_op jit(solution)/shard_map/ppermute | solution.py:16
  120.3 13.1 %copy-start.9 = (bf16[128,512]{1,0:T(8,128)(2,1)}, bf16[128,512]{1,0:T(8,128)(2,1)S(1)}, u32[]{:S(2)}) copy-start(bf16[128,512]{1,0:T(8,128)(2,1)S(1)} %fusion.10.refs_0_) | copy-start | bytes 393220
  120.3 8.4 %collective-permute-start.24 = (bf16[128,512]{1,0:T(8,128)(2,1)S(1)}, bf16[128,512]{1,0:T(8,128)(2,1)S(1)}, u32[]{:S(2)}, u32[]{:S(2)}) collective-permute-start(bf16[128,512]{1,0:T(8,128)(2,1)S(1)} %fusion.10.refs_0_), channel_id=1, source_target_pairs={{0,6},{1,7},{2,4},{3,5},{4,2},{5,3},{6,0},{7,1},{8,14},{9,15},{10,... | collective-permute-start | bytes 393224 | tf_op jit(solution)/shard_map/ppermute | solution.py:16
  122.1 11.2 %collective-permute-start.23 = (bf16[128,512]{1,0:T(8,128)(2,1)S(1)}, bf16[128,512]{1,0:T(8,128)(2,1)S(1)}, u32[]{:S(2)}, u32[]{:S(2)}) collective-permute-start(bf16[128,512]{1,0:T(8,128)(2,1)S(1)} %fusion.10.refs_0_), channel_id=1, source_target_pairs={{0,4},{1,5},{2,6},{3,7},{4,0},{5,1},{6,2},{7,3},{8,12},{9,13},{10,... | collective-permute-start | bytes 393224 | tf_op jit(solution)/shard_map/ppermute | solution.py:16
  122.1 11.2 %collective-permute-start.22 = (bf16[128,512]{1,0:T(8,128)(2,1)S(1)}, bf16[128,512]{1,0:T(8,128)(2,1)S(1)}, u32[]{:S(2)}, u32[]{:S(2)}) collective-permute-start(bf16[128,512]{1,0:T(8,128)(2,1)S(1)} %fusion.10.refs_0_), channel_id=1, source_target_pairs={{0,2},{1,3},{2,0},{3,1},{4,6},{5,7},{6,4},{7,5},{8,10},{9,11},{10,... | collective-permute-start | bytes 393224 | tf_op jit(solution)/shard_map/ppermute | solution.py:16
  128.7 4.6 %copy-start.17 = (bf16[128,512]{1,0:T(8,128)(2,1)}, bf16[128,512]{1,0:T(8,128)(2,1)S(1)}, u32[]{:S(2)}) copy-start(bf16[128,512]{1,0:T(8,128)(2,1)S(1)} %collective-permute-done.24.refs_3_) | copy-start | bytes 393220
  133.3 0.7 copy-start.18
  134.0 0.7 copy-start.19
  137.5 3.9 %collective-permute-start.25 = (bf16[4,400,512]{2,1,0:T(8,128)(2,1)}, bf16[4,400,512]{2,1,0:T(8,128)(2,1)S(1)}, u32[]{:S(2)}, u32[]{:S(2)}) collective-permute-start(bf16[4,400,512]{2,1,0:T(8,128)(2,1)} %all-to-all-done.3.own_ref), channel_id=1, source_target_pairs={{0,1},{1,0},{2,3},{3,2},{4,5},{5,4},{6,7},{7,6},{8,9},{9,8},{10,11... | collective-permute-start | bytes 4915208 | tf_op jit(solution)/shard_map/ppermute | solution.py:16
  137.5 24.6 %all-to-all-start.2 = ((bf16[4,400,512]{2,1,0:T(8,128)(2,1)}), bf16[4,400,512]{2,1,0:T(8,128)(2,1)S(1)}, u32[]{:S(2)}, u32[]{:S(2)}) async-start(bf16[4,400,512]{2,1,0:T(8,128)(2,1)} %dispatch.3), calls=%async_computation.2 | async-start | bytes 3276800 | tf_op jit(solution)/shard_map/all_to_all | solution.py:562
  141.4 1.2 copy-start.21
  162.1 3.5 %copy-start.2 = (bf16[4,400,512]{2,1,0:T(8,128)(2,1)}, bf16[4,400,512]{2,1,0:T(8,128)(2,1)S(1)}, u32[]{:S(2)}) copy-start(bf16[4,400,512]{2,1,0:T(8,128)(2,1)S(1)} %all-to-all-done.2.own_ref) | copy-start | bytes 4915204
  162.1 3.5 %collective-permute-start.26 = (bf16[4,400,512]{2,1,0:T(8,128)(2,1)S(1)}, bf16[4,400,512]{2,1,0:T(8,128)(2,1)S(1)}, u32[]{:S(2)}, u32[]{:S(2)}) collective-permute-start(bf16[4,400,512]{2,1,0:T(8,128)(2,1)S(1)} %all-to-all-done.2.own_ref), channel_id=1, source_target_pairs={{0,1},{1,0},{2,3},{3,2},{4,5},{5,4},{6,7},{7,6},{8,9},{9,8},{10,11... | collective-permute-start | bytes 4915208 | tf_op jit(solution)/shard_map/ppermute | solution.py:16
  165.6 1.3 copy-start.5
where the time goes:
time: 200 us; the launch traced here: 199 us
  Pallas kernels  66.5 us (33%)
  waiting for transfers between devices  63.1 us (32%)
  starting transfers between devices  49.1 us (25%)
  other arithmetic  9.19 us (5%)
  local copies, waits for them, and re-layouts  7.34 us (4%)
  matrix products  2.78 us (1%)
    ppermute x27, waiting for transfers between devices, exchange(): return lax.ppermute(value, axis, [(i, i ^ offset) for i in range(size)])  46 us
    ppermute x27, starting transfers between devices, exchange(): return lax.ppermute(value, axis, [(i, i ^ offset) for i in range(size)])  32.5 us
    pallas_call x1, Pallas kernels, per_device(): pl.pallas_call(functools.partial(late_kernel, float(width), tiles), out_s...  32.2 us
    pallas_call x1, Pallas kernels, per_device(): pl.pallas_call(functools.partial(early_kernel, tiles), out_shape=(sums, s...  14.9 us
    all_to_all x1, waiting for transfers between devices, per_device(): lax.all_to_all(context.reshape(experts, quarter, columns), 'expert', spli...  10.8 us
    all_to_all x2, starting transfers between devices, to_experts(): lax.all_to_all(slots[c], 'expert', split_axis=0, concat_axis=0, tiled=True)  8.36 us
    unnamed x49, local copies, waits for them, and re-layouts  5.88 us
    pallas_call x2, Pallas kernels, slots_of(): pl.pallas_call(dispatch_kernel, out_shape=jax.ShapeDtypeStruct((experts,...  5.73 us
  transfers between devices with their start and end apart: 31, of which 16 were waited for; matrix products, arithmetic and copies ran while one was open for 6% of the time, Pallas kernels for 14%

commit v1 on v0

--- a/solution.py
+++ b/solution.py
@@ -8,7 +8,7 @@
 from jax.sharding import PartitionSpec as P
 
 CHUNKS = 2
-VMEM_LIMIT = 56 * 1024 * 1024
+MEBI = 1024 * 1024
 
 
 def exchange(value, axis, offset):
@@ -36,8 +36,8 @@
     return pl.BlockSpec(memory_space=pltpu.SMEM)
 
 
-def params():
-    return pltpu.CompilerParams(vmem_limit_bytes=VMEM_LIMIT)
+def params(mebi=16):
+    return pltpu.CompilerParams(vmem_limit_bytes=mebi * MEBI)
 
 
 def signs_kernel(experts, position_ref, ids_ref, out_ref):
@@ -264,7 +264,7 @@
     experts, _, part = aux_scratch.shape
     lanes = stats_ref.shape[1]
     turn_copy = pltpu.make_async_copy(
-        turned_ref, turned_scratch.at[0], sems.at[1 + 2 * experts]
+        turned_ref, turned_scratch.at[:, pl.ds(0, part)], sems.at[1 + 2 * experts]
     )
 
     def scales():
@@ -303,11 +303,10 @@
         e = (step - tiles) % experts
         stretch_units = grad_gate_out.shape[2]
         span = slice(stretch * stretch_units, (stretch + 1) * stretch_units)
-        for c in range(CHUNKS):
-            for scratch, out in ((d_gate_scratch, grad_gate_out), (d_up_scratch, grad_up_out)):
-                out[0, c * part : (c + 1) * part] = jnp.dot(
-                    turned_scratch[c, e], scratch[:, span], preferred_element_type=jnp.float32
-                ).astype(jnp.bfloat16)
+        for scratch, out in ((d_gate_scratch, grad_gate_out), (d_up_scratch, grad_up_out)):
+            out[0] = jnp.dot(
+                turned_scratch[e], scratch[:, span], preferred_element_type=jnp.float32
+            ).astype(jnp.bfloat16)
 
     for t in range(tiles):
 
@@ -323,7 +322,7 @@
             gate_scratch[t % 2] = gate_acc[...] + product(flat_scratch, gate_ref)
             up_scratch[t % 2] = up_acc[...] + product(flat_scratch, up_ref)
             for e in shares_of(experts, tiles, t):
-                turned_scratch[1, e] = turned(flat_scratch, e, part)
+                turned_scratch[e, part:] = turned(flat_scratch, e, part)
             if t == 0:
                 scales()
             else:
@@ -437,9 +436,6 @@
     shares = lax.all_to_all(
         context.reshape(experts, quarter, columns), "expert", split_axis=0, concat_axis=0, tiled=True
     )
-    got = branch_exchange(0, branch_sends(0, 0))
-    shares, got = lax.optimization_barrier((shares, got))
-    branch_add(0, 0, got)
 
     spread_shape = (blocks, quarter + ids.shape[0], features)
     to_blocks = pl.pallas_call(
@@ -451,6 +447,8 @@
         compiler_params=params(),
         name="spread",
     )(shares, ids)
+    got = branch_exchange(0, pack(after(position, shares), branch, 0, experts))
+    branch_add(0, 0, after(got, to_blocks))
     from_blocks = lax.all_to_all(to_blocks, "fsdp", split_axis=0, concat_axis=0, tiled=True)
     for phase in range(1, bits):
         got = branch_exchange(phase, branch_sends(phase, 0))
@@ -461,7 +459,9 @@
     ids_all = from_blocks[:, quarter : quarter + id_rows].astype(jnp.int32)
     ids_all = ids_all.reshape(blocks, 4, tokens)
     own_share = from_blocks[:, :quarter]
+    packed1 = branch_sends(0, 1)
     pieces = [exchange(own_share, "expert", k) if k else own_share for k in range(experts)]
+    pieces, packed1 = lax.optimization_barrier((pieces, packed1))
     side_shape = (planes, experts, quarter, features)
     sides = pl.pallas_call(
         sides_kernel,
@@ -525,7 +525,7 @@
         )(position, ids_all, extra, *own_tokens)
 
     merged0 = merged_of(0)
-    got = branch_exchange(0, after(branch_sends(0, 1), pieces))
+    got = branch_exchange(0, packed1)
     pair0 = pair_of(merged0)
     sends0 = plane_sends(pair0)
     branch_add(0, 1, after(got, sends0))
@@ -550,9 +550,10 @@
         name="join",
     )(merged0, merged1)
     pair1 = pair_of(merged1)
-    arrived1 = plane_exchange(plane_sends(pair1))
-
-    slots0 = slots_of(0, tokens0)
+    sends1 = plane_sends(pair1)
+    arrived1 = plane_exchange(sends1)
+
+    slots0 = slots_of(0, after(tokens0, sends1))
     scaled1 = scaled_of(1, pair1, after(arrived1, slots0))
     tokens1 = [scaled1] + plane_exchange([scaled1] * (planes - 1))
     slots1 = slots_of(1, tokens1)
@@ -588,7 +589,7 @@
         ),
         grid=(tiles,),
         scratch_shapes=row_scratch + [pltpu.SemaphoreType.DMA((1 + 2 * experts,))],
-        compiler_params=params(),
+        compiler_params=params(32),
         cost_estimate=pl.CostEstimate(
             flops=8 * count * experts * part * units,
             bytes_accessed=4 * experts * part * units,
@@ -630,10 +631,10 @@
             pltpu.VMEM((2, 2 * count, tile), jnp.float32),
             pltpu.VMEM((2 * count, units), jnp.bfloat16),
             pltpu.VMEM((2 * count, units), jnp.bfloat16),
-            pltpu.VMEM((CHUNKS, experts, part, 2 * count), jnp.bfloat16),
+            pltpu.VMEM((experts, columns, 2 * count), jnp.bfloat16),
             pltpu.SemaphoreType.DMA((2 + 2 * experts,)),
         ],
-        compiler_params=params(),
+        compiler_params=params(48),
         name="late",
     )(
         position,

time: 200 us -> 194 us (0.970)
  Pallas kernels: 66.5 us -> 51.5 us
  local copies, waits for them, and re-layouts: 7.34 us -> 20.4 us
  waiting for transfers between devices: 63.1 us -> 59.3 us
    unnamed x49 -> x47, local copies, waits for them, and re-layouts: 5.88 us -> 17.7 us
    ppermute x27, waiting for transfers between devices: 46 us -> 53.9 us  [exchange(): return lax.ppermute(value, axis, [(i, i ^ offset) for i in range(size)])]
    all_to_all x1, waiting for transfers between devices: 10.8 us -> 5.3 us  [per_device(): lax.all_to_all(context.reshape(experts, quarter, columns), 'expert', spli...]
    all_to_all x2, waiting for transfers between devices: 4.58 us -> 0.01 us  [to_experts(): lax.all_to_all(slots[c], 'expert', split_axis=0, concat_axis=0, tiled=True)]
    pallas_call x2, Pallas kernels: 5.7 us -> 1.66 us  [pack(): pl.pallas_call(pack_kernel, out_shape=(shape, shape), grid_spec=pltpu.Pre...]
    pallas_call x1, Pallas kernels: 14.9 us -> 12.3 us  [per_device(): pl.pallas_call(functools.partial(early_kernel, tiles), out_shape=(sums, s...]
    pallas_call x1, Pallas kernels: 32.2 us -> 29.7 us  [per_device(): pl.pallas_call(functools.partial(late_kernel, float(width), tiles), out_s...]
    ppermute x27, starting transfers between devices: 32.5 us -> 30.3 us  [exchange(): return lax.ppermute(value, axis, [(i, i ^ offset) for i in range(size)])]
  transfers between devices with their start and end apart: 31 -> 31, of which waited for: 16 -> 19; matrix products, arithmetic and copies ran while one was open for 6% -> 6% of each run, Pallas kernels for 14% -> 9%
where the time goes in v1:
time: 194 us; the launch traced here: 193 us
  waiting for transfers between devices  59.3 us (31%)
  Pallas kernels  51.5 us (27%)
  starting transfers between devices  47.8 us (25%)
  local copies, waits for them, and re-layouts  20.4 us (11%)
  other arithmetic  9.05 us (5%)
  matrix products  3.51 us (2%)
    ppermute x27, waiting for transfers between devices, exchange(): return lax.ppermute(value, axis, [(i, i ^ offset) for i in range(size)])  53.9 us
    ppermute x27, starting transfers between devices, exchange(): return lax.ppermute(value, axis, [(i, i ^ offset) for i in range(size)])  30.3 us
    pallas_call x1, Pallas kernels, per_device(): pl.pallas_call(functools.partial(late_kernel, float(width), tiles), out_s...  29.7 us
    unnamed x47, local copies, waits for them, and re-layouts  17.7 us
    pallas_call x1, Pallas kernels, per_device(): pl.pallas_call(functools.partial(early_kernel, tiles), out_shape=(sums, s...  12.3 us
    all_to_all x2, starting transfers between devices, to_experts(): lax.all_to_all(slots[c], 'expert', split_axis=0, concat_axis=0, tiled=True)  7.39 us
    all_to_all x1, waiting for transfers between devices, per_device(): lax.all_to_all(context.reshape(experts, quarter, columns), 'expert', spli...  5.3 us
    all_to_all x1, starting transfers between devices, per_device(): lax.all_to_all(context.reshape(experts, quarter, columns), 'expert', spli...  5.18 us
  transfers between devices with their start and end apart: 31, of which 19 were waited for; matrix products, arithmetic and copies ran while one was open for 6% of the time, Pallas kernels for 9%

profile of v1, /device:TPU:0, one launch (start us, length us, event | category | flops | bytes accessed | tf_op | source)
XLA Modules:
  0.0 192.7 jit_solution(8061936674044170733)
XLA Ops:
  0.6 5.2 %all-to-all-start = ((bf16[4,32,1024]{2,1,0:T(8,128)(2,1)}), bf16[4,32,1024]{2,1,0:T(8,128)(2,1)S(1)}, u32[]{:S(2)}, u32[]{:S(2)}) async-start(bf16[4,32,1024]{2,1,0:T(8,128)(2,1)} %bitcast.110), calls=%async_computation | async-start | bytes 524288 | tf_op jit(solution)/shard_map/all_to_all | solution.py:436
  5.9 5.3 %all-to-all-done.shares_ref = bf16[4,32,1024]{2,1,0:T(8,128)(2,1)S(1)} async-done(((bf16[4,32,1024]{2,1,0:T(8,128)(2,1)}), bf16[4,32,1024]{2,1,0:T(8,128)(2,1)S(1)}, u32[]{:S(2)}, u32[]{:S(2)}) %all-to-all-start) | async-done | bytes 262176 | tf_op jit(solution)/shard_map/all_to_all | solution.py:436
  11.2 2.2 %copy-done = bf16[1,512,4096]{2,1,0:T(8,128)(2,1)S(1)} copy-done((bf16[1,512,4096]{2,1,0:T(8,128)(2,1)S(1)}, bf16[1,512,4096]{2,1,0:T(8,128)(2,1)}, u32[]{:S(2)}) %copy-start) | copy-done | bytes 4194328
  13.4 0.8 pack.2
  14.2 1.3 collective-permute-start
  16.9 4.9 %all-to-all-start.1 = ((bf16[8,48,512]{2,1,0:T(8,128)(2,1)}), bf16[8,48,512]{2,1,0:T(8,128)(2,1)S(1)}, u32[]{:S(2)}, u32[]{:S(2)}) async-start(bf16[8,48,512]{2,1,0:T(8,128)(2,1)} %spread.1), calls=%async_computation.1 | async-start | bytes 786432 | tf_op jit(solution)/shard_map/all_to_all | solution.py:452
  21.8 4.7 %collective-permute-done = bf16[2,256,512]{2,1,0:T(8,128)(2,1)S(1)} collective-permute-done((bf16[2,256,512]{2,1,0:T(8,128)(2,1)S(1)}, bf16[2,256,512]{2,1,0:T(8,128)(2,1)S(1)}, u32[]{:S(2)}, u32[]{:S(2)}) %collective-permute-start) | collective-permute-done | bytes 524320 | tf_op jit(solution)/shard_map/ppermute | solution.py:16
  26.5 1.0 collective-permute-done.1
  27.5 1.4 add_convert_fusion.2
  28.9 0.8 collective-permute-start.3
  29.7 1.5 collective-permute-start.2
  31.2 2.2 %copy-done.1 = bf16[1,512,4096]{2,1,0:T(8,128)(2,1)S(1)} copy-done((bf16[1,512,4096]{2,1,0:T(8,128)(2,1)S(1)}, bf16[1,512,4096]{2,1,0:T(8,128)(2,1)}, u32[]{:S(2)}) %copy-start.1) | copy-done | bytes 4194328
  33.4 0.8 pack.3
  34.4 0.9 collective-permute-done.3
  36.1 1.5 collective-permute-start.6
  37.6 1.3 collective-permute-start.5
  38.9 0.8 collective-permute-start.4
  39.7 1.4 add_bitcast_fusion.3
  41.2 4.9 %collective-permute-done.6 = bf16[8,32,512]{2,1,0:T(8,128)(2,1)S(1)} collective-permute-done((bf16[8,32,512]{2,1,0:T(8,128)(2,1)S(1)}, bf16[8,32,512]{2,1,0:T(8,128)(2,1)S(1)}, u32[]{:S(2)}, u32[]{:S(2)}) %collective-permute-start.6) | collective-permute-done | bytes 262176 | tf_op jit(solution)/shard_map/ppermute | solution.py:16
  46.1 2.7 %collective-permute-done.5 = bf16[8,32,512]{2,1,0:T(8,128)(2,1)S(1)} collective-permute-done((bf16[8,32,512]{2,1,0:T(8,128)(2,1)S(1)}, bf16[8,32,512]{2,1,0:T(8,128)(2,1)S(1)}, u32[]{:S(2)}, u32[]{:S(2)}) %collective-permute-start.5) | collective-permute-done | bytes 262176 | tf_op jit(solution)/shard_map/ppermute | solution.py:16
  49.5 1.2 convolution_convert_fusion.1
  50.8 1.4 collective-permute-start.7
  53.0 1.4 convert_add_fusion.1
  54.4 1.9 fusion.24
  56.2 3.8 %collective-permute-start.14 = (bf16[128,512]{1,0:T(8,128)(2,1)}, bf16[128,512]{1,0:T(8,128)(2,1)S(1)}, u32[]{:S(2)}, u32[]{:S(2)}) collective-permute-start(bf16[128,512]{1,0:T(8,128)(2,1)} %get-tuple-element.91), channel_id=1, source_target_pairs={{0,6},{1,7},{2,4},{3,5},{4,2},{5,3},{6,0},{7,1},{8,14},{9,15},{10,... | collective-permute-start | bytes 393224 | tf_op jit(solution)/shard_map/ppermute | solution.py:16
  60.6 4.6 %collective-permute-done.7 = bf16[2,256,512]{2,1,0:T(8,128)(2,1)} collective-permute-done((bf16[2,256,512]{2,1,0:T(8,128)(2,1)S(1)}, bf16[2,256,512]{2,1,0:T(8,128)(2,1)}, u32[]{:S(2)}, u32[]{:S(2)}) %collective-permute-start.7) | collective-permute-done | bytes 524320 | tf_op jit(solution)/shard_map/ppermute | solution.py:16
  65.2 1.1 collective-permute-done.8
  66.4 1.3 add_convert_fusion
  68.4 1.4 collective-permute-start.10
  69.8 2.1 %collective-permute-done.13 = bf16[128,512]{1,0:T(8,128)(2,1)} collective-permute-done((bf16[128,512]{1,0:T(8,128)(2,1)}, bf16[128,512]{1,0:T(8,128)(2,1)}, u32[]{:S(2)}, u32[]{:S(2)}) %collective-permute-start.13) | collective-permute-done | bytes 131104 | tf_op jit(solution)/shard_map/ppermute | solution.py:16
  71.9 1.2 fusion.21.refs_0_
  73.1 2.2 %collective-permute-done.11 = bf16[1,256,512]{2,1,0:T(8,128)(2,1)S(1)} collective-permute-done((bf16[1,256,512]{2,1,0:T(8,128)(2,1)S(1)}, bf16[1,256,512]{2,1,0:T(8,128)(2,1)S(1)}, u32[]{:S(2)}, u32[]{:S(2)}) %collective-permute-start.11) | collective-permute-done | bytes 262176 | tf_op jit(solution)/shard_map/ppermute | solution.py:16
  76.1 1.5 add_bitcast_fusion.1
  78.3 0.9 slice_convert_fusion
  79.2 3.7 %collective-permute-start.21 = (bf16[128,512]{1,0:T(8,128)(2,1)S(1)}, bf16[128,512]{1,0:T(8,128)(2,1)S(1)}, u32[]{:S(2)}, u32[]{:S(2)}) collective-permute-start(bf16[128,512]{1,0:T(8,128)(2,1)S(1)} %fusion.21.refs_0_), channel_id=1, source_target_pairs={{0,6},{1,7},{2,4},{3,5},{4,2},{5,3},{6,0},{7,1},{8,14},{9,15},{10,... | collective-permute-start | bytes 393224 | tf_op jit(solution)/shard_map/ppermute | solution.py:16
  82.9 0.8 collective-permute-start.19
  84.1 0.9 fusion.27
  85.0 2.5 %collective-permute-done.21.refs_3_ = bf16[128,512]{1,0:T(8,128)(2,1)S(1)} collective-permute-done((bf16[128,512]{1,0:T(8,128)(2,1)S(1)}, bf16[128,512]{1,0:T(8,128)(2,1)S(1)}, u32[]{:S(2)}, u32[]{:S(2)}) %collective-permute-start.21) | collective-permute-done | bytes 131104 | tf_op jit(solution)/shard_map/ppermute | solution.py:16
  87.5 7.3 %collective-permute-done.20.refs_2_ = bf16[128,512]{1,0:T(8,128)(2,1)S(1)} collective-permute-done((bf16[128,512]{1,0:T(8,128)(2,1)S(1)}, bf16[128,512]{1,0:T(8,128)(2,1)S(1)}, u32[]{:S(2)}, u32[]{:S(2)}) %collective-permute-start.20) | collective-permute-done | bytes 131104 | tf_op jit(solution)/shard_map/ppermute | solution.py:16
  94.8 2.3 %dispatch.2 = bf16[4,400,512]{2,1,0:T(8,128)(2,1)} custom-call(s32[3]{0:T(128)S(1)} %pad_add_fusion.position_ref, s32[8,4,128]{2,1,0:T(4,128)S(1)} %bitcast.102, bf16[16,1024]{1,0:T(8,128)(2,1)S(1)} %fusion.30.extra_ref, bf16[128,512]{1,0:T(8,128)(2,1)S(1)} %fusion.21.refs_0_, bf16[128,512]{1,0:T(8,128)(2,1)S(1)} %collective-permute-done.19.refs_1_, ...), custom_call_target="tpu_custom_call" | custom-call | tf_op jit(solution)/shard_map/dispatch/pallas_call | solution.py:515
  97.1 3.6 %all-to-all-start.3 = ((bf16[4,400,512]{2,1,0:T(8,128)(2,1)}), bf16[4,400,512]{2,1,0:T(8,128)(2,1)S(1)}, u32[]{:S(2)}, u32[]{:S(2)}) async-start(bf16[4,400,512]{2,1,0:T(8,128)(2,1)} %dispatch.2), calls=%async_computation.3 | async-start | bytes 3276800 | tf_op jit(solution)/shard_map/all_to_all | solution.py:563
  100.6 2.6 %collective-permute-start.18 = (bf16[128,512]{1,0:T(8,128)(2,1)}, bf16[128,512]{1,0:T(8,128)(2,1)S(1)}, u32[]{:S(2)}, u32[]{:S(2)}) collective-permute-start(bf16[128,512]{1,0:T(8,128)(2,1)} %get-tuple-element.88), channel_id=1, source_target_pairs={{0,6},{1,7},{2,4},{3,5},{4,2},{5,3},{6,0},{7,1},{8,14},{9,15},{10,... | collective-permute-start | bytes 393224 | tf_op jit(solution)/shard_map/ppermute | solution.py:16
  103.3 1.8 collective-permute-start.16
  105.1 4.1 %collective-permute-done.18 = bf16[128,512]{1,0:T(8,128)(2,1)S(1)} collective-permute-done((bf16[128,512]{1,0:T(8,128)(2,1)}, bf16[128,512]{1,0:T(8,128)(2,1)S(1)}, u32[]{:S(2)}, u32[]{:S(2)}) %collective-permute-start.18) | collective-permute-done | bytes 131104 | tf_op jit(solution)/shard_map/ppermute | solution.py:16
  109.2 4.5 %collective-permute-done.17 = bf16[128,512]{1,0:T(8,128)(2,1)S(1)} collective-permute-done((bf16[128,512]{1,0:T(8,128)(2,1)}, bf16[128,512]{1,0:T(8,128)(2,1)S(1)}, u32[]{:S(2)}, u32[]{:S(2)}) %collective-permute-start.17) | collective-permute-done | bytes 131104 | tf_op jit(solution)/shard_map/ppermute | solution.py:16
  113.6 1.0 fusion.16.refs_0_
  114.7 2.4 %collective-permute-start.24 = (bf16[128,512]{1,0:T(8,128)(2,1)S(1)}, bf16[128,512]{1,0:T(8,128)(2,1)S(1)}, u32[]{:S(2)}, u32[]{:S(2)}) collective-permute-start(bf16[128,512]{1,0:T(8,128)(2,1)S(1)} %fusion.16.refs_0_), channel_id=1, source_target_pairs={{0,6},{1,7},{2,4},{3,5},{4,2},{5,3},{6,0},{7,1},{8,14},{9,15},{10,... | collective-permute-start | bytes 393224 | tf_op jit(solution)/shard_map/ppermute | solution.py:16
  117.1 2.0 %collective-permute-start.22 = (bf16[128,512]{1,0:T(8,128)(2,1)S(1)}, bf16[128,512]{1,0:T(8,128)(2,1)S(1)}, u32[]{:S(2)}, u32[]{:S(2)}) collective-permute-start(bf16[128,512]{1,0:T(8,128)(2,1)S(1)} %fusion.16.refs_0_), channel_id=1, source_target_pairs={{0,2},{1,3},{2,0},{3,1},{4,6},{5,7},{6,4},{7,5},{8,10},{9,11},{10,... | collective-permute-start | bytes 393224 | tf_op jit(solution)/shard_map/ppermute | solution.py:16
  119.1 0.8 signs.1
  120.0 1.1 join.1
  121.0 2.0 %collective-permute-done.24.refs_3_ = bf16[128,512]{1,0:T(8,128)(2,1)S(1)} collective-permute-done((bf16[128,512]{1,0:T(8,128)(2,1)S(1)}, bf16[128,512]{1,0:T(8,128)(2,1)S(1)}, u32[]{:S(2)}, u32[]{:S(2)}) %collective-permute-start.24) | collective-permute-done | bytes 131104 | tf_op jit(solution)/shard_map/ppermute | solution.py:16
  123.0 5.2 %collective-permute-done.23.refs_2_ = bf16[128,512]{1,0:T(8,128)(2,1)S(1)} collective-permute-done((bf16[128,512]{1,0:T(8,128)(2,1)S(1)}, bf16[128,512]{1,0:T(8,128)(2,1)S(1)}, u32[]{:S(2)}, u32[]{:S(2)}) %collective-permute-start.23) | collective-permute-done | bytes 131104 | tf_op jit(solution)/shard_map/ppermute | solution.py:16
  128.2 2.3 %dispatch.3 = bf16[4,400,512]{2,1,0:T(8,128)(2,1)} custom-call(s32[3]{0:T(128)S(1)} %pad_add_fusion.position_ref, s32[8,4,128]{2,1,0:T(4,128)S(1)} %bitcast.104, bf16[16,1024]{1,0:T(8,128)(2,1)S(1)} %fusion.30.extra_ref, bf16[128,512]{1,0:T(8,128)(2,1)S(1)} %fusion.16.refs_0_, bf16[128,512]{1,0:T(8,128)(2,1)S(1)} %collective-permute-done.22.refs_1_, ...), custom_call_target="tpu_custom_call" | custom-call | tf_op jit(solution)/shard_map/dispatch/pallas_call | solution.py:515
  130.5 3.8 %all-to-all-start.2 = ((bf16[4,400,512]{2,1,0:T(8,128)(2,1)}), bf16[4,400,512]{2,1,0:T(8,128)(2,1)S(1)}, u32[]{:S(2)}, u32[]{:S(2)}) async-start(bf16[4,400,512]{2,1,0:T(8,128)(2,1)} %dispatch.3), calls=%async_computation.2 | async-start | bytes 3276800 | tf_op jit(solution)/shard_map/all_to_all | solution.py:563
  134.3 3.4 %copy-done.2 = bf16[1,4096,1024]{2,1,0:T(8,128)(2,1)S(1)} copy-done((bf16[1,4096,1024]{2,1,0:T(8,128)(2,1)S(1)}, bf16[1,4096,1024]{2,1,0:T(8,128)(2,1)}, u32[]{:S(2)}) %copy-start.2) | copy-done | bytes 8388632
  137.7 12.3 %early.1 = (f32[768,1024]{1,0:T(8,128)S(1)}, f32[768,1024]{1,0:T(8,128)S(1)}, f32[768,16]{1,0:T(8,128)S(1)}, bf16[4,512,768]{2,1,0:T(8,128)(2,1)S(1)}) custom-call(bf16[4,400,512]{2,1,0:T(8,128)(2,1)S(1)} %all-to-all-done.3.own_ref, bf16[4,400,512]{2,1,0:T(8,128)(2,1)} %collective-permute-done.25.other_ref, bf16[4,2,512,1024]{3,2,1,0:T(8,128)(2,1)S(1)} %bitcast.94, ...), custom_call_target="tpu_custom_call" | custom-call | flops 6442450944 | bytes 8388608 | tf_op jit(solution)/shard_map/early/pallas_call | solution.py:575
  150.0 1.7 copy-done.3
  151.7 1.7 copy-done.4
  153.4 1.6 copy-done.5
  156.2 3.1 %collective-permute-done.26.other_ref = bf16[4,400,512]{2,1,0:T(8,128)(2,1)S(1)} collective-permute-done((bf16[4,400,512]{2,1,0:T(8,128)(2,1)S(1)}, bf16[4,400,512]{2,1,0:T(8,128)(2,1)S(1)}, u32[]{:S(2)}, u32[]{:S(2)}) %collective-permute-start.26) | collective-permute-done | bytes 1638432 | tf_op jit(solution)/shard_map/ppermute | solution.py:16
  159.3 1.0 copy-done.7
  160.3 1.4 copy-done.8
  161.7 1.0 copy-done.10
  162.7 29.7 %late.1 = (bf16[4,2,96,1024]{3,2,1,0:T(8,128)(2,1)}, bf16[4,1024,1024]{2,1,0:T(8,128)(2,1)}, bf16[4,1024,1024]{2,1,0:T(8,128)(2,1)}) custom-call(s32[3]{0:T(128)S(1)} %pad_add_fusion.position_ref, bf16[4,400,512]{2,1,0:T(8,128)(2,1)S(1)} %all-to-all-done.2.own_ref, bf16[4,400,512]{2,1,0:T(8,128)(2,1)S(1)} %collective-permute-done.26.other_ref, ...), custom_call_target="tpu_custom_call" | custom-call | tf_op jit(solution)/shard_map/late/pallas_call | solution.py:614
  (79 shorter events, 8.2 us)
Async XLA Ops:
  0.6 10.5 %all-to-all-start = ((bf16[4,32,1024]{2,1,0:T(8,128)(2,1)}), bf16[4,32,1024]{2,1,0:T(8,128)(2,1)S(1)}, u32[]{:S(2)}, u32[]{:S(2)}) async-start(bf16[4,32,1024]{2,1,0:T(8,128)(2,1)} %bitcast.110), calls=%async_computation | async-start | bytes 524288 | tf_op jit(solution)/shard_map/all_to_all | solution.py:436
  11.2 2.2 %copy-start = (bf16[1,512,4096]{2,1,0:T(8,128)(2,1)S(1)}, bf16[1,512,4096]{2,1,0:T(8,128)(2,1)}, u32[]{:S(2)}) copy-start(bf16[1,512,4096]{2,1,0:T(8,128)(2,1)} %param.10) | copy-start | bytes 12582916
  13.4 2.7 %copy-start.21 = (s32[128,2]{0,1:T(2,128)S(1)}, s32[128,2]{0,1:T(2,128)}, u32[]{:S(2)}) copy-start(s32[128,2]{0,1:T(2,128)} %param.17) | copy-start | bytes 3076
  13.4 2.7 %copy-start.22 = (s32[128,2]{0,1:T(2,128)S(1)}, s32[128,2]{0,1:T(2,128)}, u32[]{:S(2)}) copy-start(s32[128,2]{0,1:T(2,128)} %param.18) | copy-start | bytes 3076
  14.2 12.3 %collective-permute-start = (bf16[2,256,512]{2,1,0:T(8,128)(2,1)S(1)}, bf16[2,256,512]{2,1,0:T(8,128)(2,1)S(1)}, u32[]{:S(2)}, u32[]{:S(2)}) collective-permute-start(bf16[2,256,512]{2,1,0:T(8,128)(2,1)S(1)} %get-tuple-element.43), channel_id=1, source_target_pairs={{0,8},{8,0},{16,24},{24,16},{1,9},{9,1},{17,25},{25,17},{2,10},{10... | collective-permute-start | bytes 1572872 | tf_op jit(solution)/shard_map/ppermute | solution.py:16
  15.5 12.0 %collective-permute-start.1 = (bf16[2,256,512]{2,1,0:T(8,128)(2,1)S(1)}, bf16[2,256,512]{2,1,0:T(8,128)(2,1)S(1)}, u32[]{:S(2)}, u32[]{:S(2)}) collective-permute-start(bf16[2,256,512]{2,1,0:T(8,128)(2,1)S(1)} %get-tuple-element.44), channel_id=1, source_target_pairs={{0,16},{8,24},{16,0},{24,8},{1,17},{9,25},{17,1},{25,9},{2,18},{10... | collective-permute-start | bytes 1572872 | tf_op jit(solution)/shard_map/ppermute | solution.py:16
  16.9 17.4 %all-to-all-start.1 = ((bf16[8,48,512]{2,1,0:T(8,128)(2,1)}), bf16[8,48,512]{2,1,0:T(8,128)(2,1)S(1)}, u32[]{:S(2)}, u32[]{:S(2)}) async-start(bf16[8,48,512]{2,1,0:T(8,128)(2,1)} %spread.1), calls=%async_computation.1 | async-start | bytes 786432 | tf_op jit(solution)/shard_map/all_to_all | solution.py:452
  26.5 4.7 %copy-start.13 = (bf16[2,256,512]{2,1,0:T(8,128)(2,1)}, bf16[2,256,512]{2,1,0:T(8,128)(2,1)S(1)}, u32[]{:S(2)}) copy-start(bf16[2,256,512]{2,1,0:T(8,128)(2,1)S(1)} %collective-permute-done) | copy-start | bytes 1572868
  27.5 3.7 %copy-start.15 = (bf16[2,256,512]{2,1,0:T(8,128)(2,1)}, bf16[2,256,512]{2,1,0:T(8,128)(2,1)S(1)}, u32[]{:S(2)}) copy-start(bf16[2,256,512]{2,1,0:T(8,128)(2,1)S(1)} %collective-permute-done.1) | copy-start | bytes 1572868
  28.9 6.4 %collective-permute-start.3 = (bf16[1,256,512]{2,1,0:T(8,128)(2,1)S(1)}, bf16[1,256,512]{2,1,0:T(8,128)(2,1)S(1)}, u32[]{:S(2)}, u32[]{:S(2)}) collective-permute-start(bf16[1,256,512]{2,1,0:T(8,128)(2,1)S(1)} %get-tuple-element.86), channel_id=1, source_target_pairs={{0,8},{8,0},{16,24},{24,16},{1,9},{9,1},{17,25},{25,17},{2,10},{10... | collective-permute-start | bytes 786440 | tf_op jit(solution)/shard_map/ppermute | solution.py:16
  29.7 6.4 %collective-permute-start.2 = (bf16[1,256,512]{2,1,0:T(8,128)(2,1)S(1)}, bf16[1,256,512]{2,1,0:T(8,128)(2,1)S(1)}, u32[]{:S(2)}, u32[]{:S(2)}) collective-permute-start(bf16[1,256,512]{2,1,0:T(8,128)(2,1)S(1)} %get-tuple-element.87), channel_id=1, source_target_pairs={{0,16},{8,24},{16,0},{24,8},{1,17},{9,25},{17,1},{25,9},{2,18},{10... | collective-permute-start | bytes 786440 | tf_op jit(solution)/shard_map/ppermute | solution.py:16
  31.2 2.2 %copy-start.1 = (bf16[1,512,4096]{2,1,0:T(8,128)(2,1)S(1)}, bf16[1,512,4096]{2,1,0:T(8,128)(2,1)}, u32[]{:S(2)}) copy-start(bf16[1,512,4096]{2,1,0:T(8,128)(2,1)} %param.10) | copy-start | bytes 12582916
  33.4 6.3 %copy-start.14 = (bf16[2,256,512]{2,1,0:T(8,128)(2,1)S(1)}, bf16[2,256,512]{2,1,0:T(8,128)(2,1)}, u32[]{:S(2)}) copy-start(bf16[2,256,512]{2,1,0:T(8,128)(2,1)} %copy-done.13) | copy-start | bytes 1572868
  34.4 4.5 %copy-start.12 = (bf16[8,48,512]{2,1,0:T(8,128)(2,1)}, bf16[8,48,512]{2,1,0:T(8,128)(2,1)S(1)}, u32[]{:S(2)}) copy-start(bf16[8,48,512]{2,1,0:T(8,128)(2,1)S(1)} %all-to-all-done.1) | copy-start | bytes 1179652
  36.1 2.8 %copy-start.18 = (bf16[1,256,512]{2,1,0:T(8,128)(2,1)}, bf16[1,256,512]{2,1,0:T(8,128)(2,1)S(1)}, u32[]{:S(2)}) copy-start(bf16[1,256,512]{2,1,0:T(8,128)(2,1)S(1)} %collective-permute-done.2) | copy-start | bytes 786436
  36.1 10.0 %collective-permute-start.6 = (bf16[8,32,512]{2,1,0:T(8,128)(2,1)S(1)}, bf16[8,32,512]{2,1,0:T(8,128)(2,1)S(1)}, u32[]{:S(2)}, u32[]{:S(2)}) collective-permute-start(bf16[8,32,512]{2,1,0:T(8,128)(2,1)S(1)} %slice.18), channel_id=1, source_target_pairs={{0,24},{8,16},{16,8},{24,0},{1,25},{9,17},{17,9},{25,1},{2,26},{10... | collective-permute-start | bytes 786440 | tf_op jit(solution)/shard_map/ppermute | solution.py:16
  37.6 11.3 %collective-permute-start.5 = (bf16[8,32,512]{2,1,0:T(8,128)(2,1)S(1)}, bf16[8,32,512]{2,1,0:T(8,128)(2,1)S(1)}, u32[]{:S(2)}, u32[]{:S(2)}) collective-permute-start(bf16[8,32,512]{2,1,0:T(8,128)(2,1)S(1)} %slice.18), channel_id=1, source_target_pairs={{0,16},{8,24},{16,0},{24,8},{1,17},{9,25},{17,1},{25,9},{2,18},{10... | collective-permute-start | bytes 786440 | tf_op jit(solution)/shard_map/ppermute | solution.py:16
  38.9 10.0 %collective-permute-start.4 = (bf16[8,32,512]{2,1,0:T(8,128)(2,1)S(1)}, bf16[8,32,512]{2,1,0:T(8,128)(2,1)S(1)}, u32[]{:S(2)}, u32[]{:S(2)}) collective-permute-start(bf16[8,32,512]{2,1,0:T(8,128)(2,1)S(1)} %slice.18), channel_id=1, source_target_pairs={{0,8},{8,0},{16,24},{24,16},{1,9},{9,1},{17,25},{25,17},{2,10},{10... | collective-permute-start | bytes 786440 | tf_op jit(solution)/shard_map/ppermute | solution.py:16
  49.5 20.3 %copy-start.19 = (bf16[1024]{0:T(1024)(128)(2,1)S(1)}, bf16[1024]{0:T(1024)(128)(2,1)}, u32[]{:S(2)}) copy-start(bf16[1024]{0:T(1024)(128)(2,1)} %param.13) | copy-start | bytes 6148
  49.5 22.4 %copy-start.16 = (bf16[128,1024]{1,0:T(8,128)(2,1)S(1)}, bf16[128,1024]{1,0:T(8,128)(2,1)}, u32[]{:S(2)}) copy-start(bf16[128,1024]{1,0:T(8,128)(2,1)} %param.12) | copy-start | bytes 786436
  50.8 2.2 %collective-permute-start.9 = (bf16[4,128,512]{2,1,0:T(8,128)(2,1)}, bf16[4,128,512]{2,1,0:T(8,128)(2,1)S(1)}, u32[]{:S(2)}, u32[]{:S(2)}) collective-permute-start(bf16[4,128,512]{2,1,0:T(8,128)(2,1)} %convolution_convert_fusion.1), channel_id=1, source_target_pairs={{0,1},{1,0},{2,3},{3,2},{4,5},{5,4},{6,7},{7,6},{8,9},{9,8},{10,11... | collective-permute-start | bytes 1572872 | tf_op jit(solution)/shard_map/ppermute | solution.py:16
  50.8 14.4 %collective-permute-start.7 = (bf16[2,256,512]{2,1,0:T(8,128)(2,1)S(1)}, bf16[2,256,512]{2,1,0:T(8,128)(2,1)}, u32[]{:S(2)}, u32[]{:S(2)}) collective-permute-start(bf16[2,256,512]{2,1,0:T(8,128)(2,1)S(1)} %get-tuple-element.52), channel_id=1, source_target_pairs={{0,8},{8,0},{16,24},{24,16},{1,9},{9,1},{17,25},{25,17},{2,10},{10... | collective-permute-start | bytes 1572872 | tf_op jit(solution)/shard_map/ppermute | solution.py:16
  52.2 14.2 %collective-permute-start.8 = (bf16[2,256,512]{2,1,0:T(8,128)(2,1)S(1)}, bf16[2,256,512]{2,1,0:T(8,128)(2,1)}, u32[]{:S(2)}, u32[]{:S(2)}) collective-permute-start(bf16[2,256,512]{2,1,0:T(8,128)(2,1)S(1)} %get-tuple-element.53), channel_id=1, source_target_pairs={{0,16},{8,24},{16,0},{24,8},{1,17},{9,25},{17,1},{25,9},{2,18},{10... | collective-permute-start | bytes 1572872 | tf_op jit(solution)/shard_map/ppermute | solution.py:16
  56.2 13.6 %collective-permute-start.14 = (bf16[128,512]{1,0:T(8,128)(2,1)}, bf16[128,512]{1,0:T(8,128)(2,1)S(1)}, u32[]{:S(2)}, u32[]{:S(2)}) collective-permute-start(bf16[128,512]{1,0:T(8,128)(2,1)} %get-tuple-element.91), channel_id=1, source_target_pairs={{0,6},{1,7},{2,4},{3,5},{4,2},{5,3},{6,0},{7,1},{8,14},{9,15},{10,... | collective-permute-start | bytes 393224 | tf_op jit(solution)/shard_map/ppermute | solution.py:16
  60.0 11.9 %collective-permute-start.13 = (bf16[128,512]{1,0:T(8,128)(2,1)}, bf16[128,512]{1,0:T(8,128)(2,1)}, u32[]{:S(2)}, u32[]{:S(2)}) collective-permute-start(bf16[128,512]{1,0:T(8,128)(2,1)} %get-tuple-element.92), channel_id=1, source_target_pairs={{0,4},{1,5},{2,6},{3,7},{4,0},{5,1},{6,2},{7,3},{8,12},{9,13},{10,... | collective-permute-start | bytes 393224 | tf_op jit(solution)/shard_map/ppermute | solution.py:16
  60.0 11.9 %collective-permute-start.12 = (bf16[128,512]{1,0:T(8,128)(2,1)}, bf16[128,512]{1,0:T(8,128)(2,1)}, u32[]{:S(2)}, u32[]{:S(2)}) collective-permute-start(bf16[128,512]{1,0:T(8,128)(2,1)} %get-tuple-element.93), channel_id=1, source_target_pairs={{0,2},{1,3},{2,0},{3,1},{4,6},{5,7},{6,4},{7,5},{8,10},{9,11},{10,... | collective-permute-start | bytes 393224 | tf_op jit(solution)/shard_map/ppermute | solution.py:16
  67.7 7.7 %collective-permute-start.11 = (bf16[1,256,512]{2,1,0:T(8,128)(2,1)S(1)}, bf16[1,256,512]{2,1,0:T(8,128)(2,1)S(1)}, u32[]{:S(2)}, u32[]{:S(2)}) collective-permute-start(bf16[1,256,512]{2,1,0:T(8,128)(2,1)S(1)} %get-tuple-element.82), channel_id=1, source_target_pairs={{0,8},{8,0},{16,24},{24,16},{1,9},{9,1},{17,25},{25,17},{2,10},{10... | collective-permute-start | bytes 786440 | tf_op jit(solution)/shard_map/ppermute | solution.py:16
  68.4 7.7 %collective-permute-start.10 = (bf16[1,256,512]{2,1,0:T(8,128)(2,1)S(1)}, bf16[1,256,512]{2,1,0:T(8,128)(2,1)}, u32[]{:S(2)}, u32[]{:S(2)}) collective-permute-start(bf16[1,256,512]{2,1,0:T(8,128)(2,1)S(1)} %get-tuple-element.83), channel_id=1, source_target_pairs={{0,16},{8,24},{16,0},{24,8},{1,17},{9,25},{17,1},{25,9},{2,18},{10... | collective-permute-start | bytes 786440 | tf_op jit(solution)/shard_map/ppermute | solution.py:16
  71.9 6.4 %copy-start.20 = (bf16[1024,4]{0,1:T(4,128)(2,1)S(1)}, bf16[1024,4]{0,1:T(4,128)(2,1)}, u32[]{:S(2)}) copy-start(bf16[1024,4]{0,1:T(4,128)(2,1)} %param.14) | copy-start | bytes 24580
  75.4 0.7 copy-start.17
  78.2 5.4 %collective-permute-start.15 = (bf16[4,128,512]{2,1,0:T(8,128)(2,1)S(1)}, bf16[4,128,512]{2,1,0:T(8,128)(2,1)S(1)}, u32[]{:S(2)}, u32[]{:S(2)}) collective-permute-start(bf16[4,128,512]{2,1,0:T(8,128)(2,1)S(1)} %convolution_convert_fusion), channel_id=1, source_target_pairs={{0,1},{1,0},{2,3},{3,2},{4,5},{5,4},{6,7},{7,6},{8,9},{9,8},{10,11... | collective-permute-start | bytes 1572872 | tf_op jit(solution)/shard_map/ppermute | solution.py:16
  79.2 8.3 %collective-permute-start.21 = (bf16[128,512]{1,0:T(8,128)(2,1)S(1)}, bf16[128,512]{1,0:T(8,128)(2,1)S(1)}, u32[]{:S(2)}, u32[]{:S(2)}) collective-permute-start(bf16[128,512]{1,0:T(8,128)(2,1)S(1)} %fusion.21.refs_0_), channel_id=1, source_target_pairs={{0,6},{1,7},{2,4},{3,5},{4,2},{5,3},{6,0},{7,1},{8,14},{9,15},{10,... | collective-permute-start | bytes 393224 | tf_op jit(solution)/shard_map/ppermute | solution.py:16
  82.9 11.9 %collective-permute-start.20 = (bf16[128,512]{1,0:T(8,128)(2,1)S(1)}, bf16[128,512]{1,0:T(8,128)(2,1)S(1)}, u32[]{:S(2)}, u32[]{:S(2)}) collective-permute-start(bf16[128,512]{1,0:T(8,128)(2,1)S(1)} %fusion.21.refs_0_), channel_id=1, source_target_pairs={{0,4},{1,5},{2,6},{3,7},{4,0},{5,1},{6,2},{7,3},{8,12},{9,13},{10,... | collective-permute-start | bytes 393224 | tf_op jit(solution)/shard_map/ppermute | solution.py:16
  82.9 11.9 %collective-permute-start.19 = (bf16[128,512]{1,0:T(8,128)(2,1)S(1)}, bf16[128,512]{1,0:T(8,128)(2,1)S(1)}, u32[]{:S(2)}, u32[]{:S(2)}) collective-permute-start(bf16[128,512]{1,0:T(8,128)(2,1)S(1)} %fusion.21.refs_0_), channel_id=1, source_target_pairs={{0,2},{1,3},{2,0},{3,1},{4,6},{5,7},{6,4},{7,5},{8,10},{9,11},{10,... | collective-permute-start | bytes 393224 | tf_op jit(solution)/shard_map/ppermute | solution.py:16
  84.1 13.0 %copy-start.11 = (f32[4,128,512]{2,1,0:T(8,128)}, f32[4,128,512]{2,1,0:T(8,128)S(1)}, u32[]{:S(2)}) copy-start(f32[4,128,512]{2,1,0:T(8,128)S(1)} %convert_add_fusion) | copy-start | bytes 3145732
  97.1 33.4 %all-to-all-start.3 = ((bf16[4,400,512]{2,1,0:T(8,128)(2,1)}), bf16[4,400,512]{2,1,0:T(8,128)(2,1)S(1)}, u32[]{:S(2)}, u32[]{:S(2)}) async-start(bf16[4,400,512]{2,1,0:T(8,128)(2,1)} %dispatch.2), calls=%async_computation.3 | async-start | bytes 3276800 | tf_op jit(solution)/shard_map/all_to_all | solution.py:563
  100.6 8.5 %collective-permute-start.18 = (bf16[128,512]{1,0:T(8,128)(2,1)}, bf16[128,512]{1,0:T(8,128)(2,1)S(1)}, u32[]{:S(2)}, u32[]{:S(2)}) collective-permute-start(bf16[128,512]{1,0:T(8,128)(2,1)} %get-tuple-element.88), channel_id=1, source_target_pairs={{0,6},{1,7},{2,4},{3,5},{4,2},{5,3},{6,0},{7,1},{8,14},{9,15},{10,... | collective-permute-start | bytes 393224 | tf_op jit(solution)/shard_map/ppermute | solution.py:16
  103.3 10.4 %collective-permute-start.17 = (bf16[128,512]{1,0:T(8,128)(2,1)}, bf16[128,512]{1,0:T(8,128)(2,1)S(1)}, u32[]{:S(2)}, u32[]{:S(2)}) collective-permute-start(bf16[128,512]{1,0:T(8,128)(2,1)} %get-tuple-element.89), channel_id=1, source_target_pairs={{0,4},{1,5},{2,6},{3,7},{4,0},{5,1},{6,2},{7,3},{8,12},{9,13},{10,... | collective-permute-start | bytes 393224 | tf_op jit(solution)/shard_map/ppermute | solution.py:16
  103.3 10.4 %collective-permute-start.16 = (bf16[128,512]{1,0:T(8,128)(2,1)S(1)}, bf16[128,512]{1,0:T(8,128)(2,1)S(1)}, u32[]{:S(2)}, u32[]{:S(2)}) collective-permute-start(bf16[128,512]{1,0:T(8,128)(2,1)S(1)} %get-tuple-element.90), channel_id=1, source_target_pairs={{0,2},{1,3},{2,0},{3,1},{4,6},{5,7},{6,4},{7,5},{8,10},{9,11},{10,... | collective-permute-start | bytes 393224 | tf_op jit(solution)/shard_map/ppermute | solution.py:16
  114.7 8.3 %collective-permute-start.24 = (bf16[128,512]{1,0:T(8,128)(2,1)S(1)}, bf16[128,512]{1,0:T(8,128)(2,1)S(1)}, u32[]{:S(2)}, u32[]{:S(2)}) collective-permute-start(bf16[128,512]{1,0:T(8,128)(2,1)S(1)} %fusion.16.refs_0_), channel_id=1, source_target_pairs={{0,6},{1,7},{2,4},{3,5},{4,2},{5,3},{6,0},{7,1},{8,14},{9,15},{10,... | collective-permute-start | bytes 393224 | tf_op jit(solution)/shard_map/ppermute | solution.py:16
  117.1 11.1 %collective-permute-start.23 = (bf16[128,512]{1,0:T(8,128)(2,1)S(1)}, bf16[128,512]{1,0:T(8,128)(2,1)S(1)}, u32[]{:S(2)}, u32[]{:S(2)}) collective-permute-start(bf16[128,512]{1,0:T(8,128)(2,1)S(1)} %fusion.16.refs_0_), channel_id=1, source_target_pairs={{0,4},{1,5},{2,6},{3,7},{4,0},{5,1},{6,2},{7,3},{8,12},{9,13},{10,... | collective-permute-start | bytes 393224 | tf_op jit(solution)/shard_map/ppermute | solution.py:16
  117.1 11.1 %collective-permute-start.22 = (bf16[128,512]{1,0:T(8,128)(2,1)S(1)}, bf16[128,512]{1,0:T(8,128)(2,1)S(1)}, u32[]{:S(2)}, u32[]{:S(2)}) collective-permute-start(bf16[128,512]{1,0:T(8,128)(2,1)S(1)} %fusion.16.refs_0_), channel_id=1, source_target_pairs={{0,2},{1,3},{2,0},{3,1},{4,6},{5,7},{6,4},{7,5},{8,10},{9,11},{10,... | collective-permute-start | bytes 393224 | tf_op jit(solution)/shard_map/ppermute | solution.py:16
  119.9 1.1 copy-start.6
  130.5 3.8 %collective-permute-start.25 = (bf16[4,400,512]{2,1,0:T(8,128)(2,1)S(1)}, bf16[4,400,512]{2,1,0:T(8,128)(2,1)}, u32[]{:S(2)}, u32[]{:S(2)}) collective-permute-start(bf16[4,400,512]{2,1,0:T(8,128)(2,1)S(1)} %all-to-all-done.3.own_ref), channel_id=1, source_target_pairs={{0,1},{1,0},{2,3},{3,2},{4,5},{5,4},{6,7},{7,6},{8,9},{9,8},{10,11... | collective-permute-start | bytes 4915208 | tf_op jit(solution)/shard_map/ppermute | solution.py:16
  130.5 25.3 %all-to-all-start.2 = ((bf16[4,400,512]{2,1,0:T(8,128)(2,1)}), bf16[4,400,512]{2,1,0:T(8,128)(2,1)S(1)}, u32[]{:S(2)}, u32[]{:S(2)}) async-start(bf16[4,400,512]{2,1,0:T(8,128)(2,1)} %dispatch.3), calls=%async_computation.2 | async-start | bytes 3276800 | tf_op jit(solution)/shard_map/all_to_all | solution.py:563
  134.3 3.4 %copy-start.2 = (bf16[1,4096,1024]{2,1,0:T(8,128)(2,1)S(1)}, bf16[1,4096,1024]{2,1,0:T(8,128)(2,1)}, u32[]{:S(2)}) copy-start(bf16[1,4096,1024]{2,1,0:T(8,128)(2,1)} %param.15) | copy-start | bytes 25165828
  150.0 1.7 copy-start.3
  151.7 1.7 copy-start.4
  153.4 1.6 copy-start.5
  155.0 0.7 copy-start.9
  155.8 3.6 %collective-permute-start.26 = (bf16[4,400,512]{2,1,0:T(8,128)(2,1)S(1)}, bf16[4,400,512]{2,1,0:T(8,128)(2,1)S(1)}, u32[]{:S(2)}, u32[]{:S(2)}) collective-permute-start(bf16[4,400,512]{2,1,0:T(8,128)(2,1)S(1)} %all-to-all-done.2.own_ref), channel_id=1, source_target_pairs={{0,1},{1,0},{2,3},{3,2},{4,5},{5,4},{6,7},{7,6},{8,9},{9,8},{10,11... | collective-permute-start | bytes 4915208 | tf_op jit(solution)/shard_map/ppermute | solution.py:16
  159.3 1.0 copy-start.7
  160.3 1.4 copy-start.8
  161.7 1.0 copy-start.10

commit v2 on v1

--- a/solution.py
+++ b/solution.py
@@ -120,9 +120,9 @@
             out_ref[:, place] = share_ref[:, position_ref[2] ^ side]
 
 
-def dispatch_kernel(position_ref, ids_ref, extra_ref, *refs):
+def dispatch_kernel(offsets, position_ref, ids_ref, extra_ref, *refs):
     *token_refs, out_ref = refs
-    planes = len(token_refs)
+    planes = len(offsets)
     experts, _, part = out_ref.shape
     lanes = extra_ref.shape[0]
     count = out_ref.shape[1] - lanes
@@ -130,26 +130,26 @@
     tokens = ids_ref.shape[2]
     plane, core = position_ref[1], position_ref[2]
     slots = lax.broadcasted_iota(jnp.int32, (experts * capacity, tokens), 0)
-    for k in range(planes):
+    for k, token_ref in zip(offsets, token_refs):
         source = plane ^ k
         ids = ids_ref[source * 2 + core]
         code0 = ids[0:1] * capacity + ids[2:3]
         code1 = ids[1:2] * capacity + ids[3:4]
         one_hot = jnp.where((code0 == slots) | (code1 == slots), 1.0, 0.0).astype(jnp.bfloat16)
-        picked = jnp.dot(one_hot, token_refs[k][...], preferred_element_type=jnp.float32)
-        rows = pl.ds(pl.multiple_of(source * capacity, 16), capacity)
+        picked = jnp.dot(one_hot, token_ref[...], preferred_element_type=jnp.float32)
+        rows = pl.ds(pl.multiple_of(source % planes * capacity, 16), capacity)
         out_ref[:, rows] = picked.reshape(experts, capacity, part).astype(jnp.bfloat16)
     for e in range(experts):
         out_ref[e, count:] = extra_ref[...]
 
 
-def row_stats(flat_ref, side, aux_ref):
-    count = flat_ref.shape[0] // 2
+def row_stats(flat_ref, group, groups, aux_ref):
+    count = flat_ref.shape[0] // groups
     experts, lanes, part = aux_ref.shape
     squares = jnp.zeros((count, part), jnp.float32)
     logits = jnp.zeros((count, lanes), jnp.float32)
     for e in range(experts):
-        rows = flat_ref[side * count : (side + 1) * count, e * part : (e + 1) * part]
+        rows = flat_ref[group * count : (group + 1) * count, e * part : (e + 1) * part]
         aux = aux_ref[e]
         ratio = rows.astype(jnp.float32) * (1.0 / aux[0:1].astype(jnp.float32))
         squares = squares + ratio * ratio
@@ -160,26 +160,29 @@
     return jnp.where(lax.broadcasted_iota(jnp.int32, logits.shape, 1) == 0, total, logits)
 
 
-def row_copies(sides, flat_ref, aux_ref, sems):
-    count = flat_ref.shape[0] // 2
-    experts, _, part = aux_ref.shape
+def row_copies(sides, halves, flat_ref, aux_ref, sems):
+    count = flat_ref.shape[0] // (2 * halves)
+    experts, lanes, part = aux_ref.shape
     copies = [
-        pltpu.make_async_copy(sides[0].at[:, pl.ds(count, aux_ref.shape[1])], aux_ref, sems.at[0])
+        pltpu.make_async_copy(sides[0].at[:, pl.ds(halves * count, lanes)], aux_ref, sems.at[0])
     ]
-    for side, rows_ref in enumerate(sides):
-        for e in range(experts):
-            copies.append(
-                pltpu.make_async_copy(
-                    rows_ref.at[e, pl.ds(0, count)],
-                    flat_ref.at[pl.ds(side * count, count), pl.ds(e * part, part)],
-                    sems.at[1 + side * experts + e],
+    for half in range(halves):
+        for side, rows_ref in enumerate(sides):
+            for e in range(experts):
+                group = half * 2 + side
+                copies.append(
+                    pltpu.make_async_copy(
+                        rows_ref.at[e, pl.ds(half * count, count)],
+                        flat_ref.at[pl.ds(group * count, count), pl.ds(e * part, part)],
+                        sems.at[1 + group * experts + e],
+                    )
                 )
-            )
     return copies
 
 
-def turned(flat_ref, e, part):
-    return flat_ref[:, e * part : (e + 1) * part].T
+def turned(flat_ref, half, halves, e, part):
+    count = flat_ref.shape[0] // halves
+    return flat_ref[half * count : (half + 1) * count, e * part : (e + 1) * part].T
 
 
 def product(flat_ref, weight_ref):
@@ -205,7 +208,7 @@
     aux_scratch,
     sems,
 ):
-    count = flat_scratch.shape[0] // 2
+    count = flat_scratch.shape[0] // 4
     experts, _, part = aux_scratch.shape
 
     for t in range(tiles):
@@ -213,7 +216,7 @@
         @pl.when(pl.program_id(0) == t)
         def _():
             if t == 0:
-                copies = row_copies((own_ref, other_ref), flat_scratch, aux_scratch, sems)
+                copies = row_copies((own_ref, other_ref), 2, flat_scratch, aux_scratch, sems)
                 for copy in copies:
                     copy.start()
                 for copy in copies:
@@ -221,17 +224,19 @@
             gate_out[...] = product(flat_scratch, gate_ref)
             up_out[...] = product(flat_scratch, up_ref)
             for e in shares_of(experts, tiles, t):
-                turned_out[e] = turned(flat_scratch, e, part)
+                for half in range(2):
+                    turned_out[half, e] = turned(flat_scratch, half, 2, e, part)
             if t == tiles - 1:
-                for side in range(2):
-                    stats_out[side * count : (side + 1) * count] = row_stats(
-                        flat_scratch, side, aux_scratch
+                for group in range(4):
+                    stats_out[group * count : (group + 1) * count] = row_stats(
+                        flat_scratch, group, 4, aux_scratch
                     )
 
 
 def late_kernel(
     width,
     tiles,
+    which,
     position_ref,
     own_ref,
     other_ref,
@@ -243,34 +248,39 @@
     stats_ref,
     signs_ref,
     cot_ref,
-    hidden_out,
-    grad_gate_out,
-    grad_up_out,
-    flat_scratch,
-    aux_scratch,
-    scale_scratch,
-    weight_scratch,
-    gate_scratch,
-    up_scratch,
-    d_gate_scratch,
-    d_up_scratch,
-    turned_scratch,
-    sems,
+    *refs,
 ):
+    (
+        hidden_out,
+        grad_gate_out,
+        grad_up_out,
+        flat_scratch,
+        aux_scratch,
+        scale_scratch,
+        weight_scratch,
+        gate_scratch,
+        up_scratch,
+        d_gate_scratch,
+        d_up_scratch,
+        turned_scratch,
+        sems,
+    ) = refs[-13:]
+    earlier = refs[1:3] if which else (None, None)
     step = pl.program_id(0)
     core = position_ref[2]
     planes, _, capacity, tile = hidden_out.shape
     count = planes * capacity
     experts, _, part = aux_scratch.shape
     lanes = stats_ref.shape[1]
+    half = position_ref[1] // planes ^ which
     turn_copy = pltpu.make_async_copy(
-        turned_ref, turned_scratch.at[:, pl.ds(0, part)], sems.at[1 + 2 * experts]
+        turned_ref.at[half], turned_scratch.at[:, pl.ds(0, part)], sems.at[1 + 2 * experts]
     )
 
     def scales():
         for side in range(2):
             span = slice(side * count, (side + 1) * count)
-            stats = stats_ref[span] + row_stats(flat_scratch, side, aux_scratch)
+            stats = stats_ref[span] + row_stats(flat_scratch, side, 2, aux_scratch)
             inverse = lax.rsqrt(stats[:, 0:1] / width + 1e-05)
             signs = signs_ref[:, pl.ds(core ^ side, 1)].reshape(count, lanes)
             filled = signs[:, lanes - 1 :]
@@ -303,17 +313,22 @@
         e = (step - tiles) % experts
         stretch_units = grad_gate_out.shape[2]
         span = slice(stretch * stretch_units, (stretch + 1) * stretch_units)
-        for scratch, out in ((d_gate_scratch, grad_gate_out), (d_up_scratch, grad_up_out)):
-            out[0] = jnp.dot(
+        for scratch, before, out in zip(
+            (d_gate_scratch, d_up_scratch), earlier, (grad_gate_out, grad_up_out)
+        ):
+            total = jnp.dot(
                 turned_scratch[e], scratch[:, span], preferred_element_type=jnp.float32
-            ).astype(jnp.bfloat16)
+            )
+            if before is not None:
+                total = total + before[0].astype(jnp.float32)
+            out[0] = total.astype(jnp.bfloat16)
 
     for t in range(tiles):
 
         @pl.when(step == t)
         def _():
             if t == 0:
-                copies = row_copies((own_ref, other_ref), flat_scratch, aux_scratch, sems)
+                copies = row_copies((own_ref, other_ref), 1, flat_scratch, aux_scratch, sems)
                 for copy in copies:
                     copy.start()
                 turn_copy.start()
@@ -322,7 +337,7 @@
             gate_scratch[t % 2] = gate_acc[...] + product(flat_scratch, gate_ref)
             up_scratch[t % 2] = up_acc[...] + product(flat_scratch, up_ref)
             for e in shares_of(experts, tiles, t):
-                turned_scratch[e, part:] = turned(flat_scratch, e, part)
+                turned_scratch[e, part:] = turned(flat_scratch, 0, 1, e, part)
             if t == 0:
                 scales()
             else:
@@ -509,20 +524,19 @@
             hstate = hstate + value.astype(jnp.float32)
         return (hstate * norm_gain[span].astype(jnp.float32)).astype(jnp.bfloat16)
 
-    height = count + lanes
-
-    def slots_of(c, own_tokens):
+    def slots_of(c, own_tokens, offsets):
+        height = len(offsets) * capacity + lanes
         return pl.pallas_call(
-            dispatch_kernel,
+            functools.partial(dispatch_kernel, tuple(offsets)),
             out_shape=jax.ShapeDtypeStruct((experts, height, part), jnp.bfloat16),
             in_specs=[smem(), whole(ids_all.shape)]
             + [pl.BlockSpec((lanes, part), lambda i, c=c: (0, c))]
-            + [whole((tokens, part))] * planes,
+            + [whole((tokens, part))] * len(offsets),
             out_specs=whole((experts, height, part)),
             grid=(1,),
             compiler_params=params(),
             name="dispatch",
-        )(position, ids_all, extra, *own_tokens)
+        )(position, ids_all, extra, *[own_tokens[k] for k in offsets])
 
     merged0 = merged_of(0)
     got = branch_exchange(0, packed1)
@@ -553,16 +567,16 @@
     sends1 = plane_sends(pair1)
     arrived1 = plane_exchange(sends1)
 
-    slots0 = slots_of(0, after(tokens0, sends1))
+    slots0 = slots_of(0, after(tokens0, sends1), range(planes))
     scaled1 = scaled_of(1, pair1, after(arrived1, slots0))
     tokens1 = [scaled1] + plane_exchange([scaled1] * (planes - 1))
-    slots1 = slots_of(1, tokens1)
-    slots = (slots0, slots1)
-
-    def to_experts(c):
-        return lax.all_to_all(slots[c], "expert", split_axis=0, concat_axis=0, tiled=True)
-
-    rows = after(to_experts(0), slots[-1], merged_out, signs)
+    near = slots_of(1, tokens1, range(planes // 2))
+    far = slots_of(1, tokens1, range(planes // 2, planes))
+
+    def to_experts(slots):
+        return lax.all_to_all(slots, "expert", split_axis=0, concat_axis=0, tiled=True)
+
+    rows = after(to_experts(slots0), far, merged_out, signs)
     other = exchange(rows, "fsdp", 1)
     weight_spec = pl.BlockSpec((experts, 1, part, tile), lambda n: (0, 0, 0, n))
     sums = jax.ShapeDtypeStruct((2 * count, units), jnp.float32)
@@ -578,17 +592,17 @@
             sums,
             sums,
             jax.ShapeDtypeStruct((2 * count, lanes), jnp.float32),
-            jax.ShapeDtypeStruct((experts, part, 2 * count), jnp.bfloat16),
+            jax.ShapeDtypeStruct((2, experts, part, count), jnp.bfloat16),
         ),
         in_specs=[any_spec, any_spec, weight_spec, weight_spec],
         out_specs=(
             sum_spec,
             sum_spec,
             whole((2 * count, lanes)),
-            whole((experts, part, 2 * count)),
+            whole((2, experts, part, count)),
         ),
         grid=(tiles,),
-        scratch_shapes=row_scratch + [pltpu.SemaphoreType.DMA((1 + 2 * experts,))],
+        scratch_shapes=row_scratch + [pltpu.SemaphoreType.DMA((1 + 4 * experts,))],
         compiler_params=params(32),
         cost_estimate=pl.CostEstimate(
             flops=8 * count * experts * part * units,
@@ -597,58 +611,95 @@
         ),
         name="early",
     )(rows, other, gate_view, up_view)
-    rows = after(to_experts(1), partial)
-    other = exchange(rows, "fsdp", 1)
-
     tile_of = lambda i: jnp.minimum(i, tiles - 1)
     behind = lambda i: jnp.clip(i - 1, 0, tiles - 1)
     place_of = lambda i: jnp.maximum(i - tiles, 0)
-    weight_spec = pl.BlockSpec((experts, 1, part, tile), lambda i: (0, 1, 0, tile_of(i)))
-    sum_spec = pl.BlockSpec((2 * count, tile), lambda i: (0, tile_of(i)))
-    unit_spec = pl.BlockSpec((planes, 2, capacity, tile), lambda i: (0, 0, 0, behind(i)))
-    grad_spec = pl.BlockSpec(
-        (1, columns, stretch), lambda i: (place_of(i) % experts, 0, place_of(i) // experts)
-    )
+    gate_sums, up_sums, stats, turned_rows = partial
     grad_shape = jax.ShapeDtypeStruct((experts, columns, units), jnp.bfloat16)
-    gate_sums, up_sums, stats, turned_rows = partial
-    hidden, grad_gate, grad_up = pl.pallas_call(
-        functools.partial(late_kernel, float(width), tiles),
-        out_shape=(
-            jax.ShapeDtypeStruct((planes, 2, capacity, units), jnp.bfloat16),
-            grad_shape,
-            grad_shape,
-        ),
-        in_specs=[smem(), any_spec, any_spec, any_spec]
-        + [weight_spec, weight_spec, sum_spec, sum_spec]
-        + [whole(stats.shape), whole(signs.shape), unit_spec],
-        out_specs=(unit_spec, grad_spec, grad_spec),
-        grid=(tiles + experts * (units // stretch),),
-        scratch_shapes=row_scratch
-        + [
-            pltpu.VMEM((2 * count, 1), jnp.float32),
-            pltpu.VMEM((2 * count, 1), jnp.float32),
-            pltpu.VMEM((2, 2 * count, tile), jnp.float32),
-            pltpu.VMEM((2, 2 * count, tile), jnp.float32),
-            pltpu.VMEM((2 * count, units), jnp.bfloat16),
-            pltpu.VMEM((2 * count, units), jnp.bfloat16),
-            pltpu.VMEM((experts, columns, 2 * count), jnp.bfloat16),
-            pltpu.SemaphoreType.DMA((2 + 2 * experts,)),
-        ],
-        compiler_params=params(48),
-        name="late",
-    )(
-        position,
-        rows,
-        other,
-        turned_rows,
-        gate_view,
-        up_view,
-        gate_sums,
-        up_sums,
-        stats,
-        signs,
-        cot_hidden.reshape(planes, 2, capacity, units),
-    )
+    half_planes = planes // 2
+    near, far = to_experts(near), to_experts(far)
+    near = after(near, partial)
+    near_other = exchange(near, "fsdp", 1)
+    far = after(far, near_other)
+    far_other = exchange(far, "fsdp", 1)
+    result = ()
+    for which, (own_rows, other_rows) in enumerate(((near, near_other), (far, far_other))):
+
+        def half_of(position_ref, which=which):
+            return position_ref[1] // half_planes ^ which
+
+        weight_spec = pl.BlockSpec(
+            (experts, 1, part, tile), lambda i, position_ref: (0, 1, 0, tile_of(i))
+        )
+        sum_spec = pl.BlockSpec(
+            (count, tile), lambda i, position_ref: (half_of(position_ref), tile_of(i))
+        )
+        stats_spec = pl.BlockSpec(
+            (count, lanes), lambda i, position_ref: (half_of(position_ref), 0)
+        )
+        signs_spec = pl.BlockSpec(
+            (half_planes, 2, capacity, lanes),
+            lambda i, position_ref: (half_of(position_ref), 0, 0, 0),
+        )
+        unit_spec = pl.BlockSpec(
+            (half_planes, 2, capacity, tile),
+            lambda i, position_ref: (half_of(position_ref), 0, 0, behind(i)),
+        )
+        grad_spec = pl.BlockSpec(
+            (1, columns, stretch),
+            lambda i, position_ref: (place_of(i) % experts, 0, place_of(i) // experts),
+        )
+        result = pl.pallas_call(
+            functools.partial(late_kernel, float(width), tiles, which),
+            out_shape=(
+                jax.ShapeDtypeStruct((planes, 2, capacity, units), jnp.bfloat16),
+                grad_shape,
+                grad_shape,
+            ),
+            grid_spec=pltpu.PrefetchScalarGridSpec(
+                num_scalar_prefetch=1,
+                grid=(tiles + experts * (units // stretch),),
+                in_specs=[any_spec, any_spec, any_spec]
+                + [weight_spec, weight_spec, sum_spec, sum_spec]
+                + [stats_spec, signs_spec, unit_spec]
+                + [any_spec, grad_spec, grad_spec][: len(result)],
+                out_specs=(unit_spec, grad_spec, grad_spec),
+                scratch_shapes=[
+                    pltpu.VMEM((count, experts * part), jnp.bfloat16),
+                    pltpu.VMEM((experts, lanes, part), jnp.bfloat16),
+                    pltpu.VMEM((count, 1), jnp.float32),
+                    pltpu.VMEM((count, 1), jnp.float32),
+                    pltpu.VMEM((2, count, tile), jnp.float32),
+                    pltpu.VMEM((2, count, tile), jnp.float32),
+                    pltpu.VMEM((count, units), jnp.bfloat16),
+                    pltpu.VMEM((count, units), jnp.bfloat16),
+                    pltpu.VMEM((experts, columns, count), jnp.bfloat16),
+                    pltpu.SemaphoreType.DMA((2 + 2 * experts,)),
+                ],
+            ),
+            input_output_aliases={11: 0} if which else {},
+            compiler_params=params(48),
+            cost_estimate=pl.CostEstimate(
+                flops=4 * count * experts * (part + columns) * units,
+                bytes_accessed=8 * experts * columns * units,
+                transcendentals=0,
+            ),
+            name="late" if which else "middle",
+        )(
+            position,
+            own_rows,
+            other_rows,
+            turned_rows,
+            gate_view,
+            up_view,
+            gate_sums,
+            up_sums,
+            stats,
+            signs,
+            cot_hidden.reshape(planes, 2, capacity, units),
+            *result,
+        )
+    hidden, grad_gate, grad_up = result
     return (
         merged_out,
         hidden.reshape(1, -1, units),

time: 194 us -> 230 us (1.19)
  Pallas kernels: 51.5 us -> 70.5 us
  blocking collectives: 0 us -> 16.6 us
  waiting for transfers between devices: 59.3 us -> 61.8 us
    pallas_call x3 -> x5, Pallas kernels: 34.3 us -> 53.2 us  [the longest x2 48.3 us: per_device(): pl.pallas_call(functools.partial(late_kernel, float(width), tiles, which)...]
    all_to_all x0 -> x1, blocking collectives: none -> 16.6 us  [to_experts(): lax.all_to_all(slots, 'expert', split_axis=0, concat_axis=0, tiled=True)]
    unnamed x47 -> x41, local copies, waits for them, and re-layouts: 17.7 us -> 14.9 us
    ppermute x27 -> x28, waiting for transfers between devices: 53.9 us -> 56.4 us  [exchange(): return lax.ppermute(value, axis, [(i, i ^ offset) for i in range(size)])]
    ppermute x27 -> x28, starting transfers between devices: 30.3 us -> 28 us  [exchange(): return lax.ppermute(value, axis, [(i, i ^ offset) for i in range(size)])]
  transfers between devices with their start and end apart: 31 -> 32, of which waited for: 19 -> 19; matrix products, arithmetic and copies ran while one was open for 6% -> 6% of each run, Pallas kernels for 9% -> 18%
where the time goes in v2:
time: 230 us; the launch traced here: 228 us
  Pallas kernels  70.5 us (31%)
  waiting for transfers between devices  61.8 us (27%)
  starting transfers between devices  46 us (20%)
  local copies, waits for them, and re-layouts  18.7 us (8%)
  blocking collectives  16.6 us (7%)
  other arithmetic  9.19 us (4%)
  matrix products  4.48 us (2%)
    ppermute x28, waiting for transfers between devices, exchange(): return lax.ppermute(value, axis, [(i, i ^ offset) for i in range(size)])  56.4 us
    pallas_call x2, Pallas kernels, per_device(): pl.pallas_call(functools.partial(late_kernel, float(width), tiles, which)...  48.3 us
    ppermute x28, starting transfers between devices, exchange(): return lax.ppermute(value, axis, [(i, i ^ offset) for i in range(size)])  28 us
    all_to_all x1, blocking collectives, to_experts(): lax.all_to_all(slots, 'expert', split_axis=0, concat_axis=0, tiled=True)  16.6 us
    unnamed x41, local copies, waits for them, and re-layouts  14.9 us
    pallas_call x1, Pallas kernels, per_device(): pl.pallas_call(functools.partial(early_kernel, tiles), out_shape=(sums, s...  12.3 us
    all_to_all x2, starting transfers between devices, to_experts(): lax.all_to_all(slots, 'expert', split_axis=0, concat_axis=0, tiled=True)  7.96 us
    all_to_all x1, waiting for transfers between devices, per_device(): lax.all_to_all(context.reshape(experts, quarter, columns), 'expert', spli...  5.3 us
  transfers between devices with their start and end apart: 32, of which 19 were waited for; matrix products, arithmetic and copies ran while one was open for 6% of the time, Pallas kernels for 18%

profile of v2, /device:TPU:0, one launch (start us, length us, event | category | flops | bytes accessed | tf_op | source)
XLA Modules:
  0.0 228.5 jit_solution(13248158969432205802)
XLA Ops:
  0.6 5.2 %all-to-all-start = ((bf16[4,32,1024]{2,1,0:T(8,128)(2,1)}), bf16[4,32,1024]{2,1,0:T(8,128)(2,1)S(1)}, u32[]{:S(2)}, u32[]{:S(2)}) async-start(bf16[4,32,1024]{2,1,0:T(8,128)(2,1)} %bitcast.116), calls=%async_computation | async-start | bytes 524288 | tf_op jit(solution)/shard_map/all_to_all | solution.py:451
  5.9 5.3 %all-to-all-done.shares_ref = bf16[4,32,1024]{2,1,0:T(8,128)(2,1)S(1)} async-done(((bf16[4,32,1024]{2,1,0:T(8,128)(2,1)}), bf16[4,32,1024]{2,1,0:T(8,128)(2,1)S(1)}, u32[]{:S(2)}, u32[]{:S(2)}) %all-to-all-start) | async-done | bytes 262176 | tf_op jit(solution)/shard_map/all_to_all | solution.py:451
  11.2 2.2 copy-done
  13.4 0.8 pack.2
  14.2 1.3 collective-permute-start
  16.9 4.9 %all-to-all-start.1 = ((bf16[8,48,512]{2,1,0:T(8,128)(2,1)}), bf16[8,48,512]{2,1,0:T(8,128)(2,1)S(1)}, u32[]{:S(2)}, u32[]{:S(2)}) async-start(bf16[8,48,512]{2,1,0:T(8,128)(2,1)} %spread.1), calls=%async_computation.1 | async-start | bytes 786432 | tf_op jit(solution)/shard_map/all_to_all | solution.py:467
  21.8 4.7 %collective-permute-done = bf16[2,256,512]{2,1,0:T(8,128)(2,1)S(1)} collective-permute-done((bf16[2,256,512]{2,1,0:T(8,128)(2,1)S(1)}, bf16[2,256,512]{2,1,0:T(8,128)(2,1)S(1)}, u32[]{:S(2)}, u32[]{:S(2)}) %collective-permute-start) | collective-permute-done | bytes 524320 | tf_op jit(solution)/shard_map/ppermute | solution.py:16
  26.5 1.0 collective-permute-done.1
  27.5 1.4 add_convert_fusion.2
  28.9 0.8 collective-permute-start.3
  29.7 1.5 collective-permute-start.2
  31.2 2.2 copy-done.1
  33.4 0.8 pack.3
  34.4 0.9 collective-permute-done.3
  36.1 1.7 collective-permute-start.6
  37.8 1.1 collective-permute-start.5
  39.7 1.5 add_bitcast_fusion.3
  41.3 5.0 %collective-permute-done.6 = bf16[8,32,512]{2,1,0:T(8,128)(2,1)S(1)} collective-permute-done((bf16[8,32,512]{2,1,0:T(8,128)(2,1)S(1)}, bf16[8,32,512]{2,1,0:T(8,128)(2,1)S(1)}, u32[]{:S(2)}, u32[]{:S(2)}) %collective-permute-start.6) | collective-permute-done | bytes 262176 | tf_op jit(solution)/shard_map/ppermute | solution.py:16
  46.3 3.2 %collective-permute-done.5 = bf16[8,32,512]{2,1,0:T(8,128)(2,1)S(1)} collective-permute-done((bf16[8,32,512]{2,1,0:T(8,128)(2,1)S(1)}, bf16[8,32,512]{2,1,0:T(8,128)(2,1)S(1)}, u32[]{:S(2)}, u32[]{:S(2)}) %collective-permute-start.5) | collective-permute-done | bytes 262176 | tf_op jit(solution)/shard_map/ppermute | solution.py:16
  50.2 1.2 convolution_convert_fusion.1
  51.5 1.4 collective-permute-start.7
  53.7 1.4 convert_add_fusion.1
  55.1 1.9 fusion.24
  56.9 1.7 collective-permute-start.14
  59.3 2.1 collective-permute-start.12
  61.3 4.6 %collective-permute-done.7 = bf16[2,256,512]{2,1,0:T(8,128)(2,1)} collective-permute-done((bf16[2,256,512]{2,1,0:T(8,128)(2,1)S(1)}, bf16[2,256,512]{2,1,0:T(8,128)(2,1)}, u32[]{:S(2)}, u32[]{:S(2)}) %collective-permute-start.7) | collective-permute-done | bytes 524320 | tf_op jit(solution)/shard_map/ppermute | solution.py:16
  65.9 1.1 collective-permute-done.8
  67.0 1.3 add_convert_fusion
  69.0 1.4 collective-permute-start.10
  70.5 1.3 collective-permute-done.13
  71.8 1.2 fusion.21.refs_0_
  73.0 3.0 %collective-permute-done.11 = bf16[1,256,512]{2,1,0:T(8,128)(2,1)S(1)} collective-permute-done((bf16[1,256,512]{2,1,0:T(8,128)(2,1)S(1)}, bf16[1,256,512]{2,1,0:T(8,128)(2,1)S(1)}, u32[]{:S(2)}, u32[]{:S(2)}) %collective-permute-start.11) | collective-permute-done | bytes 262176 | tf_op jit(solution)/shard_map/ppermute | solution.py:16
  76.8 1.5 add_bitcast_fusion.1
  79.0 0.9 slice_convert_fusion
  79.9 1.8 collective-permute-start.21
  82.1 2.2 collective-permute-start.19
  84.3 1.4 convert_add_fusion
  85.7 1.9 fusion.27
  88.2 6.4 %collective-permute-done.20.refs_2_ = bf16[128,512]{1,0:T(8,128)(2,1)S(1)} collective-permute-done((bf16[128,512]{1,0:T(8,128)(2,1)S(1)}, bf16[128,512]{1,0:T(8,128)(2,1)S(1)}, u32[]{:S(2)}, u32[]{:S(2)}) %collective-permute-start.20) | collective-permute-done | bytes 131104 | tf_op jit(solution)/shard_map/ppermute | solution.py:16
  94.6 2.3 dispatch.3
  96.9 3.6 %all-to-all-start.4 = ((bf16[4,400,512]{2,1,0:T(8,128)(2,1)}), bf16[4,400,512]{2,1,0:T(8,128)(2,1)S(1)}, u32[]{:S(2)}, u32[]{:S(2)}) async-start(bf16[4,400,512]{2,1,0:T(8,128)(2,1)} %dispatch.3), calls=%async_computation.4 | async-start | bytes 3276800 | tf_op jit(solution)/shard_map/all_to_all | solution.py:577
  100.5 2.7 %collective-permute-start.18 = (bf16[128,512]{1,0:T(8,128)(2,1)}, bf16[128,512]{1,0:T(8,128)(2,1)S(1)}, u32[]{:S(2)}, u32[]{:S(2)}) collective-permute-start(bf16[128,512]{1,0:T(8,128)(2,1)} %get-tuple-element.96), channel_id=1, source_target_pairs={{0,6},{1,7},{2,4},{3,5},{4,2},{5,3},{6,0},{7,1},{8,14},{9,15},{10,... | collective-permute-start | bytes 393224 | tf_op jit(solution)/shard_map/ppermute | solution.py:16
  103.2 1.7 collective-permute-start.16
  104.9 4.1 %collective-permute-done.18 = bf16[128,512]{1,0:T(8,128)(2,1)S(1)} collective-permute-done((bf16[128,512]{1,0:T(8,128)(2,1)}, bf16[128,512]{1,0:T(8,128)(2,1)S(1)}, u32[]{:S(2)}, u32[]{:S(2)}) %collective-permute-start.18) | collective-permute-done | bytes 131104 | tf_op jit(solution)/shard_map/ppermute | solution.py:16
  109.0 4.5 %collective-permute-done.17 = bf16[128,512]{1,0:T(8,128)(2,1)S(1)} collective-permute-done((bf16[128,512]{1,0:T(8,128)(2,1)}, bf16[128,512]{1,0:T(8,128)(2,1)S(1)}, u32[]{:S(2)}, u32[]{:S(2)}) %collective-permute-start.17) | collective-permute-done | bytes 131104 | tf_op jit(solution)/shard_map/ppermute | solution.py:16
  113.5 1.0 fusion.16.refs_0_
  114.6 2.4 %collective-permute-start.23 = (bf16[128,512]{1,0:T(8,128)(2,1)S(1)}, bf16[128,512]{1,0:T(8,128)(2,1)S(1)}, u32[]{:S(2)}, u32[]{:S(2)}) collective-permute-start(bf16[128,512]{1,0:T(8,128)(2,1)S(1)} %fusion.16.refs_0_), channel_id=1, source_target_pairs={{0,6},{1,7},{2,4},{3,5},{4,2},{5,3},{6,0},{7,1},{8,14},{9,15},{10,... | collective-permute-start | bytes 393224 | tf_op jit(solution)/shard_map/ppermute | solution.py:16
  117.0 0.8 signs.1
  117.8 1.1 join.1
  118.9 4.0 %collective-permute-done.23.refs_1_ = bf16[128,512]{1,0:T(8,128)(2,1)S(1)} collective-permute-done((bf16[128,512]{1,0:T(8,128)(2,1)S(1)}, bf16[128,512]{1,0:T(8,128)(2,1)S(1)}, u32[]{:S(2)}, u32[]{:S(2)}) %collective-permute-start.23) | collective-permute-done | bytes 131104 | tf_op jit(solution)/shard_map/ppermute | solution.py:16
  122.9 5.2 %collective-permute-done.22.refs_0_ = bf16[128,512]{1,0:T(8,128)(2,1)S(1)} collective-permute-done((bf16[128,512]{1,0:T(8,128)(2,1)S(1)}, bf16[128,512]{1,0:T(8,128)(2,1)S(1)}, u32[]{:S(2)}, u32[]{:S(2)}) %collective-permute-start.22) | collective-permute-done | bytes 131104 | tf_op jit(solution)/shard_map/ppermute | solution.py:16
  128.1 0.9 dispatch.4
  129.1 5.8 %collective-permute-done.24.refs_1_ = bf16[128,512]{1,0:T(8,128)(2,1)S(1)} collective-permute-done((bf16[128,512]{1,0:T(8,128)(2,1)S(1)}, bf16[128,512]{1,0:T(8,128)(2,1)S(1)}, u32[]{:S(2)}, u32[]{:S(2)}) %collective-permute-start.24) | collective-permute-done | bytes 131104 | tf_op jit(solution)/shard_map/ppermute | solution.py:16
  135.0 1.8 dispatch.5
  136.8 4.4 %all-to-all-start.3 = ((bf16[4,208,512]{2,1,0:T(8,128)(2,1)}), bf16[4,208,512]{2,1,0:T(8,128)(2,1)}, u32[]{:S(2)}, u32[]{:S(2)}) async-start(bf16[4,208,512]{2,1,0:T(8,128)(2,1)} %dispatch.5), calls=%async_computation.3 | async-start | bytes 1703936 | tf_op jit(solution)/shard_map/all_to_all | solution.py:577
  141.2 3.4 %copy-done.2 = bf16[1,4096,1024]{2,1,0:T(8,128)(2,1)S(1)} copy-done((bf16[1,4096,1024]{2,1,0:T(8,128)(2,1)S(1)}, bf16[1,4096,1024]{2,1,0:T(8,128)(2,1)}, u32[]{:S(2)}) %copy-start.2) | copy-done | bytes 8388632
  144.6 12.3 %early.1 = (f32[768,1024]{1,0:T(8,128)S(1)}, f32[768,1024]{1,0:T(8,128)S(1)}, f32[768,16]{1,0:T(8,128)S(1)}, bf16[2,4,512,384]{3,2,1,0:T(8,128)(2,1)S(1)}) custom-call(bf16[4,400,512]{2,1,0:T(8,128)(2,1)S(1)} %all-to-all-done.4.own_ref, bf16[4,400,512]{2,1,0:T(8,128)(2,1)} %collective-permute-done.25.other_ref, bf16[4,2,512,1024]{3,2,1,0:T(8,128)(2,1)S(1)} %bitcast.95, ...), custom_call_target="tpu_custom_call" | custom-call | flops 6442450944 | bytes 8388608 | tf_op jit(solution)/shard_map/early/pallas_call | solution.py:589
  156.9 1.7 copy-done.3
  158.6 1.7 copy-done.4
  160.3 1.6 copy-done.5
  161.9 16.6 %all_to_all.25.own_ref = bf16[4,208,512]{2,1,0:T(8,128)(2,1)S(1)} all-to-all(bf16[4,208,512]{2,1,0:T(8,128)(2,1)S(1)} %dispatch.4), channel_id=1, replica_groups=mesh['expert'=4,'fsdp'=8] {'expert'}, dimensions={0} | all-to-all | bytes 1703936 | tf_op jit(solution)/shard_map/all_to_all | solution.py:577
  178.6 1.4 copy-done.6
  180.0 22.8 %middle.1 = (bf16[4,2,96,1024]{3,2,1,0:T(8,128)(2,1)}, bf16[4,1024,1024]{2,1,0:T(8,128)(2,1)}, bf16[4,1024,1024]{2,1,0:T(8,128)(2,1)}) custom-call(s32[3]{0:T(128)S(1)} %pad_add_fusion.position_ref, bf16[4,208,512]{2,1,0:T(8,128)(2,1)} %all-to-all-done.3.own_ref, bf16[4,208,512]{2,1,0:T(8,128)(2,1)S(1)} %collective-permute-done.26.other_ref, ...), custom_call_target="tpu_custom_call" | custom-call | flops 9663676416 | bytes 33554432 | tf_op jit(solution)/shard_map/middle/pallas_call | solution.py:652
  202.8 25.4 %late.1 = (bf16[4,2,96,1024]{3,2,1,0:T(8,128)(2,1)}, bf16[4,1024,1024]{2,1,0:T(8,128)(2,1)}, bf16[4,1024,1024]{2,1,0:T(8,128)(2,1)}) custom-call(s32[3]{0:T(128)S(1)} %pad_add_fusion.position_ref, bf16[4,208,512]{2,1,0:T(8,128)(2,1)S(1)} %all_to_all.25.own_ref, ...), custom_call_target="tpu_custom_call", output_to_operand_aliasing={{0}: (11, {})} | custom-call | flops 9663676416 | bytes 33554432 | tf_op jit(solution)/shard_map/late/pallas_call | solution.py:652
  (78 shorter events, 8.7 us)
Async XLA Ops:
  0.6 10.5 %all-to-all-start = ((bf16[4,32,1024]{2,1,0:T(8,128)(2,1)}), bf16[4,32,1024]{2,1,0:T(8,128)(2,1)S(1)}, u32[]{:S(2)}, u32[]{:S(2)}) async-start(bf16[4,32,1024]{2,1,0:T(8,128)(2,1)} %bitcast.116), calls=%async_computation | async-start | bytes 524288 | tf_op jit(solution)/shard_map/all_to_all | solution.py:451
  11.2 2.2 copy-start
  13.4 2.7 %copy-start.18 = (s32[128,2]{0,1:T(2,128)S(1)}, s32[128,2]{0,1:T(2,128)}, u32[]{:S(2)}) copy-start(s32[128,2]{0,1:T(2,128)} %param.17) | copy-start | bytes 3076
  13.4 2.7 %copy-start.19 = (s32[128,2]{0,1:T(2,128)S(1)}, s32[128,2]{0,1:T(2,128)}, u32[]{:S(2)}) copy-start(s32[128,2]{0,1:T(2,128)} %param.18) | copy-start | bytes 3076
  14.2 12.3 %collective-permute-start = (bf16[2,256,512]{2,1,0:T(8,128)(2,1)S(1)}, bf16[2,256,512]{2,1,0:T(8,128)(2,1)S(1)}, u32[]{:S(2)}, u32[]{:S(2)}) collective-permute-start(bf16[2,256,512]{2,1,0:T(8,128)(2,1)S(1)} %get-tuple-element.47), channel_id=1, source_target_pairs={{0,8},{8,0},{16,24},{24,16},{1,9},{9,1},{17,25},{25,17},{2,10},{10... | collective-permute-start | bytes 1572872 | tf_op jit(solution)/shard_map/ppermute | solution.py:16
  15.5 12.0 %collective-permute-start.1 = (bf16[2,256,512]{2,1,0:T(8,128)(2,1)S(1)}, bf16[2,256,512]{2,1,0:T(8,128)(2,1)S(1)}, u32[]{:S(2)}, u32[]{:S(2)}) collective-permute-start(bf16[2,256,512]{2,1,0:T(8,128)(2,1)S(1)} %get-tuple-element.48), channel_id=1, source_target_pairs={{0,16},{8,24},{16,0},{24,8},{1,17},{9,25},{17,1},{25,9},{2,18},{10... | collective-permute-start | bytes 1572872 | tf_op jit(solution)/shard_map/ppermute | solution.py:16
  16.9 17.4 %all-to-all-start.1 = ((bf16[8,48,512]{2,1,0:T(8,128)(2,1)}), bf16[8,48,512]{2,1,0:T(8,128)(2,1)S(1)}, u32[]{:S(2)}, u32[]{:S(2)}) async-start(bf16[8,48,512]{2,1,0:T(8,128)(2,1)} %spread.1), calls=%async_computation.1 | async-start | bytes 786432 | tf_op jit(solution)/shard_map/all_to_all | solution.py:467
  26.5 4.7 %copy-start.8 = (bf16[2,256,512]{2,1,0:T(8,128)(2,1)}, bf16[2,256,512]{2,1,0:T(8,128)(2,1)S(1)}, u32[]{:S(2)}) copy-start(bf16[2,256,512]{2,1,0:T(8,128)(2,1)S(1)} %collective-permute-done) | copy-start | bytes 1572868
  27.5 3.7 %copy-start.10 = (bf16[2,256,512]{2,1,0:T(8,128)(2,1)}, bf16[2,256,512]{2,1,0:T(8,128)(2,1)S(1)}, u32[]{:S(2)}) copy-start(bf16[2,256,512]{2,1,0:T(8,128)(2,1)S(1)} %collective-permute-done.1) | copy-start | bytes 1572868
  28.9 6.4 %collective-permute-start.3 = (bf16[1,256,512]{2,1,0:T(8,128)(2,1)S(1)}, bf16[1,256,512]{2,1,0:T(8,128)(2,1)S(1)}, u32[]{:S(2)}, u32[]{:S(2)}) collective-permute-start(bf16[1,256,512]{2,1,0:T(8,128)(2,1)S(1)} %get-tuple-element.94), channel_id=1, source_target_pairs={{0,8},{8,0},{16,24},{24,16},{1,9},{9,1},{17,25},{25,17},{2,10},{10... | collective-permute-start | bytes 786440 | tf_op jit(solution)/shard_map/ppermute | solution.py:16
  29.7 6.4 %collective-permute-start.2 = (bf16[1,256,512]{2,1,0:T(8,128)(2,1)S(1)}, bf16[1,256,512]{2,1,0:T(8,128)(2,1)S(1)}, u32[]{:S(2)}, u32[]{:S(2)}) collective-permute-start(bf16[1,256,512]{2,1,0:T(8,128)(2,1)S(1)} %get-tuple-element.95), channel_id=1, source_target_pairs={{0,16},{8,24},{16,0},{24,8},{1,17},{9,25},{17,1},{25,9},{2,18},{10... | collective-permute-start | bytes 786440 | tf_op jit(solution)/shard_map/ppermute | solution.py:16
  31.2 2.2 copy-start.1
  33.4 6.3 %copy-start.9 = (bf16[2,256,512]{2,1,0:T(8,128)(2,1)S(1)}, bf16[2,256,512]{2,1,0:T(8,128)(2,1)}, u32[]{:S(2)}) copy-start(bf16[2,256,512]{2,1,0:T(8,128)(2,1)} %copy-done.8) | copy-start | bytes 1572868
  34.4 4.5 %copy-start.7 = (bf16[8,48,512]{2,1,0:T(8,128)(2,1)}, bf16[8,48,512]{2,1,0:T(8,128)(2,1)S(1)}, u32[]{:S(2)}) copy-start(bf16[8,48,512]{2,1,0:T(8,128)(2,1)S(1)} %all-to-all-done.1) | copy-start | bytes 1179652
  35.3 0.8 copy-start.14
  36.1 2.8 %copy-start.15 = (bf16[1,256,512]{2,1,0:T(8,128)(2,1)}, bf16[1,256,512]{2,1,0:T(8,128)(2,1)S(1)}, u32[]{:S(2)}) copy-start(bf16[1,256,512]{2,1,0:T(8,128)(2,1)S(1)} %collective-permute-done.2) | copy-start | bytes 786436
  36.1 10.2 %collective-permute-start.6 = (bf16[8,32,512]{2,1,0:T(8,128)(2,1)S(1)}, bf16[8,32,512]{2,1,0:T(8,128)(2,1)S(1)}, u32[]{:S(2)}, u32[]{:S(2)}) collective-permute-start(bf16[8,32,512]{2,1,0:T(8,128)(2,1)S(1)} %slice.18), channel_id=1, source_target_pairs={{0,24},{8,16},{16,8},{24,0},{1,25},{9,17},{17,9},{25,1},{2,26},{10... | collective-permute-start | bytes 786440 | tf_op jit(solution)/shard_map/ppermute | solution.py:16
  37.8 11.8 %collective-permute-start.5 = (bf16[8,32,512]{2,1,0:T(8,128)(2,1)S(1)}, bf16[8,32,512]{2,1,0:T(8,128)(2,1)S(1)}, u32[]{:S(2)}, u32[]{:S(2)}) collective-permute-start(bf16[8,32,512]{2,1,0:T(8,128)(2,1)S(1)} %slice.18), channel_id=1, source_target_pairs={{0,16},{8,24},{16,0},{24,8},{1,17},{9,25},{17,1},{25,9},{2,18},{10... | collective-permute-start | bytes 786440 | tf_op jit(solution)/shard_map/ppermute | solution.py:16
  38.9 10.7 %collective-permute-start.4 = (bf16[8,32,512]{2,1,0:T(8,128)(2,1)S(1)}, bf16[8,32,512]{2,1,0:T(8,128)(2,1)S(1)}, u32[]{:S(2)}, u32[]{:S(2)}) collective-permute-start(bf16[8,32,512]{2,1,0:T(8,128)(2,1)S(1)} %slice.18), channel_id=1, source_target_pairs={{0,8},{8,0},{16,24},{24,16},{1,9},{9,1},{17,25},{25,17},{2,10},{10... | collective-permute-start | bytes 786440 | tf_op jit(solution)/shard_map/ppermute | solution.py:16
  41.3 29.2 %copy-start.16 = (bf16[1024]{0:T(1024)(128)(2,1)S(1)}, bf16[1024]{0:T(1024)(128)(2,1)}, u32[]{:S(2)}) copy-start(bf16[1024]{0:T(1024)(128)(2,1)} %param.13) | copy-start | bytes 6148
  41.3 30.5 %copy-start.11 = (bf16[128,1024]{1,0:T(8,128)(2,1)S(1)}, bf16[128,1024]{1,0:T(8,128)(2,1)}, u32[]{:S(2)}) copy-start(bf16[128,1024]{1,0:T(8,128)(2,1)} %param.12) | copy-start | bytes 786436
  51.5 2.2 collective-permute-start.9
  51.5 14.4 %collective-permute-start.7 = (bf16[2,256,512]{2,1,0:T(8,128)(2,1)S(1)}, bf16[2,256,512]{2,1,0:T(8,128)(2,1)}, u32[]{:S(2)}, u32[]{:S(2)}) collective-permute-start(bf16[2,256,512]{2,1,0:T(8,128)(2,1)S(1)} %get-tuple-element.56), channel_id=1, source_target_pairs={{0,8},{8,0},{16,24},{24,16},{1,9},{9,1},{17,25},{25,17},{2,10},{10... | collective-permute-start | bytes 1572872 | tf_op jit(solution)/shard_map/ppermute | solution.py:16
  52.9 14.1 %collective-permute-start.8 = (bf16[2,256,512]{2,1,0:T(8,128)(2,1)S(1)}, bf16[2,256,512]{2,1,0:T(8,128)(2,1)}, u32[]{:S(2)}, u32[]{:S(2)}) collective-permute-start(bf16[2,256,512]{2,1,0:T(8,128)(2,1)S(1)} %get-tuple-element.57), channel_id=1, source_target_pairs={{0,16},{8,24},{16,0},{24,8},{1,17},{9,25},{17,1},{25,9},{2,18},{10... | collective-permute-start | bytes 1572872 | tf_op jit(solution)/shard_map/ppermute | solution.py:16
  56.9 22.0 %copy-start.17 = (bf16[1024,4]{0,1:T(4,128)(2,1)S(1)}, bf16[1024,4]{0,1:T(4,128)(2,1)}, u32[]{:S(2)}) copy-start(bf16[1024,4]{0,1:T(4,128)(2,1)} %param.14) | copy-start | bytes 24580
  56.9 13.5 %collective-permute-start.14 = (bf16[128,512]{1,0:T(8,128)(2,1)}, bf16[128,512]{1,0:T(8,128)(2,1)}, u32[]{:S(2)}, u32[]{:S(2)}) collective-permute-start(bf16[128,512]{1,0:T(8,128)(2,1)} %get-tuple-element.99), channel_id=1, source_target_pairs={{0,6},{1,7},{2,4},{3,5},{4,2},{5,3},{6,0},{7,1},{8,14},{9,15},{10,... | collective-permute-start | bytes 393224 | tf_op jit(solution)/shard_map/ppermute | solution.py:16
  58.6 13.1 %collective-permute-start.13 = (bf16[128,512]{1,0:T(8,128)(2,1)}, bf16[128,512]{1,0:T(8,128)(2,1)}, u32[]{:S(2)}, u32[]{:S(2)}) collective-permute-start(bf16[128,512]{1,0:T(8,128)(2,1)} %get-tuple-element.100), channel_id=1, source_target_pairs={{0,4},{1,5},{2,6},{3,7},{4,0},{5,1},{6,2},{7,3},{8,12},{9,13},{10,... | collective-permute-start | bytes 393224 | tf_op jit(solution)/shard_map/ppermute | solution.py:16
  59.3 12.5 %collective-permute-start.12 = (bf16[128,512]{1,0:T(8,128)(2,1)}, bf16[128,512]{1,0:T(8,128)(2,1)}, u32[]{:S(2)}, u32[]{:S(2)}) collective-permute-start(bf16[128,512]{1,0:T(8,128)(2,1)} %get-tuple-element.101), channel_id=1, source_target_pairs={{0,2},{1,3},{2,0},{3,1},{4,6},{5,7},{6,4},{7,5},{8,10},{9,11},{10,... | collective-permute-start | bytes 393224 | tf_op jit(solution)/shard_map/ppermute | solution.py:16
  68.4 7.7 %collective-permute-start.11 = (bf16[1,256,512]{2,1,0:T(8,128)(2,1)S(1)}, bf16[1,256,512]{2,1,0:T(8,128)(2,1)S(1)}, u32[]{:S(2)}, u32[]{:S(2)}) collective-permute-start(bf16[1,256,512]{2,1,0:T(8,128)(2,1)S(1)} %get-tuple-element.90), channel_id=1, source_target_pairs={{0,8},{8,0},{16,24},{24,16},{1,9},{9,1},{17,25},{25,17},{2,10},{10... | collective-permute-start | bytes 786440 | tf_op jit(solution)/shard_map/ppermute | solution.py:16
  69.0 7.7 %collective-permute-start.10 = (bf16[1,256,512]{2,1,0:T(8,128)(2,1)S(1)}, bf16[1,256,512]{2,1,0:T(8,128)(2,1)}, u32[]{:S(2)}, u32[]{:S(2)}) collective-permute-start(bf16[1,256,512]{2,1,0:T(8,128)(2,1)S(1)} %get-tuple-element.91), channel_id=1, source_target_pairs={{0,16},{8,24},{16,0},{24,8},{1,17},{9,25},{17,1},{25,9},{2,18},{10... | collective-permute-start | bytes 786440 | tf_op jit(solution)/shard_map/ppermute | solution.py:16
  76.0 0.7 copy-start.13
  78.9 5.5 %collective-permute-start.15 = (bf16[4,128,512]{2,1,0:T(8,128)(2,1)S(1)}, bf16[4,128,512]{2,1,0:T(8,128)(2,1)S(1)}, u32[]{:S(2)}, u32[]{:S(2)}) collective-permute-start(bf16[4,128,512]{2,1,0:T(8,128)(2,1)S(1)} %convolution_convert_fusion), channel_id=1, source_target_pairs={{0,1},{1,0},{2,3},{3,2},{4,5},{5,4},{6,7},{7,6},{8,9},{9,8},{10,11... | collective-permute-start | bytes 1572872 | tf_op jit(solution)/shard_map/ppermute | solution.py:16
  79.9 33.7 %copy-start.12 = (bf16[128,1024]{1,0:T(8,128)(2,1)S(1)}, bf16[128,1024]{1,0:T(8,128)(2,1)}, u32[]{:S(2)}) copy-start(bf16[128,1024]{1,0:T(8,128)(2,1)} %param.12) | copy-start | bytes 786436
  79.9 8.3 %collective-permute-start.21 = (bf16[128,512]{1,0:T(8,128)(2,1)S(1)}, bf16[128,512]{1,0:T(8,128)(2,1)S(1)}, u32[]{:S(2)}, u32[]{:S(2)}) collective-permute-start(bf16[128,512]{1,0:T(8,128)(2,1)S(1)} %fusion.21.refs_0_), channel_id=1, source_target_pairs={{0,6},{1,7},{2,4},{3,5},{4,2},{5,3},{6,0},{7,1},{8,14},{9,15},{10,... | collective-permute-start | bytes 393224 | tf_op jit(solution)/shard_map/ppermute | solution.py:16
  81.6 13.0 %collective-permute-start.20 = (bf16[128,512]{1,0:T(8,128)(2,1)S(1)}, bf16[128,512]{1,0:T(8,128)(2,1)S(1)}, u32[]{:S(2)}, u32[]{:S(2)}) collective-permute-start(bf16[128,512]{1,0:T(8,128)(2,1)S(1)} %fusion.21.refs_0_), channel_id=1, source_target_pairs={{0,4},{1,5},{2,6},{3,7},{4,0},{5,1},{6,2},{7,3},{8,12},{9,13},{10,... | collective-permute-start | bytes 393224 | tf_op jit(solution)/shard_map/ppermute | solution.py:16
  82.1 12.5 %collective-permute-start.19 = (bf16[128,512]{1,0:T(8,128)(2,1)S(1)}, bf16[128,512]{1,0:T(8,128)(2,1)S(1)}, u32[]{:S(2)}, u32[]{:S(2)}) collective-permute-start(bf16[128,512]{1,0:T(8,128)(2,1)S(1)} %fusion.21.refs_0_), channel_id=1, source_target_pairs={{0,2},{1,3},{2,0},{3,1},{4,6},{5,7},{6,4},{7,5},{8,10},{9,11},{10,... | collective-permute-start | bytes 393224 | tf_op jit(solution)/shard_map/ppermute | solution.py:16
  96.9 32.1 %all-to-all-start.4 = ((bf16[4,400,512]{2,1,0:T(8,128)(2,1)}), bf16[4,400,512]{2,1,0:T(8,128)(2,1)S(1)}, u32[]{:S(2)}, u32[]{:S(2)}) async-start(bf16[4,400,512]{2,1,0:T(8,128)(2,1)} %dispatch.3), calls=%async_computation.4 | async-start | bytes 3276800 | tf_op jit(solution)/shard_map/all_to_all | solution.py:577
  100.5 8.5 %collective-permute-start.18 = (bf16[128,512]{1,0:T(8,128)(2,1)}, bf16[128,512]{1,0:T(8,128)(2,1)S(1)}, u32[]{:S(2)}, u32[]{:S(2)}) collective-permute-start(bf16[128,512]{1,0:T(8,128)(2,1)} %get-tuple-element.96), channel_id=1, source_target_pairs={{0,6},{1,7},{2,4},{3,5},{4,2},{5,3},{6,0},{7,1},{8,14},{9,15},{10,... | collective-permute-start | bytes 393224 | tf_op jit(solution)/shard_map/ppermute | solution.py:16
  103.2 10.4 %collective-permute-start.17 = (bf16[128,512]{1,0:T(8,128)(2,1)}, bf16[128,512]{1,0:T(8,128)(2,1)S(1)}, u32[]{:S(2)}, u32[]{:S(2)}) collective-permute-start(bf16[128,512]{1,0:T(8,128)(2,1)} %get-tuple-element.97), channel_id=1, source_target_pairs={{0,4},{1,5},{2,6},{3,7},{4,0},{5,1},{6,2},{7,3},{8,12},{9,13},{10,... | collective-permute-start | bytes 393224 | tf_op jit(solution)/shard_map/ppermute | solution.py:16
  103.2 10.4 %collective-permute-start.16 = (bf16[128,512]{1,0:T(8,128)(2,1)}, bf16[128,512]{1,0:T(8,128)(2,1)S(1)}, u32[]{:S(2)}, u32[]{:S(2)}) collective-permute-start(bf16[128,512]{1,0:T(8,128)(2,1)} %get-tuple-element.98), channel_id=1, source_target_pairs={{0,2},{1,3},{2,0},{3,1},{4,6},{5,7},{6,4},{7,5},{8,10},{9,11},{10,... | collective-permute-start | bytes 393224 | tf_op jit(solution)/shard_map/ppermute | solution.py:16
  114.6 8.3 %collective-permute-start.23 = (bf16[128,512]{1,0:T(8,128)(2,1)S(1)}, bf16[128,512]{1,0:T(8,128)(2,1)S(1)}, u32[]{:S(2)}, u32[]{:S(2)}) collective-permute-start(bf16[128,512]{1,0:T(8,128)(2,1)S(1)} %fusion.16.refs_0_), channel_id=1, source_target_pairs={{0,6},{1,7},{2,4},{3,5},{4,2},{5,3},{6,0},{7,1},{8,14},{9,15},{10,... | collective-permute-start | bytes 393224 | tf_op jit(solution)/shard_map/ppermute | solution.py:16
  117.0 11.1 %collective-permute-start.22 = (bf16[128,512]{1,0:T(8,128)(2,1)S(1)}, bf16[128,512]{1,0:T(8,128)(2,1)S(1)}, u32[]{:S(2)}, u32[]{:S(2)}) collective-permute-start(bf16[128,512]{1,0:T(8,128)(2,1)S(1)} %fusion.16.refs_0_), channel_id=1, source_target_pairs={{0,4},{1,5},{2,6},{3,7},{4,0},{5,1},{6,2},{7,3},{8,12},{9,13},{10,... | collective-permute-start | bytes 393224 | tf_op jit(solution)/shard_map/ppermute | solution.py:16
  129.0 12.2 %collective-permute-start.25 = (bf16[4,400,512]{2,1,0:T(8,128)(2,1)S(1)}, bf16[4,400,512]{2,1,0:T(8,128)(2,1)}, u32[]{:S(2)}, u32[]{:S(2)}) collective-permute-start(bf16[4,400,512]{2,1,0:T(8,128)(2,1)S(1)} %all-to-all-done.4.own_ref), channel_id=1, source_target_pairs={{0,1},{1,0},{2,3},{3,2},{4,5},{5,4},{6,7},{7,6},{8,9},{9,8},{10,11... | collective-permute-start | bytes 4915208 | tf_op jit(solution)/shard_map/ppermute | solution.py:16
  129.1 5.9 %collective-permute-start.24 = (bf16[128,512]{1,0:T(8,128)(2,1)S(1)}, bf16[128,512]{1,0:T(8,128)(2,1)S(1)}, u32[]{:S(2)}, u32[]{:S(2)}) collective-permute-start(bf16[128,512]{1,0:T(8,128)(2,1)S(1)} %fusion.16.refs_0_), channel_id=1, source_target_pairs={{0,2},{1,3},{2,0},{3,1},{4,6},{5,7},{6,4},{7,5},{8,10},{9,11},{10,... | collective-permute-start | bytes 393224 | tf_op jit(solution)/shard_map/ppermute | solution.py:16
  136.8 25.2 %all-to-all-start.3 = ((bf16[4,208,512]{2,1,0:T(8,128)(2,1)}), bf16[4,208,512]{2,1,0:T(8,128)(2,1)}, u32[]{:S(2)}, u32[]{:S(2)}) async-start(bf16[4,208,512]{2,1,0:T(8,128)(2,1)} %dispatch.5), calls=%async_computation.3 | async-start | bytes 1703936 | tf_op jit(solution)/shard_map/all_to_all | solution.py:577
  141.2 3.4 %copy-start.2 = (bf16[1,4096,1024]{2,1,0:T(8,128)(2,1)S(1)}, bf16[1,4096,1024]{2,1,0:T(8,128)(2,1)}, u32[]{:S(2)}) copy-start(bf16[1,4096,1024]{2,1,0:T(8,128)(2,1)} %param.15) | copy-start | bytes 25165828
  156.9 1.7 copy-start.3
  158.6 1.7 copy-start.4
  160.3 1.6 copy-start.5
  161.9 16.6 %collective-permute-start.26 = (bf16[4,208,512]{2,1,0:T(8,128)(2,1)}, bf16[4,208,512]{2,1,0:T(8,128)(2,1)S(1)}, u32[]{:S(2)}, u32[]{:S(2)}) collective-permute-start(bf16[4,208,512]{2,1,0:T(8,128)(2,1)} %all-to-all-done.3.own_ref), channel_id=1, source_target_pairs={{0,1},{1,0},{2,3},{3,2},{4,5},{5,4},{6,7},{7,6},{8,9},{9,8},{10,11... | collective-permute-start | bytes 2555912 | tf_op jit(solution)/shard_map/ppermute | solution.py:16
  178.6 24.2 %collective-permute-start.27 = (bf16[4,208,512]{2,1,0:T(8,128)(2,1)S(1)}, bf16[4,208,512]{2,1,0:T(8,128)(2,1)S(1)}, u32[]{:S(2)}, u32[]{:S(2)}) collective-permute-start(bf16[4,208,512]{2,1,0:T(8,128)(2,1)S(1)} %all_to_all.25.own_ref), channel_id=1, source_target_pairs={{0,1},{1,0},{2,3},{3,2},{4,5},{5,4},{6,7},{7,6},{8,9},{9,8},{10,11... | collective-permute-start | bytes 2555912 | tf_op jit(solution)/shard_map/ppermute | solution.py:16
  178.6 1.4 copy-start.6

commit v3 on v1

--- a/solution.py
+++ b/solution.py
@@ -447,7 +447,7 @@
         compiler_params=params(),
         name="spread",
     )(shares, ids)
-    got = branch_exchange(0, pack(after(position, shares), branch, 0, experts))
+    got = branch_exchange(0, after(pack(position, branch, 0, experts), shares))
     branch_add(0, 0, after(got, to_blocks))
     from_blocks = lax.all_to_all(to_blocks, "fsdp", split_axis=0, concat_axis=0, tiled=True)
     for phase in range(1, bits):
@@ -568,6 +568,7 @@
     sums = jax.ShapeDtypeStruct((2 * count, units), jnp.float32)
     sum_spec = pl.BlockSpec((2 * count, tile), lambda n: (0, n))
     any_spec = pl.BlockSpec(memory_space=pl.ANY)
+    row_spec = pl.BlockSpec(memory_space=pltpu.HBM)
     row_scratch = [
         pltpu.VMEM((2 * count, experts * part), jnp.bfloat16),
         pltpu.VMEM((experts, lanes, part), jnp.bfloat16),
@@ -618,7 +619,7 @@
             grad_shape,
             grad_shape,
         ),
-        in_specs=[smem(), any_spec, any_spec, any_spec]
+        in_specs=[smem(), row_spec, row_spec, any_spec]
         + [weight_spec, weight_spec, sum_spec, sum_spec]
         + [whole(stats.shape), whole(signs.shape), unit_spec],
         out_specs=(unit_spec, grad_spec, grad_spec),

time: 194 us -> 190 us (0.979)
  waiting for transfers between devices: 59.3 us -> 56.1 us
    all_to_all x1, waiting for transfers between devices: 5.3 us -> 2.27 us  [per_device(): lax.all_to_all(context.reshape(experts, quarter, columns), 'expert', spli...]
  transfers between devices with their start and end apart: 31 -> 31, of which waited for: 19 -> 19; matrix products, arithmetic and copies ran while one was open for 6% -> 6% of each run, Pallas kernels for 9% -> 10%
where the time goes in v3:
time: 190 us; the launch traced here: 189 us
  waiting for transfers between devices  56.1 us (30%)
  Pallas kernels  51.5 us (27%)
  starting transfers between devices  47.8 us (25%)
  local copies, waits for them, and re-layouts  20.4 us (11%)
  other arithmetic  9.05 us (5%)
  matrix products  3.51 us (2%)
    ppermute x27, waiting for transfers between devices, exchange(): return lax.ppermute(value, axis, [(i, i ^ offset) for i in range(size)])  53.7 us
    ppermute x27, starting transfers between devices, exchange(): return lax.ppermute(value, axis, [(i, i ^ offset) for i in range(size)])  30.3 us
    pallas_call x1, Pallas kernels, per_device(): pl.pallas_call(functools.partial(late_kernel, float(width), tiles), out_s...  29.7 us
    unnamed x47, local copies, waits for them, and re-layouts  17.7 us
    pallas_call x1, Pallas kernels, per_device(): pl.pallas_call(functools.partial(early_kernel, tiles), out_shape=(sums, s...  12.3 us
    all_to_all x2, starting transfers between devices, to_experts(): lax.all_to_all(slots[c], 'expert', split_axis=0, concat_axis=0, tiled=True)  7.39 us
    all_to_all x1, starting transfers between devices, per_device(): lax.all_to_all(context.reshape(experts, quarter, columns), 'expert', spli...  5.18 us
    all_to_all x1, starting transfers between devices, per_device(): lax.all_to_all(to_blocks, 'fsdp', split_axis=0, concat_axis=0, tiled=True)  4.88 us
  transfers between devices with their start and end apart: 31, of which 19 were waited for; matrix products, arithmetic and copies ran while one was open for 6% of the time, Pallas kernels for 10%

profile of v3, /device:TPU:0, one launch (start us, length us, event | category | flops | bytes accessed | tf_op | source)
XLA Modules:
  0.0 189.4 jit_solution(6230530500064592871)
XLA Ops:
  0.6 5.2 %all-to-all-start = ((bf16[4,32,1024]{2,1,0:T(8,128)(2,1)}), bf16[4,32,1024]{2,1,0:T(8,128)(2,1)S(1)}, u32[]{:S(2)}, u32[]{:S(2)}) async-start(bf16[4,32,1024]{2,1,0:T(8,128)(2,1)} %bitcast.110), calls=%async_computation | async-start | bytes 524288 | tf_op jit(solution)/shard_map/all_to_all | solution.py:436
  5.9 2.2 %copy-done = bf16[1,512,4096]{2,1,0:T(8,128)(2,1)S(1)} copy-done((bf16[1,512,4096]{2,1,0:T(8,128)(2,1)S(1)}, bf16[1,512,4096]{2,1,0:T(8,128)(2,1)}, u32[]{:S(2)}) %copy-start) | copy-done | bytes 4194328
  8.1 0.8 pack.2
  8.9 2.3 %all-to-all-done.shares_ref = bf16[4,32,1024]{2,1,0:T(8,128)(2,1)S(1)} async-done(((bf16[4,32,1024]{2,1,0:T(8,128)(2,1)}), bf16[4,32,1024]{2,1,0:T(8,128)(2,1)S(1)}, u32[]{:S(2)}, u32[]{:S(2)}) %all-to-all-start) | async-done | bytes 262176 | tf_op jit(solution)/shard_map/all_to_all | solution.py:436
  11.2 1.3 collective-permute-start
  13.8 4.9 %all-to-all-start.1 = ((bf16[8,48,512]{2,1,0:T(8,128)(2,1)}), bf16[8,48,512]{2,1,0:T(8,128)(2,1)S(1)}, u32[]{:S(2)}, u32[]{:S(2)}) async-start(bf16[8,48,512]{2,1,0:T(8,128)(2,1)} %spread.1), calls=%async_computation.1 | async-start | bytes 786432 | tf_op jit(solution)/shard_map/all_to_all | solution.py:452
  18.7 4.7 %collective-permute-done = bf16[2,256,512]{2,1,0:T(8,128)(2,1)S(1)} collective-permute-done((bf16[2,256,512]{2,1,0:T(8,128)(2,1)S(1)}, bf16[2,256,512]{2,1,0:T(8,128)(2,1)S(1)}, u32[]{:S(2)}, u32[]{:S(2)}) %collective-permute-start) | collective-permute-done | bytes 524320 | tf_op jit(solution)/shard_map/ppermute | solution.py:16
  23.4 1.0 collective-permute-done.1
  24.4 1.4 add_convert_fusion.2
  25.8 0.8 collective-permute-start.3
  26.6 1.5 collective-permute-start.2
  28.1 2.2 %copy-done.1 = bf16[1,512,4096]{2,1,0:T(8,128)(2,1)S(1)} copy-done((bf16[1,512,4096]{2,1,0:T(8,128)(2,1)S(1)}, bf16[1,512,4096]{2,1,0:T(8,128)(2,1)}, u32[]{:S(2)}) %copy-start.1) | copy-done | bytes 4194328
  30.3 0.8 pack.3
  31.3 0.9 collective-permute-done.3
  32.2 0.8 collective-permute-done.2
  33.0 1.6 collective-permute-start.6
  34.6 1.1 collective-permute-start.5
  35.8 0.8 collective-permute-start.4
  36.6 1.4 add_bitcast_fusion.3
  38.1 4.9 %collective-permute-done.6 = bf16[8,32,512]{2,1,0:T(8,128)(2,1)S(1)} collective-permute-done((bf16[8,32,512]{2,1,0:T(8,128)(2,1)S(1)}, bf16[8,32,512]{2,1,0:T(8,128)(2,1)S(1)}, u32[]{:S(2)}, u32[]{:S(2)}) %collective-permute-start.6) | collective-permute-done | bytes 262176 | tf_op jit(solution)/shard_map/ppermute | solution.py:16
  43.0 2.7 %collective-permute-done.5 = bf16[8,32,512]{2,1,0:T(8,128)(2,1)S(1)} collective-permute-done((bf16[8,32,512]{2,1,0:T(8,128)(2,1)S(1)}, bf16[8,32,512]{2,1,0:T(8,128)(2,1)S(1)}, u32[]{:S(2)}, u32[]{:S(2)}) %collective-permute-start.5) | collective-permute-done | bytes 262176 | tf_op jit(solution)/shard_map/ppermute | solution.py:16
  46.5 1.2 convolution_convert_fusion.1
  47.7 1.4 collective-permute-start.7
  49.9 1.4 convert_add_fusion.1
  51.3 1.9 fusion.24
  53.1 3.9 %collective-permute-start.14 = (bf16[128,512]{1,0:T(8,128)(2,1)}, bf16[128,512]{1,0:T(8,128)(2,1)S(1)}, u32[]{:S(2)}, u32[]{:S(2)}) collective-permute-start(bf16[128,512]{1,0:T(8,128)(2,1)} %get-tuple-element.93), channel_id=1, source_target_pairs={{0,6},{1,7},{2,4},{3,5},{4,2},{5,3},{6,0},{7,1},{8,14},{9,15},{10,... | collective-permute-start | bytes 393224 | tf_op jit(solution)/shard_map/ppermute | solution.py:16
  57.6 4.6 %collective-permute-done.7 = bf16[2,256,512]{2,1,0:T(8,128)(2,1)} collective-permute-done((bf16[2,256,512]{2,1,0:T(8,128)(2,1)S(1)}, bf16[2,256,512]{2,1,0:T(8,128)(2,1)}, u32[]{:S(2)}, u32[]{:S(2)}) %collective-permute-start.7) | collective-permute-done | bytes 524320 | tf_op jit(solution)/shard_map/ppermute | solution.py:16
  62.1 1.1 collective-permute-done.8
  63.3 1.3 add_convert_fusion
  65.3 1.4 collective-permute-start.10
  66.7 2.1 %collective-permute-done.13 = bf16[128,512]{1,0:T(8,128)(2,1)} collective-permute-done((bf16[128,512]{1,0:T(8,128)(2,1)}, bf16[128,512]{1,0:T(8,128)(2,1)}, u32[]{:S(2)}, u32[]{:S(2)}) %collective-permute-start.13) | collective-permute-done | bytes 131104 | tf_op jit(solution)/shard_map/ppermute | solution.py:16
  68.8 1.2 fusion.21.refs_0_
  70.0 2.2 %collective-permute-done.11 = bf16[1,256,512]{2,1,0:T(8,128)(2,1)S(1)} collective-permute-done((bf16[1,256,512]{2,1,0:T(8,128)(2,1)S(1)}, bf16[1,256,512]{2,1,0:T(8,128)(2,1)S(1)}, u32[]{:S(2)}, u32[]{:S(2)}) %collective-permute-start.11) | collective-permute-done | bytes 262176 | tf_op jit(solution)/shard_map/ppermute | solution.py:16
  73.0 1.5 add_bitcast_fusion.1
  75.2 0.9 slice_convert_fusion
  76.1 3.7 %collective-permute-start.21 = (bf16[128,512]{1,0:T(8,128)(2,1)S(1)}, bf16[128,512]{1,0:T(8,128)(2,1)S(1)}, u32[]{:S(2)}, u32[]{:S(2)}) collective-permute-start(bf16[128,512]{1,0:T(8,128)(2,1)S(1)} %fusion.21.refs_0_), channel_id=1, source_target_pairs={{0,6},{1,7},{2,4},{3,5},{4,2},{5,3},{6,0},{7,1},{8,14},{9,15},{10,... | collective-permute-start | bytes 393224 | tf_op jit(solution)/shard_map/ppermute | solution.py:16
  81.0 0.9 fusion.27
  81.9 2.4 %collective-permute-done.21.refs_3_ = bf16[128,512]{1,0:T(8,128)(2,1)S(1)} collective-permute-done((bf16[128,512]{1,0:T(8,128)(2,1)S(1)}, bf16[128,512]{1,0:T(8,128)(2,1)S(1)}, u32[]{:S(2)}, u32[]{:S(2)}) %collective-permute-start.21) | collective-permute-done | bytes 131104 | tf_op jit(solution)/shard_map/ppermute | solution.py:16
  84.3 7.3 %collective-permute-done.20.refs_2_ = bf16[128,512]{1,0:T(8,128)(2,1)S(1)} collective-permute-done((bf16[128,512]{1,0:T(8,128)(2,1)S(1)}, bf16[128,512]{1,0:T(8,128)(2,1)S(1)}, u32[]{:S(2)}, u32[]{:S(2)}) %collective-permute-start.20) | collective-permute-done | bytes 131104 | tf_op jit(solution)/shard_map/ppermute | solution.py:16
  91.7 2.3 %dispatch.2 = bf16[4,400,512]{2,1,0:T(8,128)(2,1)} custom-call(s32[3]{0:T(128)S(1)} %pad_add_fusion.position_ref, s32[8,4,128]{2,1,0:T(4,128)S(1)} %bitcast.102, bf16[16,1024]{1,0:T(8,128)(2,1)S(1)} %fusion.30.extra_ref, bf16[128,512]{1,0:T(8,128)(2,1)S(1)} %fusion.21.refs_0_, bf16[128,512]{1,0:T(8,128)(2,1)S(1)} %collective-permute-done.19.refs_1_, ...), custom_call_target="tpu_custom_call" | custom-call | tf_op jit(solution)/shard_map/dispatch/pallas_call | solution.py:515
  94.0 3.6 %all-to-all-start.3 = ((bf16[4,400,512]{2,1,0:T(8,128)(2,1)}), bf16[4,400,512]{2,1,0:T(8,128)(2,1)S(1)}, u32[]{:S(2)}, u32[]{:S(2)}) async-start(bf16[4,400,512]{2,1,0:T(8,128)(2,1)} %dispatch.2), calls=%async_computation.3 | async-start | bytes 3276800 | tf_op jit(solution)/shard_map/all_to_all | solution.py:563
  97.5 2.5 %collective-permute-start.18 = (bf16[128,512]{1,0:T(8,128)(2,1)}, bf16[128,512]{1,0:T(8,128)(2,1)S(1)}, u32[]{:S(2)}, u32[]{:S(2)}) collective-permute-start(bf16[128,512]{1,0:T(8,128)(2,1)} %get-tuple-element.90), channel_id=1, source_target_pairs={{0,6},{1,7},{2,4},{3,5},{4,2},{5,3},{6,0},{7,1},{8,14},{9,15},{10,... | collective-permute-start | bytes 393224 | tf_op jit(solution)/shard_map/ppermute | solution.py:16
  100.1 1.9 %collective-permute-start.16 = (bf16[128,512]{1,0:T(8,128)(2,1)S(1)}, bf16[128,512]{1,0:T(8,128)(2,1)S(1)}, u32[]{:S(2)}, u32[]{:S(2)}) collective-permute-start(bf16[128,512]{1,0:T(8,128)(2,1)S(1)} %get-tuple-element.92), channel_id=1, source_target_pairs={{0,2},{1,3},{2,0},{3,1},{4,6},{5,7},{6,4},{7,5},{8,10},{9,11},{10,... | collective-permute-start | bytes 393224 | tf_op jit(solution)/shard_map/ppermute | solution.py:16
  102.0 4.1 %collective-permute-done.18 = bf16[128,512]{1,0:T(8,128)(2,1)S(1)} collective-permute-done((bf16[128,512]{1,0:T(8,128)(2,1)}, bf16[128,512]{1,0:T(8,128)(2,1)S(1)}, u32[]{:S(2)}, u32[]{:S(2)}) %collective-permute-start.18) | collective-permute-done | bytes 131104 | tf_op jit(solution)/shard_map/ppermute | solution.py:16
  106.1 4.4 %collective-permute-done.17 = bf16[128,512]{1,0:T(8,128)(2,1)S(1)} collective-permute-done((bf16[128,512]{1,0:T(8,128)(2,1)}, bf16[128,512]{1,0:T(8,128)(2,1)S(1)}, u32[]{:S(2)}, u32[]{:S(2)}) %collective-permute-start.17) | collective-permute-done | bytes 131104 | tf_op jit(solution)/shard_map/ppermute | solution.py:16
  110.5 1.0 fusion.16.refs_0_
  111.5 2.4 %collective-permute-start.24 = (bf16[128,512]{1,0:T(8,128)(2,1)S(1)}, bf16[128,512]{1,0:T(8,128)(2,1)S(1)}, u32[]{:S(2)}, u32[]{:S(2)}) collective-permute-start(bf16[128,512]{1,0:T(8,128)(2,1)S(1)} %fusion.16.refs_0_), channel_id=1, source_target_pairs={{0,6},{1,7},{2,4},{3,5},{4,2},{5,3},{6,0},{7,1},{8,14},{9,15},{10,... | collective-permute-start | bytes 393224 | tf_op jit(solution)/shard_map/ppermute | solution.py:16
  113.9 2.1 %collective-permute-start.22 = (bf16[128,512]{1,0:T(8,128)(2,1)S(1)}, bf16[128,512]{1,0:T(8,128)(2,1)S(1)}, u32[]{:S(2)}, u32[]{:S(2)}) collective-permute-start(bf16[128,512]{1,0:T(8,128)(2,1)S(1)} %fusion.16.refs_0_), channel_id=1, source_target_pairs={{0,2},{1,3},{2,0},{3,1},{4,6},{5,7},{6,4},{7,5},{8,10},{9,11},{10,... | collective-permute-start | bytes 393224 | tf_op jit(solution)/shard_map/ppermute | solution.py:16
  116.0 0.8 signs.1
  116.8 1.1 join.1
  117.9 2.0 %collective-permute-done.24.refs_3_ = bf16[128,512]{1,0:T(8,128)(2,1)S(1)} collective-permute-done((bf16[128,512]{1,0:T(8,128)(2,1)S(1)}, bf16[128,512]{1,0:T(8,128)(2,1)S(1)}, u32[]{:S(2)}, u32[]{:S(2)}) %collective-permute-start.24) | collective-permute-done | bytes 131104 | tf_op jit(solution)/shard_map/ppermute | solution.py:16
  119.9 5.1 %collective-permute-done.23.refs_2_ = bf16[128,512]{1,0:T(8,128)(2,1)S(1)} collective-permute-done((bf16[128,512]{1,0:T(8,128)(2,1)S(1)}, bf16[128,512]{1,0:T(8,128)(2,1)S(1)}, u32[]{:S(2)}, u32[]{:S(2)}) %collective-permute-start.23) | collective-permute-done | bytes 131104 | tf_op jit(solution)/shard_map/ppermute | solution.py:16
  125.0 2.3 %dispatch.3 = bf16[4,400,512]{2,1,0:T(8,128)(2,1)} custom-call(s32[3]{0:T(128)S(1)} %pad_add_fusion.position_ref, s32[8,4,128]{2,1,0:T(4,128)S(1)} %bitcast.104, bf16[16,1024]{1,0:T(8,128)(2,1)S(1)} %fusion.30.extra_ref, bf16[128,512]{1,0:T(8,128)(2,1)S(1)} %fusion.16.refs_0_, bf16[128,512]{1,0:T(8,128)(2,1)S(1)} %collective-permute-done.22.refs_1_, ...), custom_call_target="tpu_custom_call" | custom-call | tf_op jit(solution)/shard_map/dispatch/pallas_call | solution.py:515
  127.3 3.8 %all-to-all-start.2 = ((bf16[4,400,512]{2,1,0:T(8,128)(2,1)}), bf16[4,400,512]{2,1,0:T(8,128)(2,1)S(1)}, u32[]{:S(2)}, u32[]{:S(2)}) async-start(bf16[4,400,512]{2,1,0:T(8,128)(2,1)} %dispatch.3), calls=%async_computation.2 | async-start | bytes 3276800 | tf_op jit(solution)/shard_map/all_to_all | solution.py:563
  131.1 3.4 %copy-done.2 = bf16[1,4096,1024]{2,1,0:T(8,128)(2,1)S(1)} copy-done((bf16[1,4096,1024]{2,1,0:T(8,128)(2,1)S(1)}, bf16[1,4096,1024]{2,1,0:T(8,128)(2,1)}, u32[]{:S(2)}) %copy-start.2) | copy-done | bytes 8388632
  134.5 12.3 %early.1 = (f32[768,1024]{1,0:T(8,128)S(1)}, f32[768,1024]{1,0:T(8,128)S(1)}, f32[768,16]{1,0:T(8,128)S(1)}, bf16[4,512,768]{2,1,0:T(8,128)(2,1)S(1)}) custom-call(bf16[4,400,512]{2,1,0:T(8,128)(2,1)S(1)} %all-to-all-done.3.own_ref, bf16[4,400,512]{2,1,0:T(8,128)(2,1)} %collective-permute-done.25.other_ref, bf16[4,2,512,1024]{3,2,1,0:T(8,128)(2,1)S(1)} %bitcast.94, ...), custom_call_target="tpu_custom_call" | custom-call | flops 6442450944 | bytes 8388608 | tf_op jit(solution)/shard_map/early/pallas_call | solution.py:576
  146.8 1.7 copy-done.3
  148.5 1.7 copy-done.4
  150.2 1.6 copy-done.5
  153.0 3.1 %collective-permute-done.26.other_ref = bf16[4,400,512]{2,1,0:T(8,128)(2,1)S(1)} collective-permute-done((bf16[4,400,512]{2,1,0:T(8,128)(2,1)S(1)}, bf16[4,400,512]{2,1,0:T(8,128)(2,1)S(1)}, u32[]{:S(2)}, u32[]{:S(2)}) %collective-permute-start.26) | collective-permute-done | bytes 1638432 | tf_op jit(solution)/shard_map/ppermute | solution.py:16
  156.1 1.0 copy-done.7
  157.1 1.4 copy-done.8
  158.5 1.0 copy-done.10
  159.5 29.7 %late.1 = (bf16[4,2,96,1024]{3,2,1,0:T(8,128)(2,1)}, bf16[4,1024,1024]{2,1,0:T(8,128)(2,1)}, bf16[4,1024,1024]{2,1,0:T(8,128)(2,1)}) custom-call(s32[3]{0:T(128)S(1)} %pad_add_fusion.position_ref, bf16[4,400,512]{2,1,0:T(8,128)(2,1)S(1)} %all-to-all-done.2.own_ref, bf16[4,400,512]{2,1,0:T(8,128)(2,1)S(1)} %collective-permute-done.26.other_ref, ...), custom_call_target="tpu_custom_call" | custom-call | tf_op jit(solution)/shard_map/late/pallas_call | solution.py:615
  (79 shorter events, 8.2 us)
Async XLA Ops:
  0.6 10.5 %all-to-all-start = ((bf16[4,32,1024]{2,1,0:T(8,128)(2,1)}), bf16[4,32,1024]{2,1,0:T(8,128)(2,1)S(1)}, u32[]{:S(2)}, u32[]{:S(2)}) async-start(bf16[4,32,1024]{2,1,0:T(8,128)(2,1)} %bitcast.110), calls=%async_computation | async-start | bytes 524288 | tf_op jit(solution)/shard_map/all_to_all | solution.py:436
  5.9 2.2 %copy-start = (bf16[1,512,4096]{2,1,0:T(8,128)(2,1)S(1)}, bf16[1,512,4096]{2,1,0:T(8,128)(2,1)}, u32[]{:S(2)}) copy-start(bf16[1,512,4096]{2,1,0:T(8,128)(2,1)} %param.10) | copy-start | bytes 12582916
  8.1 4.9 %copy-start.21 = (s32[128,2]{0,1:T(2,128)S(1)}, s32[128,2]{0,1:T(2,128)}, u32[]{:S(2)}) copy-start(s32[128,2]{0,1:T(2,128)} %param.17) | copy-start | bytes 3076
  8.1 4.9 %copy-start.22 = (s32[128,2]{0,1:T(2,128)S(1)}, s32[128,2]{0,1:T(2,128)}, u32[]{:S(2)}) copy-start(s32[128,2]{0,1:T(2,128)} %param.18) | copy-start | bytes 3076
  11.2 12.3 %collective-permute-start = (bf16[2,256,512]{2,1,0:T(8,128)(2,1)S(1)}, bf16[2,256,512]{2,1,0:T(8,128)(2,1)S(1)}, u32[]{:S(2)}, u32[]{:S(2)}) collective-permute-start(bf16[2,256,512]{2,1,0:T(8,128)(2,1)S(1)} %get-tuple-element.45), channel_id=1, source_target_pairs={{0,8},{8,0},{16,24},{24,16},{1,9},{9,1},{17,25},{25,17},{2,10},{10... | collective-permute-start | bytes 1572872 | tf_op jit(solution)/shard_map/ppermute | solution.py:16
  12.4 12.0 %collective-permute-start.1 = (bf16[2,256,512]{2,1,0:T(8,128)(2,1)S(1)}, bf16[2,256,512]{2,1,0:T(8,128)(2,1)S(1)}, u32[]{:S(2)}, u32[]{:S(2)}) collective-permute-start(bf16[2,256,512]{2,1,0:T(8,128)(2,1)S(1)} %get-tuple-element.46), channel_id=1, source_target_pairs={{0,16},{8,24},{16,0},{24,8},{1,17},{9,25},{17,1},{25,9},{2,18},{10... | collective-permute-start | bytes 1572872 | tf_op jit(solution)/shard_map/ppermute | solution.py:16
  13.8 17.4 %all-to-all-start.1 = ((bf16[8,48,512]{2,1,0:T(8,128)(2,1)}), bf16[8,48,512]{2,1,0:T(8,128)(2,1)S(1)}, u32[]{:S(2)}, u32[]{:S(2)}) async-start(bf16[8,48,512]{2,1,0:T(8,128)(2,1)} %spread.1), calls=%async_computation.1 | async-start | bytes 786432 | tf_op jit(solution)/shard_map/all_to_all | solution.py:452
  23.4 4.7 %copy-start.13 = (bf16[2,256,512]{2,1,0:T(8,128)(2,1)}, bf16[2,256,512]{2,1,0:T(8,128)(2,1)S(1)}, u32[]{:S(2)}) copy-start(bf16[2,256,512]{2,1,0:T(8,128)(2,1)S(1)} %collective-permute-done) | copy-start | bytes 1572868
  24.4 3.7 %copy-start.15 = (bf16[2,256,512]{2,1,0:T(8,128)(2,1)}, bf16[2,256,512]{2,1,0:T(8,128)(2,1)S(1)}, u32[]{:S(2)}) copy-start(bf16[2,256,512]{2,1,0:T(8,128)(2,1)S(1)} %collective-permute-done.1) | copy-start | bytes 1572868
  25.8 6.4 %collective-permute-start.3 = (bf16[1,256,512]{2,1,0:T(8,128)(2,1)S(1)}, bf16[1,256,512]{2,1,0:T(8,128)(2,1)S(1)}, u32[]{:S(2)}, u32[]{:S(2)}) collective-permute-start(bf16[1,256,512]{2,1,0:T(8,128)(2,1)S(1)} %get-tuple-element.88), channel_id=1, source_target_pairs={{0,8},{8,0},{16,24},{24,16},{1,9},{9,1},{17,25},{25,17},{2,10},{10... | collective-permute-start | bytes 786440 | tf_op jit(solution)/shard_map/ppermute | solution.py:16
  26.6 6.4 %collective-permute-start.2 = (bf16[1,256,512]{2,1,0:T(8,128)(2,1)S(1)}, bf16[1,256,512]{2,1,0:T(8,128)(2,1)S(1)}, u32[]{:S(2)}, u32[]{:S(2)}) collective-permute-start(bf16[1,256,512]{2,1,0:T(8,128)(2,1)S(1)} %get-tuple-element.89), channel_id=1, source_target_pairs={{0,16},{8,24},{16,0},{24,8},{1,17},{9,25},{17,1},{25,9},{2,18},{10... | collective-permute-start | bytes 786440 | tf_op jit(solution)/shard_map/ppermute | solution.py:16
  28.1 2.2 %copy-start.1 = (bf16[1,512,4096]{2,1,0:T(8,128)(2,1)S(1)}, bf16[1,512,4096]{2,1,0:T(8,128)(2,1)}, u32[]{:S(2)}) copy-start(bf16[1,512,4096]{2,1,0:T(8,128)(2,1)} %param.10) | copy-start | bytes 12582916
  30.3 6.3 %copy-start.14 = (bf16[2,256,512]{2,1,0:T(8,128)(2,1)S(1)}, bf16[2,256,512]{2,1,0:T(8,128)(2,1)}, u32[]{:S(2)}) copy-start(bf16[2,256,512]{2,1,0:T(8,128)(2,1)} %copy-done.13) | copy-start | bytes 1572868
  31.3 4.5 %copy-start.12 = (bf16[8,48,512]{2,1,0:T(8,128)(2,1)}, bf16[8,48,512]{2,1,0:T(8,128)(2,1)S(1)}, u32[]{:S(2)}) copy-start(bf16[8,48,512]{2,1,0:T(8,128)(2,1)S(1)} %all-to-all-done.1) | copy-start | bytes 1179652
  33.0 2.8 %copy-start.18 = (bf16[1,256,512]{2,1,0:T(8,128)(2,1)}, bf16[1,256,512]{2,1,0:T(8,128)(2,1)S(1)}, u32[]{:S(2)}) copy-start(bf16[1,256,512]{2,1,0:T(8,128)(2,1)S(1)} %collective-permute-done.2) | copy-start | bytes 786436
  33.0 10.0 %collective-permute-start.6 = (bf16[8,32,512]{2,1,0:T(8,128)(2,1)S(1)}, bf16[8,32,512]{2,1,0:T(8,128)(2,1)S(1)}, u32[]{:S(2)}, u32[]{:S(2)}) collective-permute-start(bf16[8,32,512]{2,1,0:T(8,128)(2,1)S(1)} %slice.18), channel_id=1, source_target_pairs={{0,24},{8,16},{16,8},{24,0},{1,25},{9,17},{17,9},{25,1},{2,26},{10... | collective-permute-start | bytes 786440 | tf_op jit(solution)/shard_map/ppermute | solution.py:16
  34.6 11.1 %collective-permute-start.5 = (bf16[8,32,512]{2,1,0:T(8,128)(2,1)S(1)}, bf16[8,32,512]{2,1,0:T(8,128)(2,1)S(1)}, u32[]{:S(2)}, u32[]{:S(2)}) collective-permute-start(bf16[8,32,512]{2,1,0:T(8,128)(2,1)S(1)} %slice.18), channel_id=1, source_target_pairs={{0,16},{8,24},{16,0},{24,8},{1,17},{9,25},{17,1},{25,9},{2,18},{10... | collective-permute-start | bytes 786440 | tf_op jit(solution)/shard_map/ppermute | solution.py:16
  35.8 10.0 %collective-permute-start.4 = (bf16[8,32,512]{2,1,0:T(8,128)(2,1)S(1)}, bf16[8,32,512]{2,1,0:T(8,128)(2,1)S(1)}, u32[]{:S(2)}, u32[]{:S(2)}) collective-permute-start(bf16[8,32,512]{2,1,0:T(8,128)(2,1)S(1)} %slice.18), channel_id=1, source_target_pairs={{0,8},{8,0},{16,24},{24,16},{1,9},{9,1},{17,25},{25,17},{2,10},{10... | collective-permute-start | bytes 786440 | tf_op jit(solution)/shard_map/ppermute | solution.py:16
  46.4 20.3 %copy-start.19 = (bf16[1024]{0:T(1024)(128)(2,1)S(1)}, bf16[1024]{0:T(1024)(128)(2,1)}, u32[]{:S(2)}) copy-start(bf16[1024]{0:T(1024)(128)(2,1)} %param.13) | copy-start | bytes 6148
  46.4 22.4 %copy-start.16 = (bf16[128,1024]{1,0:T(8,128)(2,1)S(1)}, bf16[128,1024]{1,0:T(8,128)(2,1)}, u32[]{:S(2)}) copy-start(bf16[128,1024]{1,0:T(8,128)(2,1)} %param.12) | copy-start | bytes 786436
  47.7 2.2 %collective-permute-start.9 = (bf16[4,128,512]{2,1,0:T(8,128)(2,1)}, bf16[4,128,512]{2,1,0:T(8,128)(2,1)S(1)}, u32[]{:S(2)}, u32[]{:S(2)}) collective-permute-start(bf16[4,128,512]{2,1,0:T(8,128)(2,1)} %convolution_convert_fusion.1), channel_id=1, source_target_pairs={{0,1},{1,0},{2,3},{3,2},{4,5},{5,4},{6,7},{7,6},{8,9},{9,8},{10,11... | collective-permute-start | bytes 1572872 | tf_op jit(solution)/shard_map/ppermute | solution.py:16
  47.7 14.4 %collective-permute-start.7 = (bf16[2,256,512]{2,1,0:T(8,128)(2,1)S(1)}, bf16[2,256,512]{2,1,0:T(8,128)(2,1)}, u32[]{:S(2)}, u32[]{:S(2)}) collective-permute-start(bf16[2,256,512]{2,1,0:T(8,128)(2,1)S(1)} %get-tuple-element.54), channel_id=1, source_target_pairs={{0,8},{8,0},{16,24},{24,16},{1,9},{9,1},{17,25},{25,17},{2,10},{10... | collective-permute-start | bytes 1572872 | tf_op jit(solution)/shard_map/ppermute | solution.py:16
  49.1 14.2 %collective-permute-start.8 = (bf16[2,256,512]{2,1,0:T(8,128)(2,1)S(1)}, bf16[2,256,512]{2,1,0:T(8,128)(2,1)}, u32[]{:S(2)}, u32[]{:S(2)}) collective-permute-start(bf16[2,256,512]{2,1,0:T(8,128)(2,1)S(1)} %get-tuple-element.55), channel_id=1, source_target_pairs={{0,16},{8,24},{16,0},{24,8},{1,17},{9,25},{17,1},{25,9},{2,18},{10... | collective-permute-start | bytes 1572872 | tf_op jit(solution)/shard_map/ppermute | solution.py:16
  53.1 13.6 %collective-permute-start.14 = (bf16[128,512]{1,0:T(8,128)(2,1)}, bf16[128,512]{1,0:T(8,128)(2,1)S(1)}, u32[]{:S(2)}, u32[]{:S(2)}) collective-permute-start(bf16[128,512]{1,0:T(8,128)(2,1)} %get-tuple-element.93), channel_id=1, source_target_pairs={{0,6},{1,7},{2,4},{3,5},{4,2},{5,3},{6,0},{7,1},{8,14},{9,15},{10,... | collective-permute-start | bytes 393224 | tf_op jit(solution)/shard_map/ppermute | solution.py:16
  57.0 11.8 %collective-permute-start.13 = (bf16[128,512]{1,0:T(8,128)(2,1)}, bf16[128,512]{1,0:T(8,128)(2,1)}, u32[]{:S(2)}, u32[]{:S(2)}) collective-permute-start(bf16[128,512]{1,0:T(8,128)(2,1)} %get-tuple-element.94), channel_id=1, source_target_pairs={{0,4},{1,5},{2,6},{3,7},{4,0},{5,1},{6,2},{7,3},{8,12},{9,13},{10,... | collective-permute-start | bytes 393224 | tf_op jit(solution)/shard_map/ppermute | solution.py:16
  57.0 11.8 %collective-permute-start.12 = (bf16[128,512]{1,0:T(8,128)(2,1)}, bf16[128,512]{1,0:T(8,128)(2,1)}, u32[]{:S(2)}, u32[]{:S(2)}) collective-permute-start(bf16[128,512]{1,0:T(8,128)(2,1)} %get-tuple-element.95), channel_id=1, source_target_pairs={{0,2},{1,3},{2,0},{3,1},{4,6},{5,7},{6,4},{7,5},{8,10},{9,11},{10,... | collective-permute-start | bytes 393224 | tf_op jit(solution)/shard_map/ppermute | solution.py:16
  64.6 7.7 %collective-permute-start.11 = (bf16[1,256,512]{2,1,0:T(8,128)(2,1)S(1)}, bf16[1,256,512]{2,1,0:T(8,128)(2,1)S(1)}, u32[]{:S(2)}, u32[]{:S(2)}) collective-permute-start(bf16[1,256,512]{2,1,0:T(8,128)(2,1)S(1)} %get-tuple-element.84), channel_id=1, source_target_pairs={{0,8},{8,0},{16,24},{24,16},{1,9},{9,1},{17,25},{25,17},{2,10},{10... | collective-permute-start | bytes 786440 | tf_op jit(solution)/shard_map/ppermute | solution.py:16
  65.3 7.7 %collective-permute-start.10 = (bf16[1,256,512]{2,1,0:T(8,128)(2,1)S(1)}, bf16[1,256,512]{2,1,0:T(8,128)(2,1)}, u32[]{:S(2)}, u32[]{:S(2)}) collective-permute-start(bf16[1,256,512]{2,1,0:T(8,128)(2,1)S(1)} %get-tuple-element.85), channel_id=1, source_target_pairs={{0,16},{8,24},{16,0},{24,8},{1,17},{9,25},{17,1},{25,9},{2,18},{10... | collective-permute-start | bytes 786440 | tf_op jit(solution)/shard_map/ppermute | solution.py:16
  68.8 6.4 %copy-start.20 = (bf16[1024,4]{0,1:T(4,128)(2,1)S(1)}, bf16[1024,4]{0,1:T(4,128)(2,1)}, u32[]{:S(2)}) copy-start(bf16[1024,4]{0,1:T(4,128)(2,1)} %param.14) | copy-start | bytes 24580
  72.3 0.7 copy-start.17
  75.1 5.5 %collective-permute-start.15 = (bf16[4,128,512]{2,1,0:T(8,128)(2,1)S(1)}, bf16[4,128,512]{2,1,0:T(8,128)(2,1)S(1)}, u32[]{:S(2)}, u32[]{:S(2)}) collective-permute-start(bf16[4,128,512]{2,1,0:T(8,128)(2,1)S(1)} %convolution_convert_fusion), channel_id=1, source_target_pairs={{0,1},{1,0},{2,3},{3,2},{4,5},{5,4},{6,7},{7,6},{8,9},{9,8},{10,11... | collective-permute-start | bytes 1572872 | tf_op jit(solution)/shard_map/ppermute | solution.py:16
  76.1 8.2 %collective-permute-start.21 = (bf16[128,512]{1,0:T(8,128)(2,1)S(1)}, bf16[128,512]{1,0:T(8,128)(2,1)S(1)}, u32[]{:S(2)}, u32[]{:S(2)}) collective-permute-start(bf16[128,512]{1,0:T(8,128)(2,1)S(1)} %fusion.21.refs_0_), channel_id=1, source_target_pairs={{0,6},{1,7},{2,4},{3,5},{4,2},{5,3},{6,0},{7,1},{8,14},{9,15},{10,... | collective-permute-start | bytes 393224 | tf_op jit(solution)/shard_map/ppermute | solution.py:16
  79.8 11.9 %collective-permute-start.20 = (bf16[128,512]{1,0:T(8,128)(2,1)S(1)}, bf16[128,512]{1,0:T(8,128)(2,1)S(1)}, u32[]{:S(2)}, u32[]{:S(2)}) collective-permute-start(bf16[128,512]{1,0:T(8,128)(2,1)S(1)} %fusion.21.refs_0_), channel_id=1, source_target_pairs={{0,4},{1,5},{2,6},{3,7},{4,0},{5,1},{6,2},{7,3},{8,12},{9,13},{10,... | collective-permute-start | bytes 393224 | tf_op jit(solution)/shard_map/ppermute | solution.py:16
  79.8 11.9 %collective-permute-start.19 = (bf16[128,512]{1,0:T(8,128)(2,1)S(1)}, bf16[128,512]{1,0:T(8,128)(2,1)S(1)}, u32[]{:S(2)}, u32[]{:S(2)}) collective-permute-start(bf16[128,512]{1,0:T(8,128)(2,1)S(1)} %fusion.21.refs_0_), channel_id=1, source_target_pairs={{0,2},{1,3},{2,0},{3,1},{4,6},{5,7},{6,4},{7,5},{8,10},{9,11},{10,... | collective-permute-start | bytes 393224 | tf_op jit(solution)/shard_map/ppermute | solution.py:16
  81.0 12.9 %copy-start.11 = (f32[4,128,512]{2,1,0:T(8,128)}, f32[4,128,512]{2,1,0:T(8,128)S(1)}, u32[]{:S(2)}) copy-start(f32[4,128,512]{2,1,0:T(8,128)S(1)} %convert_add_fusion) | copy-start | bytes 3145732
  94.0 33.3 %all-to-all-start.3 = ((bf16[4,400,512]{2,1,0:T(8,128)(2,1)}), bf16[4,400,512]{2,1,0:T(8,128)(2,1)S(1)}, u32[]{:S(2)}, u32[]{:S(2)}) async-start(bf16[4,400,512]{2,1,0:T(8,128)(2,1)} %dispatch.2), calls=%async_computation.3 | async-start | bytes 3276800 | tf_op jit(solution)/shard_map/all_to_all | solution.py:563
  97.5 8.5 %collective-permute-start.18 = (bf16[128,512]{1,0:T(8,128)(2,1)}, bf16[128,512]{1,0:T(8,128)(2,1)S(1)}, u32[]{:S(2)}, u32[]{:S(2)}) collective-permute-start(bf16[128,512]{1,0:T(8,128)(2,1)} %get-tuple-element.90), channel_id=1, source_target_pairs={{0,6},{1,7},{2,4},{3,5},{4,2},{5,3},{6,0},{7,1},{8,14},{9,15},{10,... | collective-permute-start | bytes 393224 | tf_op jit(solution)/shard_map/ppermute | solution.py:16
  100.1 10.4 %collective-permute-start.17 = (bf16[128,512]{1,0:T(8,128)(2,1)}, bf16[128,512]{1,0:T(8,128)(2,1)S(1)}, u32[]{:S(2)}, u32[]{:S(2)}) collective-permute-start(bf16[128,512]{1,0:T(8,128)(2,1)} %get-tuple-element.91), channel_id=1, source_target_pairs={{0,4},{1,5},{2,6},{3,7},{4,0},{5,1},{6,2},{7,3},{8,12},{9,13},{10,... | collective-permute-start | bytes 393224 | tf_op jit(solution)/shard_map/ppermute | solution.py:16
  100.1 10.4 %collective-permute-start.16 = (bf16[128,512]{1,0:T(8,128)(2,1)S(1)}, bf16[128,512]{1,0:T(8,128)(2,1)S(1)}, u32[]{:S(2)}, u32[]{:S(2)}) collective-permute-start(bf16[128,512]{1,0:T(8,128)(2,1)S(1)} %get-tuple-element.92), channel_id=1, source_target_pairs={{0,2},{1,3},{2,0},{3,1},{4,6},{5,7},{6,4},{7,5},{8,10},{9,11},{10,... | collective-permute-start | bytes 393224 | tf_op jit(solution)/shard_map/ppermute | solution.py:16
  111.5 8.3 %collective-permute-start.24 = (bf16[128,512]{1,0:T(8,128)(2,1)S(1)}, bf16[128,512]{1,0:T(8,128)(2,1)S(1)}, u32[]{:S(2)}, u32[]{:S(2)}) collective-permute-start(bf16[128,512]{1,0:T(8,128)(2,1)S(1)} %fusion.16.refs_0_), channel_id=1, source_target_pairs={{0,6},{1,7},{2,4},{3,5},{4,2},{5,3},{6,0},{7,1},{8,14},{9,15},{10,... | collective-permute-start | bytes 393224 | tf_op jit(solution)/shard_map/ppermute | solution.py:16
  113.9 11.1 %collective-permute-start.23 = (bf16[128,512]{1,0:T(8,128)(2,1)S(1)}, bf16[128,512]{1,0:T(8,128)(2,1)S(1)}, u32[]{:S(2)}, u32[]{:S(2)}) collective-permute-start(bf16[128,512]{1,0:T(8,128)(2,1)S(1)} %fusion.16.refs_0_), channel_id=1, source_target_pairs={{0,4},{1,5},{2,6},{3,7},{4,0},{5,1},{6,2},{7,3},{8,12},{9,13},{10,... | collective-permute-start | bytes 393224 | tf_op jit(solution)/shard_map/ppermute | solution.py:16
  113.9 11.1 %collective-permute-start.22 = (bf16[128,512]{1,0:T(8,128)(2,1)S(1)}, bf16[128,512]{1,0:T(8,128)(2,1)S(1)}, u32[]{:S(2)}, u32[]{:S(2)}) collective-permute-start(bf16[128,512]{1,0:T(8,128)(2,1)S(1)} %fusion.16.refs_0_), channel_id=1, source_target_pairs={{0,2},{1,3},{2,0},{3,1},{4,6},{5,7},{6,4},{7,5},{8,10},{9,11},{10,... | collective-permute-start | bytes 393224 | tf_op jit(solution)/shard_map/ppermute | solution.py:16
  116.8 1.1 copy-start.6
  127.3 3.8 %collective-permute-start.25 = (bf16[4,400,512]{2,1,0:T(8,128)(2,1)S(1)}, bf16[4,400,512]{2,1,0:T(8,128)(2,1)}, u32[]{:S(2)}, u32[]{:S(2)}) collective-permute-start(bf16[4,400,512]{2,1,0:T(8,128)(2,1)S(1)} %all-to-all-done.3.own_ref), channel_id=1, source_target_pairs={{0,1},{1,0},{2,3},{3,2},{4,5},{5,4},{6,7},{7,6},{8,9},{9,8},{10,11... | collective-permute-start | bytes 4915208 | tf_op jit(solution)/shard_map/ppermute | solution.py:16
  127.3 25.3 %all-to-all-start.2 = ((bf16[4,400,512]{2,1,0:T(8,128)(2,1)}), bf16[4,400,512]{2,1,0:T(8,128)(2,1)S(1)}, u32[]{:S(2)}, u32[]{:S(2)}) async-start(bf16[4,400,512]{2,1,0:T(8,128)(2,1)} %dispatch.3), calls=%async_computation.2 | async-start | bytes 3276800 | tf_op jit(solution)/shard_map/all_to_all | solution.py:563
  131.1 3.4 %copy-start.2 = (bf16[1,4096,1024]{2,1,0:T(8,128)(2,1)S(1)}, bf16[1,4096,1024]{2,1,0:T(8,128)(2,1)}, u32[]{:S(2)}) copy-start(bf16[1,4096,1024]{2,1,0:T(8,128)(2,1)} %param.15) | copy-start | bytes 25165828
  146.8 1.7 copy-start.3
  148.5 1.7 copy-start.4
  150.2 1.6 copy-start.5
  151.8 0.7 copy-start.9
  152.5 3.6 %collective-permute-start.26 = (bf16[4,400,512]{2,1,0:T(8,128)(2,1)S(1)}, bf16[4,400,512]{2,1,0:T(8,128)(2,1)S(1)}, u32[]{:S(2)}, u32[]{:S(2)}) collective-permute-start(bf16[4,400,512]{2,1,0:T(8,128)(2,1)S(1)} %all-to-all-done.2.own_ref), channel_id=1, source_target_pairs={{0,1},{1,0},{2,3},{3,2},{4,5},{5,4},{6,7},{7,6},{8,9},{9,8},{10,11... | collective-permute-start | bytes 4915208 | tf_op jit(solution)/shard_map/ppermute | solution.py:16
  156.1 1.0 copy-start.7
  157.1 1.4 copy-start.8
  158.5 1.0 copy-start.10

commit v4 on v3

--- a/solution.py
+++ b/solution.py
@@ -240,9 +240,9 @@
     up_ref,
     gate_acc,
     up_acc,
-    stats_ref,
-    signs_ref,
-    cot_ref,
+    stats_hbm,
+    signs_hbm,
+    cot_hbm,
     hidden_out,
     grad_gate_out,
     grad_up_out,
@@ -255,6 +255,9 @@
     d_gate_scratch,
     d_up_scratch,
     turned_scratch,
+    stats_ref,
+    signs_ref,
+    cot_ref,
     sems,
 ):
     step = pl.program_id(0)
@@ -267,7 +270,13 @@
         turned_ref, turned_scratch.at[:, pl.ds(0, part)], sems.at[1 + 2 * experts]
     )
 
+    stats_copy = pltpu.make_async_copy(stats_hbm, stats_ref, sems.at[2 + 2 * experts])
+    signs_copy = pltpu.make_async_copy(signs_hbm, signs_ref, sems.at[3 + 2 * experts])
+    cot_copy = pltpu.make_async_copy(cot_hbm, cot_ref, sems.at[4 + 2 * experts])
+
     def scales():
+        stats_copy.wait()
+        signs_copy.wait()
         for side in range(2):
             span = slice(side * count, (side + 1) * count)
             stats = stats_ref[span] + row_stats(flat_scratch, side, aux_scratch)
@@ -282,6 +291,9 @@
             weight_scratch[span] = jnp.where(filled > 0.0, prob, 0.0)
 
     def units_of(t):
+        columns = slice(t * tile, (t + 1) * tile)
+        if t == 0:
+            cot_copy.wait()
         for side in range(2):
             span = slice(side * count, (side + 1) * count)
             inverse = scale_scratch[span]
@@ -292,10 +304,9 @@
             act_gate = gate_pre * sig_gate
             hidden = (weight * act_gate * up_pre).astype(jnp.bfloat16)
             hidden_out[:, pl.ds(core ^ side, 1)] = hidden.reshape(planes, 1, capacity, tile)
-            cot = cot_ref[:, pl.ds(core ^ side, 1)].reshape(count, tile)
+            cot = cot_ref[:, pl.ds(core ^ side, 1), :, columns].reshape(count, tile)
             d_pre = cot.astype(jnp.float32) * (weight * inverse)
             d_gate = d_pre * up_pre * sig_gate * (1.0 + gate_pre * (1.0 - sig_gate))
-            columns = slice(t * tile, (t + 1) * tile)
             d_gate_scratch[span, columns] = d_gate.astype(jnp.bfloat16)
             d_up_scratch[span, columns] = (d_pre * act_gate).astype(jnp.bfloat16)
 
@@ -316,7 +327,8 @@
                 copies = row_copies((own_ref, other_ref), flat_scratch, aux_scratch, sems)
                 for copy in copies:
                     copy.start()
-                turn_copy.start()
+                for copy in (stats_copy, signs_copy, cot_copy, turn_copy):
+                    copy.start()
                 for copy in copies:
                     copy.wait()
             gate_scratch[t % 2] = gate_acc[...] + product(flat_scratch, gate_ref)
@@ -621,7 +633,7 @@
         ),
         in_specs=[smem(), row_spec, row_spec, any_spec]
         + [weight_spec, weight_spec, sum_spec, sum_spec]
-        + [whole(stats.shape), whole(signs.shape), unit_spec],
+        + [row_spec] * 3,
         out_specs=(unit_spec, grad_spec, grad_spec),
         grid=(tiles + experts * (units // stretch),),
         scratch_shapes=row_scratch
@@ -633,7 +645,10 @@
             pltpu.VMEM((2 * count, units), jnp.bfloat16),
             pltpu.VMEM((2 * count, units), jnp.bfloat16),
             pltpu.VMEM((experts, columns, 2 * count), jnp.bfloat16),
-            pltpu.SemaphoreType.DMA((2 + 2 * experts,)),
+            pltpu.VMEM((2 * count, lanes), jnp.float32),
+            pltpu.VMEM(signs.shape, jnp.float32),
+            pltpu.VMEM((planes, 2, capacity, units), jnp.bfloat16),
+            pltpu.SemaphoreType.DMA((5 + 2 * experts,)),
         ],
         compiler_params=params(48),
         name="late",

time: 190 us -> 191 us (level)
  no operation moved by 1% of the time
where the time goes in v4:
time: 191 us
  waiting for transfers between devices  56.1 us (29%)
  Pallas kernels  52.6 us (28%)
  starting transfers between devices  47.8 us (25%)
  local copies, waits for them, and re-layouts  20.4 us (11%)
  other arithmetic  9.05 us (5%)
  matrix products  3.51 us (2%)
    ppermute x27, waiting for transfers between devices, exchange(): return lax.ppermute(value, axis, [(i, i ^ offset) for i in range(size)])  53.7 us
    pallas_call x1, Pallas kernels, per_device(): pl.pallas_call(functools.partial(late_kernel, float(width), tiles), out_s...  30.8 us
    ppermute x27, starting transfers between devices, exchange(): return lax.ppermute(value, axis, [(i, i ^ offset) for i in range(size)])  30.3 us
    unnamed x47, local copies, waits for them, and re-layouts  17.7 us
    pallas_call x1, Pallas kernels, per_device(): pl.pallas_call(functools.partial(early_kernel, tiles), out_shape=(sums, s...  12.3 us
    all_to_all x2, starting transfers between devices, to_experts(): lax.all_to_all(slots[c], 'expert', split_axis=0, concat_axis=0, tiled=True)  7.39 us
    all_to_all x1, starting transfers between devices, per_device(): lax.all_to_all(context.reshape(experts, quarter, columns), 'expert', spli...  5.18 us
    all_to_all x1, starting transfers between devices, per_device(): lax.all_to_all(to_blocks, 'fsdp', split_axis=0, concat_axis=0, tiled=True)  4.88 us
  transfers between devices with their start and end apart: 31, of which 19 were waited for; matrix products, arithmetic and copies ran while one was open for 6% of the time, Pallas kernels for 10%

profile of v4, /device:TPU:0, one launch (start us, length us, event | category | flops | bytes accessed | tf_op | source)
XLA Modules:
  0.0 190.5 jit_solution(2782725493406771935)
XLA Ops:
  0.6 5.2 %all-to-all-start = ((bf16[4,32,1024]{2,1,0:T(8,128)(2,1)}), bf16[4,32,1024]{2,1,0:T(8,128)(2,1)S(1)}, u32[]{:S(2)}, u32[]{:S(2)}) async-start(bf16[4,32,1024]{2,1,0:T(8,128)(2,1)} %bitcast.110), calls=%async_computation | async-start | bytes 524288 | tf_op jit(solution)/shard_map/all_to_all | solution.py:448
  5.9 2.2 %copy-done = bf16[1,512,4096]{2,1,0:T(8,128)(2,1)S(1)} copy-done((bf16[1,512,4096]{2,1,0:T(8,128)(2,1)S(1)}, bf16[1,512,4096]{2,1,0:T(8,128)(2,1)}, u32[]{:S(2)}) %copy-start) | copy-done | bytes 4194328
  8.1 0.8 pack.2
  8.9 2.3 %all-to-all-done.shares_ref = bf16[4,32,1024]{2,1,0:T(8,128)(2,1)S(1)} async-done(((bf16[4,32,1024]{2,1,0:T(8,128)(2,1)}), bf16[4,32,1024]{2,1,0:T(8,128)(2,1)S(1)}, u32[]{:S(2)}, u32[]{:S(2)}) %all-to-all-start) | async-done | bytes 262176 | tf_op jit(solution)/shard_map/all_to_all | solution.py:448
  11.2 1.3 collective-permute-start
  13.8 4.9 %all-to-all-start.1 = ((bf16[8,48,512]{2,1,0:T(8,128)(2,1)}), bf16[8,48,512]{2,1,0:T(8,128)(2,1)S(1)}, u32[]{:S(2)}, u32[]{:S(2)}) async-start(bf16[8,48,512]{2,1,0:T(8,128)(2,1)} %spread.1), calls=%async_computation.1 | async-start | bytes 786432 | tf_op jit(solution)/shard_map/all_to_all | solution.py:464
  18.7 4.7 %collective-permute-done = bf16[2,256,512]{2,1,0:T(8,128)(2,1)S(1)} collective-permute-done((bf16[2,256,512]{2,1,0:T(8,128)(2,1)S(1)}, bf16[2,256,512]{2,1,0:T(8,128)(2,1)S(1)}, u32[]{:S(2)}, u32[]{:S(2)}) %collective-permute-start) | collective-permute-done | bytes 524320 | tf_op jit(solution)/shard_map/ppermute | solution.py:16
  23.4 1.0 collective-permute-done.1
  24.4 1.4 add_convert_fusion.2
  25.8 0.8 collective-permute-start.3
  26.6 1.5 collective-permute-start.2
  28.1 2.2 %copy-done.1 = bf16[1,512,4096]{2,1,0:T(8,128)(2,1)S(1)} copy-done((bf16[1,512,4096]{2,1,0:T(8,128)(2,1)S(1)}, bf16[1,512,4096]{2,1,0:T(8,128)(2,1)}, u32[]{:S(2)}) %copy-start.1) | copy-done | bytes 4194328
  30.3 0.8 pack.3
  31.3 0.9 collective-permute-done.3
  32.2 0.8 collective-permute-done.2
  33.0 1.6 collective-permute-start.6
  34.6 1.1 collective-permute-start.5
  35.8 0.8 collective-permute-start.4
  36.6 1.4 add_bitcast_fusion.3
  38.1 4.9 %collective-permute-done.6 = bf16[8,32,512]{2,1,0:T(8,128)(2,1)S(1)} collective-permute-done((bf16[8,32,512]{2,1,0:T(8,128)(2,1)S(1)}, bf16[8,32,512]{2,1,0:T(8,128)(2,1)S(1)}, u32[]{:S(2)}, u32[]{:S(2)}) %collective-permute-start.6) | collective-permute-done | bytes 262176 | tf_op jit(solution)/shard_map/ppermute | solution.py:16
  43.0 2.7 %collective-permute-done.5 = bf16[8,32,512]{2,1,0:T(8,128)(2,1)S(1)} collective-permute-done((bf16[8,32,512]{2,1,0:T(8,128)(2,1)S(1)}, bf16[8,32,512]{2,1,0:T(8,128)(2,1)S(1)}, u32[]{:S(2)}, u32[]{:S(2)}) %collective-permute-start.5) | collective-permute-done | bytes 262176 | tf_op jit(solution)/shard_map/ppermute | solution.py:16
  46.5 1.2 convolution_convert_fusion.1
  47.7 1.4 collective-permute-start.7
  49.9 1.4 convert_add_fusion.1
  51.3 1.9 fusion.24
  53.1 3.9 %collective-permute-start.14 = (bf16[128,512]{1,0:T(8,128)(2,1)}, bf16[128,512]{1,0:T(8,128)(2,1)S(1)}, u32[]{:S(2)}, u32[]{:S(2)}) collective-permute-start(bf16[128,512]{1,0:T(8,128)(2,1)} %get-tuple-element.93), channel_id=1, source_target_pairs={{0,6},{1,7},{2,4},{3,5},{4,2},{5,3},{6,0},{7,1},{8,14},{9,15},{10,... | collective-permute-start | bytes 393224 | tf_op jit(solution)/shard_map/ppermute | solution.py:16
  57.6 4.6 %collective-permute-done.7 = bf16[2,256,512]{2,1,0:T(8,128)(2,1)} collective-permute-done((bf16[2,256,512]{2,1,0:T(8,128)(2,1)S(1)}, bf16[2,256,512]{2,1,0:T(8,128)(2,1)}, u32[]{:S(2)}, u32[]{:S(2)}) %collective-permute-start.7) | collective-permute-done | bytes 524320 | tf_op jit(solution)/shard_map/ppermute | solution.py:16
  62.1 1.1 collective-permute-done.8
  63.3 1.3 add_convert_fusion
  65.3 1.4 collective-permute-start.10
  66.7 2.1 %collective-permute-done.13 = bf16[128,512]{1,0:T(8,128)(2,1)} collective-permute-done((bf16[128,512]{1,0:T(8,128)(2,1)}, bf16[128,512]{1,0:T(8,128)(2,1)}, u32[]{:S(2)}, u32[]{:S(2)}) %collective-permute-start.13) | collective-permute-done | bytes 131104 | tf_op jit(solution)/shard_map/ppermute | solution.py:16
  68.8 1.2 fusion.21.refs_0_
  70.0 2.2 %collective-permute-done.11 = bf16[1,256,512]{2,1,0:T(8,128)(2,1)S(1)} collective-permute-done((bf16[1,256,512]{2,1,0:T(8,128)(2,1)S(1)}, bf16[1,256,512]{2,1,0:T(8,128)(2,1)S(1)}, u32[]{:S(2)}, u32[]{:S(2)}) %collective-permute-start.11) | collective-permute-done | bytes 262176 | tf_op jit(solution)/shard_map/ppermute | solution.py:16
  73.0 1.5 add_bitcast_fusion.1
  75.2 0.9 slice_convert_fusion
  76.1 3.7 %collective-permute-start.21 = (bf16[128,512]{1,0:T(8,128)(2,1)S(1)}, bf16[128,512]{1,0:T(8,128)(2,1)S(1)}, u32[]{:S(2)}, u32[]{:S(2)}) collective-permute-start(bf16[128,512]{1,0:T(8,128)(2,1)S(1)} %fusion.21.refs_0_), channel_id=1, source_target_pairs={{0,6},{1,7},{2,4},{3,5},{4,2},{5,3},{6,0},{7,1},{8,14},{9,15},{10,... | collective-permute-start | bytes 393224 | tf_op jit(solution)/shard_map/ppermute | solution.py:16
  81.0 0.9 fusion.27
  81.9 2.4 %collective-permute-done.21.refs_3_ = bf16[128,512]{1,0:T(8,128)(2,1)S(1)} collective-permute-done((bf16[128,512]{1,0:T(8,128)(2,1)S(1)}, bf16[128,512]{1,0:T(8,128)(2,1)S(1)}, u32[]{:S(2)}, u32[]{:S(2)}) %collective-permute-start.21) | collective-permute-done | bytes 131104 | tf_op jit(solution)/shard_map/ppermute | solution.py:16
  84.3 7.3 %collective-permute-done.20.refs_2_ = bf16[128,512]{1,0:T(8,128)(2,1)S(1)} collective-permute-done((bf16[128,512]{1,0:T(8,128)(2,1)S(1)}, bf16[128,512]{1,0:T(8,128)(2,1)S(1)}, u32[]{:S(2)}, u32[]{:S(2)}) %collective-permute-start.20) | collective-permute-done | bytes 131104 | tf_op jit(solution)/shard_map/ppermute | solution.py:16
  91.7 2.3 %dispatch.2 = bf16[4,400,512]{2,1,0:T(8,128)(2,1)} custom-call(s32[3]{0:T(128)S(1)} %pad_add_fusion.position_ref, s32[8,4,128]{2,1,0:T(4,128)S(1)} %bitcast.102, bf16[16,1024]{1,0:T(8,128)(2,1)S(1)} %fusion.30.extra_ref, bf16[128,512]{1,0:T(8,128)(2,1)S(1)} %fusion.21.refs_0_, bf16[128,512]{1,0:T(8,128)(2,1)S(1)} %collective-permute-done.19.refs_1_, ...), custom_call_target="tpu_custom_call" | custom-call | tf_op jit(solution)/shard_map/dispatch/pallas_call | solution.py:527
  94.0 3.6 %all-to-all-start.3 = ((bf16[4,400,512]{2,1,0:T(8,128)(2,1)}), bf16[4,400,512]{2,1,0:T(8,128)(2,1)S(1)}, u32[]{:S(2)}, u32[]{:S(2)}) async-start(bf16[4,400,512]{2,1,0:T(8,128)(2,1)} %dispatch.2), calls=%async_computation.3 | async-start | bytes 3276800 | tf_op jit(solution)/shard_map/all_to_all | solution.py:575
  97.5 2.5 %collective-permute-start.18 = (bf16[128,512]{1,0:T(8,128)(2,1)}, bf16[128,512]{1,0:T(8,128)(2,1)S(1)}, u32[]{:S(2)}, u32[]{:S(2)}) collective-permute-start(bf16[128,512]{1,0:T(8,128)(2,1)} %get-tuple-element.90), channel_id=1, source_target_pairs={{0,6},{1,7},{2,4},{3,5},{4,2},{5,3},{6,0},{7,1},{8,14},{9,15},{10,... | collective-permute-start | bytes 393224 | tf_op jit(solution)/shard_map/ppermute | solution.py:16
  100.1 1.9 %collective-permute-start.16 = (bf16[128,512]{1,0:T(8,128)(2,1)S(1)}, bf16[128,512]{1,0:T(8,128)(2,1)S(1)}, u32[]{:S(2)}, u32[]{:S(2)}) collective-permute-start(bf16[128,512]{1,0:T(8,128)(2,1)S(1)} %get-tuple-element.92), channel_id=1, source_target_pairs={{0,2},{1,3},{2,0},{3,1},{4,6},{5,7},{6,4},{7,5},{8,10},{9,11},{10,... | collective-permute-start | bytes 393224 | tf_op jit(solution)/shard_map/ppermute | solution.py:16
  102.0 4.1 %collective-permute-done.18 = bf16[128,512]{1,0:T(8,128)(2,1)S(1)} collective-permute-done((bf16[128,512]{1,0:T(8,128)(2,1)}, bf16[128,512]{1,0:T(8,128)(2,1)S(1)}, u32[]{:S(2)}, u32[]{:S(2)}) %collective-permute-start.18) | collective-permute-done | bytes 131104 | tf_op jit(solution)/shard_map/ppermute | solution.py:16
  106.1 4.4 %collective-permute-done.17 = bf16[128,512]{1,0:T(8,128)(2,1)S(1)} collective-permute-done((bf16[128,512]{1,0:T(8,128)(2,1)}, bf16[128,512]{1,0:T(8,128)(2,1)S(1)}, u32[]{:S(2)}, u32[]{:S(2)}) %collective-permute-start.17) | collective-permute-done | bytes 131104 | tf_op jit(solution)/shard_map/ppermute | solution.py:16
  110.5 1.0 fusion.16.refs_0_
  111.5 2.4 %collective-permute-start.24 = (bf16[128,512]{1,0:T(8,128)(2,1)S(1)}, bf16[128,512]{1,0:T(8,128)(2,1)S(1)}, u32[]{:S(2)}, u32[]{:S(2)}) collective-permute-start(bf16[128,512]{1,0:T(8,128)(2,1)S(1)} %fusion.16.refs_0_), channel_id=1, source_target_pairs={{0,6},{1,7},{2,4},{3,5},{4,2},{5,3},{6,0},{7,1},{8,14},{9,15},{10,... | collective-permute-start | bytes 393224 | tf_op jit(solution)/shard_map/ppermute | solution.py:16
  113.9 2.1 %collective-permute-start.22 = (bf16[128,512]{1,0:T(8,128)(2,1)S(1)}, bf16[128,512]{1,0:T(8,128)(2,1)S(1)}, u32[]{:S(2)}, u32[]{:S(2)}) collective-permute-start(bf16[128,512]{1,0:T(8,128)(2,1)S(1)} %fusion.16.refs_0_), channel_id=1, source_target_pairs={{0,2},{1,3},{2,0},{3,1},{4,6},{5,7},{6,4},{7,5},{8,10},{9,11},{10,... | collective-permute-start | bytes 393224 | tf_op jit(solution)/shard_map/ppermute | solution.py:16
  116.0 0.8 signs.1
  116.8 1.1 join.1
  117.9 2.0 %collective-permute-done.24.refs_3_ = bf16[128,512]{1,0:T(8,128)(2,1)S(1)} collective-permute-done((bf16[128,512]{1,0:T(8,128)(2,1)S(1)}, bf16[128,512]{1,0:T(8,128)(2,1)S(1)}, u32[]{:S(2)}, u32[]{:S(2)}) %collective-permute-start.24) | collective-permute-done | bytes 131104 | tf_op jit(solution)/shard_map/ppermute | solution.py:16
  119.9 5.1 %collective-permute-done.23.refs_2_ = bf16[128,512]{1,0:T(8,128)(2,1)S(1)} collective-permute-done((bf16[128,512]{1,0:T(8,128)(2,1)S(1)}, bf16[128,512]{1,0:T(8,128)(2,1)S(1)}, u32[]{:S(2)}, u32[]{:S(2)}) %collective-permute-start.23) | collective-permute-done | bytes 131104 | tf_op jit(solution)/shard_map/ppermute | solution.py:16
  125.0 2.3 %dispatch.3 = bf16[4,400,512]{2,1,0:T(8,128)(2,1)} custom-call(s32[3]{0:T(128)S(1)} %pad_add_fusion.position_ref, s32[8,4,128]{2,1,0:T(4,128)S(1)} %bitcast.104, bf16[16,1024]{1,0:T(8,128)(2,1)S(1)} %fusion.30.extra_ref, bf16[128,512]{1,0:T(8,128)(2,1)S(1)} %fusion.16.refs_0_, bf16[128,512]{1,0:T(8,128)(2,1)S(1)} %collective-permute-done.22.refs_1_, ...), custom_call_target="tpu_custom_call" | custom-call | tf_op jit(solution)/shard_map/dispatch/pallas_call | solution.py:527
  127.3 3.8 %all-to-all-start.2 = ((bf16[4,400,512]{2,1,0:T(8,128)(2,1)}), bf16[4,400,512]{2,1,0:T(8,128)(2,1)S(1)}, u32[]{:S(2)}, u32[]{:S(2)}) async-start(bf16[4,400,512]{2,1,0:T(8,128)(2,1)} %dispatch.3), calls=%async_computation.2 | async-start | bytes 3276800 | tf_op jit(solution)/shard_map/all_to_all | solution.py:575
  131.1 3.4 %copy-done.2 = bf16[1,4096,1024]{2,1,0:T(8,128)(2,1)S(1)} copy-done((bf16[1,4096,1024]{2,1,0:T(8,128)(2,1)S(1)}, bf16[1,4096,1024]{2,1,0:T(8,128)(2,1)}, u32[]{:S(2)}) %copy-start.2) | copy-done | bytes 8388632
  134.5 12.3 %early.1 = (f32[768,1024]{1,0:T(8,128)S(1)}, f32[768,1024]{1,0:T(8,128)S(1)}, f32[768,16]{1,0:T(8,128)S(1)}, bf16[4,512,768]{2,1,0:T(8,128)(2,1)S(1)}) custom-call(bf16[4,400,512]{2,1,0:T(8,128)(2,1)S(1)} %all-to-all-done.3.own_ref, bf16[4,400,512]{2,1,0:T(8,128)(2,1)} %collective-permute-done.25.other_ref, bf16[4,2,512,1024]{3,2,1,0:T(8,128)(2,1)S(1)} %bitcast.94, ...), custom_call_target="tpu_custom_call" | custom-call | flops 6442450944 | bytes 8388608 | tf_op jit(solution)/shard_map/early/pallas_call | solution.py:588
  146.8 1.7 copy-done.3
  148.5 1.7 copy-done.4
  150.2 1.6 copy-done.5
  153.0 3.1 %collective-permute-done.26.other_ref = bf16[4,400,512]{2,1,0:T(8,128)(2,1)S(1)} collective-permute-done((bf16[4,400,512]{2,1,0:T(8,128)(2,1)S(1)}, bf16[4,400,512]{2,1,0:T(8,128)(2,1)S(1)}, u32[]{:S(2)}, u32[]{:S(2)}) %collective-permute-start.26) | collective-permute-done | bytes 1638432 | tf_op jit(solution)/shard_map/ppermute | solution.py:16
  156.1 1.0 copy-done.7
  157.1 1.4 copy-done.8
  158.5 1.0 copy-done.10
  159.5 30.8 %late.1 = (bf16[4,2,96,1024]{3,2,1,0:T(8,128)(2,1)}, bf16[4,1024,1024]{2,1,0:T(8,128)(2,1)}, bf16[4,1024,1024]{2,1,0:T(8,128)(2,1)}) custom-call(s32[3]{0:T(128)S(1)} %pad_add_fusion.position_ref, bf16[4,400,512]{2,1,0:T(8,128)(2,1)S(1)} %all-to-all-done.2.own_ref, bf16[4,400,512]{2,1,0:T(8,128)(2,1)S(1)} %collective-permute-done.26.other_ref, ...), custom_call_target="tpu_custom_call" | custom-call | tf_op jit(solution)/shard_map/late/pallas_call | solution.py:627
  (79 shorter events, 8.2 us)
Async XLA Ops:
  0.6 10.5 %all-to-all-start = ((bf16[4,32,1024]{2,1,0:T(8,128)(2,1)}), bf16[4,32,1024]{2,1,0:T(8,128)(2,1)S(1)}, u32[]{:S(2)}, u32[]{:S(2)}) async-start(bf16[4,32,1024]{2,1,0:T(8,128)(2,1)} %bitcast.110), calls=%async_computation | async-start | bytes 524288 | tf_op jit(solution)/shard_map/all_to_all | solution.py:448
  5.9 2.2 %copy-start = (bf16[1,512,4096]{2,1,0:T(8,128)(2,1)S(1)}, bf16[1,512,4096]{2,1,0:T(8,128)(2,1)}, u32[]{:S(2)}) copy-start(bf16[1,512,4096]{2,1,0:T(8,128)(2,1)} %param.10) | copy-start | bytes 12582916
  8.1 4.9 %copy-start.21 = (s32[128,2]{0,1:T(2,128)S(1)}, s32[128,2]{0,1:T(2,128)}, u32[]{:S(2)}) copy-start(s32[128,2]{0,1:T(2,128)} %param.17) | copy-start | bytes 3076
  8.1 4.9 %copy-start.22 = (s32[128,2]{0,1:T(2,128)S(1)}, s32[128,2]{0,1:T(2,128)}, u32[]{:S(2)}) copy-start(s32[128,2]{0,1:T(2,128)} %param.18) | copy-start | bytes 3076
  11.2 12.3 %collective-permute-start = (bf16[2,256,512]{2,1,0:T(8,128)(2,1)S(1)}, bf16[2,256,512]{2,1,0:T(8,128)(2,1)S(1)}, u32[]{:S(2)}, u32[]{:S(2)}) collective-permute-start(bf16[2,256,512]{2,1,0:T(8,128)(2,1)S(1)} %get-tuple-element.45), channel_id=1, source_target_pairs={{0,8},{8,0},{16,24},{24,16},{1,9},{9,1},{17,25},{25,17},{2,10},{10... | collective-permute-start | bytes 1572872 | tf_op jit(solution)/shard_map/ppermute | solution.py:16
  12.4 12.0 %collective-permute-start.1 = (bf16[2,256,512]{2,1,0:T(8,128)(2,1)S(1)}, bf16[2,256,512]{2,1,0:T(8,128)(2,1)S(1)}, u32[]{:S(2)}, u32[]{:S(2)}) collective-permute-start(bf16[2,256,512]{2,1,0:T(8,128)(2,1)S(1)} %get-tuple-element.46), channel_id=1, source_target_pairs={{0,16},{8,24},{16,0},{24,8},{1,17},{9,25},{17,1},{25,9},{2,18},{10... | collective-permute-start | bytes 1572872 | tf_op jit(solution)/shard_map/ppermute | solution.py:16
  13.8 17.4 %all-to-all-start.1 = ((bf16[8,48,512]{2,1,0:T(8,128)(2,1)}), bf16[8,48,512]{2,1,0:T(8,128)(2,1)S(1)}, u32[]{:S(2)}, u32[]{:S(2)}) async-start(bf16[8,48,512]{2,1,0:T(8,128)(2,1)} %spread.1), calls=%async_computation.1 | async-start | bytes 786432 | tf_op jit(solution)/shard_map/all_to_all | solution.py:464
  23.4 4.7 %copy-start.13 = (bf16[2,256,512]{2,1,0:T(8,128)(2,1)}, bf16[2,256,512]{2,1,0:T(8,128)(2,1)S(1)}, u32[]{:S(2)}) copy-start(bf16[2,256,512]{2,1,0:T(8,128)(2,1)S(1)} %collective-permute-done) | copy-start | bytes 1572868
  24.4 3.7 %copy-start.15 = (bf16[2,256,512]{2,1,0:T(8,128)(2,1)}, bf16[2,256,512]{2,1,0:T(8,128)(2,1)S(1)}, u32[]{:S(2)}) copy-start(bf16[2,256,512]{2,1,0:T(8,128)(2,1)S(1)} %collective-permute-done.1) | copy-start | bytes 1572868
  25.8 6.4 %collective-permute-start.3 = (bf16[1,256,512]{2,1,0:T(8,128)(2,1)S(1)}, bf16[1,256,512]{2,1,0:T(8,128)(2,1)S(1)}, u32[]{:S(2)}, u32[]{:S(2)}) collective-permute-start(bf16[1,256,512]{2,1,0:T(8,128)(2,1)S(1)} %get-tuple-element.88), channel_id=1, source_target_pairs={{0,8},{8,0},{16,24},{24,16},{1,9},{9,1},{17,25},{25,17},{2,10},{10... | collective-permute-start | bytes 786440 | tf_op jit(solution)/shard_map/ppermute | solution.py:16
  26.6 6.4 %collective-permute-start.2 = (bf16[1,256,512]{2,1,0:T(8,128)(2,1)S(1)}, bf16[1,256,512]{2,1,0:T(8,128)(2,1)S(1)}, u32[]{:S(2)}, u32[]{:S(2)}) collective-permute-start(bf16[1,256,512]{2,1,0:T(8,128)(2,1)S(1)} %get-tuple-element.89), channel_id=1, source_target_pairs={{0,16},{8,24},{16,0},{24,8},{1,17},{9,25},{17,1},{25,9},{2,18},{10... | collective-permute-start | bytes 786440 | tf_op jit(solution)/shard_map/ppermute | solution.py:16
  28.1 2.2 %copy-start.1 = (bf16[1,512,4096]{2,1,0:T(8,128)(2,1)S(1)}, bf16[1,512,4096]{2,1,0:T(8,128)(2,1)}, u32[]{:S(2)}) copy-start(bf16[1,512,4096]{2,1,0:T(8,128)(2,1)} %param.10) | copy-start | bytes 12582916
  30.3 6.3 %copy-start.14 = (bf16[2,256,512]{2,1,0:T(8,128)(2,1)S(1)}, bf16[2,256,512]{2,1,0:T(8,128)(2,1)}, u32[]{:S(2)}) copy-start(bf16[2,256,512]{2,1,0:T(8,128)(2,1)} %copy-done.13) | copy-start | bytes 1572868
  31.3 4.5 %copy-start.12 = (bf16[8,48,512]{2,1,0:T(8,128)(2,1)}, bf16[8,48,512]{2,1,0:T(8,128)(2,1)S(1)}, u32[]{:S(2)}) copy-start(bf16[8,48,512]{2,1,0:T(8,128)(2,1)S(1)} %all-to-all-done.1) | copy-start | bytes 1179652
  33.0 2.8 %copy-start.18 = (bf16[1,256,512]{2,1,0:T(8,128)(2,1)}, bf16[1,256,512]{2,1,0:T(8,128)(2,1)S(1)}, u32[]{:S(2)}) copy-start(bf16[1,256,512]{2,1,0:T(8,128)(2,1)S(1)} %collective-permute-done.2) | copy-start | bytes 786436
  33.0 10.0 %collective-permute-start.6 = (bf16[8,32,512]{2,1,0:T(8,128)(2,1)S(1)}, bf16[8,32,512]{2,1,0:T(8,128)(2,1)S(1)}, u32[]{:S(2)}, u32[]{:S(2)}) collective-permute-start(bf16[8,32,512]{2,1,0:T(8,128)(2,1)S(1)} %slice.18), channel_id=1, source_target_pairs={{0,24},{8,16},{16,8},{24,0},{1,25},{9,17},{17,9},{25,1},{2,26},{10... | collective-permute-start | bytes 786440 | tf_op jit(solution)/shard_map/ppermute | solution.py:16
  34.6 11.1 %collective-permute-start.5 = (bf16[8,32,512]{2,1,0:T(8,128)(2,1)S(1)}, bf16[8,32,512]{2,1,0:T(8,128)(2,1)S(1)}, u32[]{:S(2)}, u32[]{:S(2)}) collective-permute-start(bf16[8,32,512]{2,1,0:T(8,128)(2,1)S(1)} %slice.18), channel_id=1, source_target_pairs={{0,16},{8,24},{16,0},{24,8},{1,17},{9,25},{17,1},{25,9},{2,18},{10... | collective-permute-start | bytes 786440 | tf_op jit(solution)/shard_map/ppermute | solution.py:16
  35.8 10.0 %collective-permute-start.4 = (bf16[8,32,512]{2,1,0:T(8,128)(2,1)S(1)}, bf16[8,32,512]{2,1,0:T(8,128)(2,1)S(1)}, u32[]{:S(2)}, u32[]{:S(2)}) collective-permute-start(bf16[8,32,512]{2,1,0:T(8,128)(2,1)S(1)} %slice.18), channel_id=1, source_target_pairs={{0,8},{8,0},{16,24},{24,16},{1,9},{9,1},{17,25},{25,17},{2,10},{10... | collective-permute-start | bytes 786440 | tf_op jit(solution)/shard_map/ppermute | solution.py:16
  46.4 20.3 %copy-start.19 = (bf16[1024]{0:T(1024)(128)(2,1)S(1)}, bf16[1024]{0:T(1024)(128)(2,1)}, u32[]{:S(2)}) copy-start(bf16[1024]{0:T(1024)(128)(2,1)} %param.13) | copy-start | bytes 6148
  46.4 22.4 %copy-start.16 = (bf16[128,1024]{1,0:T(8,128)(2,1)S(1)}, bf16[128,1024]{1,0:T(8,128)(2,1)}, u32[]{:S(2)}) copy-start(bf16[128,1024]{1,0:T(8,128)(2,1)} %param.12) | copy-start | bytes 786436
  47.7 2.2 %collective-permute-start.9 = (bf16[4,128,512]{2,1,0:T(8,128)(2,1)}, bf16[4,128,512]{2,1,0:T(8,128)(2,1)S(1)}, u32[]{:S(2)}, u32[]{:S(2)}) collective-permute-start(bf16[4,128,512]{2,1,0:T(8,128)(2,1)} %convolution_convert_fusion.1), channel_id=1, source_target_pairs={{0,1},{1,0},{2,3},{3,2},{4,5},{5,4},{6,7},{7,6},{8,9},{9,8},{10,11... | collective-permute-start | bytes 1572872 | tf_op jit(solution)/shard_map/ppermute | solution.py:16
  47.7 14.4 %collective-permute-start.7 = (bf16[2,256,512]{2,1,0:T(8,128)(2,1)S(1)}, bf16[2,256,512]{2,1,0:T(8,128)(2,1)}, u32[]{:S(2)}, u32[]{:S(2)}) collective-permute-start(bf16[2,256,512]{2,1,0:T(8,128)(2,1)S(1)} %get-tuple-element.54), channel_id=1, source_target_pairs={{0,8},{8,0},{16,24},{24,16},{1,9},{9,1},{17,25},{25,17},{2,10},{10... | collective-permute-start | bytes 1572872 | tf_op jit(solution)/shard_map/ppermute | solution.py:16
  49.1 14.2 %collective-permute-start.8 = (bf16[2,256,512]{2,1,0:T(8,128)(2,1)S(1)}, bf16[2,256,512]{2,1,0:T(8,128)(2,1)}, u32[]{:S(2)}, u32[]{:S(2)}) collective-permute-start(bf16[2,256,512]{2,1,0:T(8,128)(2,1)S(1)} %get-tuple-element.55), channel_id=1, source_target_pairs={{0,16},{8,24},{16,0},{24,8},{1,17},{9,25},{17,1},{25,9},{2,18},{10... | collective-permute-start | bytes 1572872 | tf_op jit(solution)/shard_map/ppermute | solution.py:16
  53.1 13.6 %collective-permute-start.14 = (bf16[128,512]{1,0:T(8,128)(2,1)}, bf16[128,512]{1,0:T(8,128)(2,1)S(1)}, u32[]{:S(2)}, u32[]{:S(2)}) collective-permute-start(bf16[128,512]{1,0:T(8,128)(2,1)} %get-tuple-element.93), channel_id=1, source_target_pairs={{0,6},{1,7},{2,4},{3,5},{4,2},{5,3},{6,0},{7,1},{8,14},{9,15},{10,... | collective-permute-start | bytes 393224 | tf_op jit(solution)/shard_map/ppermute | solution.py:16
  57.0 11.8 %collective-permute-start.13 = (bf16[128,512]{1,0:T(8,128)(2,1)}, bf16[128,512]{1,0:T(8,128)(2,1)}, u32[]{:S(2)}, u32[]{:S(2)}) collective-permute-start(bf16[128,512]{1,0:T(8,128)(2,1)} %get-tuple-element.94), channel_id=1, source_target_pairs={{0,4},{1,5},{2,6},{3,7},{4,0},{5,1},{6,2},{7,3},{8,12},{9,13},{10,... | collective-permute-start | bytes 393224 | tf_op jit(solution)/shard_map/ppermute | solution.py:16
  57.0 11.8 %collective-permute-start.12 = (bf16[128,512]{1,0:T(8,128)(2,1)}, bf16[128,512]{1,0:T(8,128)(2,1)}, u32[]{:S(2)}, u32[]{:S(2)}) collective-permute-start(bf16[128,512]{1,0:T(8,128)(2,1)} %get-tuple-element.95), channel_id=1, source_target_pairs={{0,2},{1,3},{2,0},{3,1},{4,6},{5,7},{6,4},{7,5},{8,10},{9,11},{10,... | collective-permute-start | bytes 393224 | tf_op jit(solution)/shard_map/ppermute | solution.py:16
  64.6 7.7 %collective-permute-start.11 = (bf16[1,256,512]{2,1,0:T(8,128)(2,1)S(1)}, bf16[1,256,512]{2,1,0:T(8,128)(2,1)S(1)}, u32[]{:S(2)}, u32[]{:S(2)}) collective-permute-start(bf16[1,256,512]{2,1,0:T(8,128)(2,1)S(1)} %get-tuple-element.84), channel_id=1, source_target_pairs={{0,8},{8,0},{16,24},{24,16},{1,9},{9,1},{17,25},{25,17},{2,10},{10... | collective-permute-start | bytes 786440 | tf_op jit(solution)/shard_map/ppermute | solution.py:16
  65.3 7.7 %collective-permute-start.10 = (bf16[1,256,512]{2,1,0:T(8,128)(2,1)S(1)}, bf16[1,256,512]{2,1,0:T(8,128)(2,1)}, u32[]{:S(2)}, u32[]{:S(2)}) collective-permute-start(bf16[1,256,512]{2,1,0:T(8,128)(2,1)S(1)} %get-tuple-element.85), channel_id=1, source_target_pairs={{0,16},{8,24},{16,0},{24,8},{1,17},{9,25},{17,1},{25,9},{2,18},{10... | collective-permute-start | bytes 786440 | tf_op jit(solution)/shard_map/ppermute | solution.py:16
  68.8 6.4 %copy-start.20 = (bf16[1024,4]{0,1:T(4,128)(2,1)S(1)}, bf16[1024,4]{0,1:T(4,128)(2,1)}, u32[]{:S(2)}) copy-start(bf16[1024,4]{0,1:T(4,128)(2,1)} %param.14) | copy-start | bytes 24580
  72.3 0.7 copy-start.17
  75.1 5.5 %collective-permute-start.15 = (bf16[4,128,512]{2,1,0:T(8,128)(2,1)S(1)}, bf16[4,128,512]{2,1,0:T(8,128)(2,1)S(1)}, u32[]{:S(2)}, u32[]{:S(2)}) collective-permute-start(bf16[4,128,512]{2,1,0:T(8,128)(2,1)S(1)} %convolution_convert_fusion), channel_id=1, source_target_pairs={{0,1},{1,0},{2,3},{3,2},{4,5},{5,4},{6,7},{7,6},{8,9},{9,8},{10,11... | collective-permute-start | bytes 1572872 | tf_op jit(solution)/shard_map/ppermute | solution.py:16
  76.1 8.2 %collective-permute-start.21 = (bf16[128,512]{1,0:T(8,128)(2,1)S(1)}, bf16[128,512]{1,0:T(8,128)(2,1)S(1)}, u32[]{:S(2)}, u32[]{:S(2)}) collective-permute-start(bf16[128,512]{1,0:T(8,128)(2,1)S(1)} %fusion.21.refs_0_), channel_id=1, source_target_pairs={{0,6},{1,7},{2,4},{3,5},{4,2},{5,3},{6,0},{7,1},{8,14},{9,15},{10,... | collective-permute-start | bytes 393224 | tf_op jit(solution)/shard_map/ppermute | solution.py:16
  79.8 11.9 %collective-permute-start.20 = (bf16[128,512]{1,0:T(8,128)(2,1)S(1)}, bf16[128,512]{1,0:T(8,128)(2,1)S(1)}, u32[]{:S(2)}, u32[]{:S(2)}) collective-permute-start(bf16[128,512]{1,0:T(8,128)(2,1)S(1)} %fusion.21.refs_0_), channel_id=1, source_target_pairs={{0,4},{1,5},{2,6},{3,7},{4,0},{5,1},{6,2},{7,3},{8,12},{9,13},{10,... | collective-permute-start | bytes 393224 | tf_op jit(solution)/shard_map/ppermute | solution.py:16
  79.8 11.9 %collective-permute-start.19 = (bf16[128,512]{1,0:T(8,128)(2,1)S(1)}, bf16[128,512]{1,0:T(8,128)(2,1)S(1)}, u32[]{:S(2)}, u32[]{:S(2)}) collective-permute-start(bf16[128,512]{1,0:T(8,128)(2,1)S(1)} %fusion.21.refs_0_), channel_id=1, source_target_pairs={{0,2},{1,3},{2,0},{3,1},{4,6},{5,7},{6,4},{7,5},{8,10},{9,11},{10,... | collective-permute-start | bytes 393224 | tf_op jit(solution)/shard_map/ppermute | solution.py:16
  81.0 12.9 %copy-start.11 = (f32[4,128,512]{2,1,0:T(8,128)}, f32[4,128,512]{2,1,0:T(8,128)S(1)}, u32[]{:S(2)}) copy-start(f32[4,128,512]{2,1,0:T(8,128)S(1)} %convert_add_fusion) | copy-start | bytes 3145732
  94.0 33.3 %all-to-all-start.3 = ((bf16[4,400,512]{2,1,0:T(8,128)(2,1)}), bf16[4,400,512]{2,1,0:T(8,128)(2,1)S(1)}, u32[]{:S(2)}, u32[]{:S(2)}) async-start(bf16[4,400,512]{2,1,0:T(8,128)(2,1)} %dispatch.2), calls=%async_computation.3 | async-start | bytes 3276800 | tf_op jit(solution)/shard_map/all_to_all | solution.py:575
  97.5 8.5 %collective-permute-start.18 = (bf16[128,512]{1,0:T(8,128)(2,1)}, bf16[128,512]{1,0:T(8,128)(2,1)S(1)}, u32[]{:S(2)}, u32[]{:S(2)}) collective-permute-start(bf16[128,512]{1,0:T(8,128)(2,1)} %get-tuple-element.90), channel_id=1, source_target_pairs={{0,6},{1,7},{2,4},{3,5},{4,2},{5,3},{6,0},{7,1},{8,14},{9,15},{10,... | collective-permute-start | bytes 393224 | tf_op jit(solution)/shard_map/ppermute | solution.py:16
  100.1 10.4 %collective-permute-start.17 = (bf16[128,512]{1,0:T(8,128)(2,1)}, bf16[128,512]{1,0:T(8,128)(2,1)S(1)}, u32[]{:S(2)}, u32[]{:S(2)}) collective-permute-start(bf16[128,512]{1,0:T(8,128)(2,1)} %get-tuple-element.91), channel_id=1, source_target_pairs={{0,4},{1,5},{2,6},{3,7},{4,0},{5,1},{6,2},{7,3},{8,12},{9,13},{10,... | collective-permute-start | bytes 393224 | tf_op jit(solution)/shard_map/ppermute | solution.py:16
  100.1 10.4 %collective-permute-start.16 = (bf16[128,512]{1,0:T(8,128)(2,1)S(1)}, bf16[128,512]{1,0:T(8,128)(2,1)S(1)}, u32[]{:S(2)}, u32[]{:S(2)}) collective-permute-start(bf16[128,512]{1,0:T(8,128)(2,1)S(1)} %get-tuple-element.92), channel_id=1, source_target_pairs={{0,2},{1,3},{2,0},{3,1},{4,6},{5,7},{6,4},{7,5},{8,10},{9,11},{10,... | collective-permute-start | bytes 393224 | tf_op jit(solution)/shard_map/ppermute | solution.py:16
  111.5 8.3 %collective-permute-start.24 = (bf16[128,512]{1,0:T(8,128)(2,1)S(1)}, bf16[128,512]{1,0:T(8,128)(2,1)S(1)}, u32[]{:S(2)}, u32[]{:S(2)}) collective-permute-start(bf16[128,512]{1,0:T(8,128)(2,1)S(1)} %fusion.16.refs_0_), channel_id=1, source_target_pairs={{0,6},{1,7},{2,4},{3,5},{4,2},{5,3},{6,0},{7,1},{8,14},{9,15},{10,... | collective-permute-start | bytes 393224 | tf_op jit(solution)/shard_map/ppermute | solution.py:16
  113.9 11.1 %collective-permute-start.23 = (bf16[128,512]{1,0:T(8,128)(2,1)S(1)}, bf16[128,512]{1,0:T(8,128)(2,1)S(1)}, u32[]{:S(2)}, u32[]{:S(2)}) collective-permute-start(bf16[128,512]{1,0:T(8,128)(2,1)S(1)} %fusion.16.refs_0_), channel_id=1, source_target_pairs={{0,4},{1,5},{2,6},{3,7},{4,0},{5,1},{6,2},{7,3},{8,12},{9,13},{10,... | collective-permute-start | bytes 393224 | tf_op jit(solution)/shard_map/ppermute | solution.py:16
  113.9 11.1 %collective-permute-start.22 = (bf16[128,512]{1,0:T(8,128)(2,1)S(1)}, bf16[128,512]{1,0:T(8,128)(2,1)S(1)}, u32[]{:S(2)}, u32[]{:S(2)}) collective-permute-start(bf16[128,512]{1,0:T(8,128)(2,1)S(1)} %fusion.16.refs_0_), channel_id=1, source_target_pairs={{0,2},{1,3},{2,0},{3,1},{4,6},{5,7},{6,4},{7,5},{8,10},{9,11},{10,... | collective-permute-start | bytes 393224 | tf_op jit(solution)/shard_map/ppermute | solution.py:16
  116.8 1.1 copy-start.6
  127.3 3.8 %collective-permute-start.25 = (bf16[4,400,512]{2,1,0:T(8,128)(2,1)S(1)}, bf16[4,400,512]{2,1,0:T(8,128)(2,1)}, u32[]{:S(2)}, u32[]{:S(2)}) collective-permute-start(bf16[4,400,512]{2,1,0:T(8,128)(2,1)S(1)} %all-to-all-done.3.own_ref), channel_id=1, source_target_pairs={{0,1},{1,0},{2,3},{3,2},{4,5},{5,4},{6,7},{7,6},{8,9},{9,8},{10,11... | collective-permute-start | bytes 4915208 | tf_op jit(solution)/shard_map/ppermute | solution.py:16
  127.3 25.3 %all-to-all-start.2 = ((bf16[4,400,512]{2,1,0:T(8,128)(2,1)}), bf16[4,400,512]{2,1,0:T(8,128)(2,1)S(1)}, u32[]{:S(2)}, u32[]{:S(2)}) async-start(bf16[4,400,512]{2,1,0:T(8,128)(2,1)} %dispatch.3), calls=%async_computation.2 | async-start | bytes 3276800 | tf_op jit(solution)/shard_map/all_to_all | solution.py:575
  131.1 3.4 %copy-start.2 = (bf16[1,4096,1024]{2,1,0:T(8,128)(2,1)S(1)}, bf16[1,4096,1024]{2,1,0:T(8,128)(2,1)}, u32[]{:S(2)}) copy-start(bf16[1,4096,1024]{2,1,0:T(8,128)(2,1)} %param.15) | copy-start | bytes 25165828
  146.8 1.7 copy-start.3
  148.5 1.7 copy-start.4
  150.2 1.6 copy-start.5
  151.8 0.7 copy-start.9
  152.5 3.6 %collective-permute-start.26 = (bf16[4,400,512]{2,1,0:T(8,128)(2,1)S(1)}, bf16[4,400,512]{2,1,0:T(8,128)(2,1)S(1)}, u32[]{:S(2)}, u32[]{:S(2)}) collective-permute-start(bf16[4,400,512]{2,1,0:T(8,128)(2,1)S(1)} %all-to-all-done.2.own_ref), channel_id=1, source_target_pairs={{0,1},{1,0},{2,3},{3,2},{4,5},{5,4},{6,7},{7,6},{8,9},{9,8},{10,11... | collective-permute-start | bytes 4915208 | tf_op jit(solution)/shard_map/ppermute | solution.py:16
  156.1 1.0 copy-start.7
  157.1 1.4 copy-start.8
  158.5 1.0 copy-start.10

commit v5 on v4

--- a/solution.py
+++ b/solution.py
@@ -650,7 +650,7 @@
             pltpu.VMEM((planes, 2, capacity, units), jnp.bfloat16),
             pltpu.SemaphoreType.DMA((5 + 2 * experts,)),
         ],
-        compiler_params=params(48),
+        compiler_params=params(60),
         name="late",
     )(
         position,

time: 191 us -> 191 us (level)
  local copies, waits for them, and re-layouts: 20.4 us -> 17.6 us
    unnamed x47 -> x43, local copies, waits for them, and re-layouts: 17.7 us -> 14.8 us
  transfers between devices with their start and end apart: 31 -> 31, of which waited for: 19 -> 20; matrix products, arithmetic and copies ran while one was open for 6% -> 6% of each run, Pallas kernels for 10% -> 10%
where the time goes in v5:
time: 191 us
  waiting for transfers between devices  56.7 us (30%)
  Pallas kernels  54 us (28%)
  starting transfers between devices  48.7 us (25%)
  local copies, waits for them, and re-layouts  17.6 us (9%)
  other arithmetic  8.95 us (5%)
  matrix products  3.51 us (2%)
    ppermute x27, waiting for transfers between devices, exchange(): return lax.ppermute(value, axis, [(i, i ^ offset) for i in range(size)])  54.3 us
    pallas_call x1, Pallas kernels, per_device(): pl.pallas_call(functools.partial(late_kernel, float(width), tiles), out_s...  32.3 us
    ppermute x27, starting transfers between devices, exchange(): return lax.ppermute(value, axis, [(i, i ^ offset) for i in range(size)])  30.6 us
    unnamed x43, local copies, waits for them, and re-layouts  14.8 us
    pallas_call x1, Pallas kernels, per_device(): pl.pallas_call(functools.partial(early_kernel, tiles), out_shape=(sums, s...  12.3 us
    all_to_all x2, starting transfers between devices, to_experts(): lax.all_to_all(slots[c], 'expert', split_axis=0, concat_axis=0, tiled=True)  8.13 us
    all_to_all x1, starting transfers between devices, per_device(): lax.all_to_all(context.reshape(experts, quarter, columns), 'expert', spli...  5.18 us
    all_to_all x1, starting transfers between devices, per_device(): lax.all_to_all(to_blocks, 'fsdp', split_axis=0, concat_axis=0, tiled=True)  4.88 us
  transfers between devices with their start and end apart: 31, of which 20 were waited for; matrix products, arithmetic and copies ran while one was open for 6% of the time, Pallas kernels for 10%

profile of v5, /device:TPU:0, one launch (start us, length us, event | category | flops | bytes accessed | tf_op | source)
XLA Modules:
  0.0 190.6 jit_solution(9647886959259309706)
XLA Ops:
  0.6 5.2 %all-to-all-start = ((bf16[4,32,1024]{2,1,0:T(8,128)(2,1)}), bf16[4,32,1024]{2,1,0:T(8,128)(2,1)S(1)}, u32[]{:S(2)}, u32[]{:S(2)}) async-start(bf16[4,32,1024]{2,1,0:T(8,128)(2,1)} %bitcast.110), calls=%async_computation | async-start | bytes 524288 | tf_op jit(solution)/shard_map/all_to_all | solution.py:448
  5.9 2.2 %copy-done = bf16[1,512,4096]{2,1,0:T(8,128)(2,1)S(1)} copy-done((bf16[1,512,4096]{2,1,0:T(8,128)(2,1)S(1)}, bf16[1,512,4096]{2,1,0:T(8,128)(2,1)}, u32[]{:S(2)}) %copy-start) | copy-done | bytes 4194328
  8.1 0.8 pack.2
  8.9 2.3 %all-to-all-done.shares_ref = bf16[4,32,1024]{2,1,0:T(8,128)(2,1)S(1)} async-done(((bf16[4,32,1024]{2,1,0:T(8,128)(2,1)}), bf16[4,32,1024]{2,1,0:T(8,128)(2,1)S(1)}, u32[]{:S(2)}, u32[]{:S(2)}) %all-to-all-start) | async-done | bytes 262176 | tf_op jit(solution)/shard_map/all_to_all | solution.py:448
  11.2 1.3 collective-permute-start
  13.1 0.8 spread.1
  13.8 4.9 %all-to-all-start.1 = ((bf16[8,48,512]{2,1,0:T(8,128)(2,1)}), bf16[8,48,512]{2,1,0:T(8,128)(2,1)S(1)}, u32[]{:S(2)}, u32[]{:S(2)}) async-start(bf16[8,48,512]{2,1,0:T(8,128)(2,1)} %spread.1), calls=%async_computation.1 | async-start | bytes 786432 | tf_op jit(solution)/shard_map/all_to_all | solution.py:464
  18.7 4.7 %collective-permute-done = bf16[2,256,512]{2,1,0:T(8,128)(2,1)S(1)} collective-permute-done((bf16[2,256,512]{2,1,0:T(8,128)(2,1)S(1)}, bf16[2,256,512]{2,1,0:T(8,128)(2,1)S(1)}, u32[]{:S(2)}, u32[]{:S(2)}) %collective-permute-start) | collective-permute-done | bytes 524320 | tf_op jit(solution)/shard_map/ppermute | solution.py:16
  23.4 1.0 collective-permute-done.1
  24.4 1.4 add_convert_fusion.2
  25.8 0.8 collective-permute-start.3
  26.6 1.5 collective-permute-start.2
  28.1 2.2 %copy-done.1 = bf16[1,512,4096]{2,1,0:T(8,128)(2,1)S(1)} copy-done((bf16[1,512,4096]{2,1,0:T(8,128)(2,1)S(1)}, bf16[1,512,4096]{2,1,0:T(8,128)(2,1)}, u32[]{:S(2)}) %copy-start.1) | copy-done | bytes 4194328
  30.3 0.8 pack.3
  31.3 0.9 collective-permute-done.3
  32.2 0.8 collective-permute-done.2
  33.0 1.7 collective-permute-start.6
  34.7 1.1 collective-permute-start.5
  35.8 0.8 collective-permute-start.4
  36.6 1.4 add_bitcast_fusion.3
  38.1 4.9 %collective-permute-done.6 = bf16[8,32,512]{2,1,0:T(8,128)(2,1)S(1)} collective-permute-done((bf16[8,32,512]{2,1,0:T(8,128)(2,1)S(1)}, bf16[8,32,512]{2,1,0:T(8,128)(2,1)S(1)}, u32[]{:S(2)}, u32[]{:S(2)}) %collective-permute-start.6) | collective-permute-done | bytes 262176 | tf_op jit(solution)/shard_map/ppermute | solution.py:16
  43.0 2.7 %collective-permute-done.5 = bf16[8,32,512]{2,1,0:T(8,128)(2,1)S(1)} collective-permute-done((bf16[8,32,512]{2,1,0:T(8,128)(2,1)S(1)}, bf16[8,32,512]{2,1,0:T(8,128)(2,1)S(1)}, u32[]{:S(2)}, u32[]{:S(2)}) %collective-permute-start.5) | collective-permute-done | bytes 262176 | tf_op jit(solution)/shard_map/ppermute | solution.py:16
  46.5 1.2 convolution_convert_fusion.1
  47.7 1.4 collective-permute-start.7
  49.1 0.8 collective-permute-start.8
  49.9 1.4 convert_add_fusion.1
  51.3 1.9 fusion.24
  53.1 3.9 %collective-permute-start.14 = (bf16[128,512]{1,0:T(8,128)(2,1)}, bf16[128,512]{1,0:T(8,128)(2,1)}, u32[]{:S(2)}, u32[]{:S(2)}) collective-permute-start(bf16[128,512]{1,0:T(8,128)(2,1)} %get-tuple-element.93), channel_id=1, source_target_pairs={{0,6},{1,7},{2,4},{3,5},{4,2},{5,3},{6,0},{7,1},{8,14},{9,15},{10,... | collective-permute-start | bytes 393224 | tf_op jit(solution)/shard_map/ppermute | solution.py:16
  57.6 4.6 %collective-permute-done.7 = bf16[2,256,512]{2,1,0:T(8,128)(2,1)} collective-permute-done((bf16[2,256,512]{2,1,0:T(8,128)(2,1)S(1)}, bf16[2,256,512]{2,1,0:T(8,128)(2,1)}, u32[]{:S(2)}, u32[]{:S(2)}) %collective-permute-start.7) | collective-permute-done | bytes 524320 | tf_op jit(solution)/shard_map/ppermute | solution.py:16
  62.1 1.1 collective-permute-done.8
  63.3 1.3 add_convert_fusion
  65.3 1.4 collective-permute-start.10
  66.7 2.1 %collective-permute-done.13 = bf16[128,512]{1,0:T(8,128)(2,1)} collective-permute-done((bf16[128,512]{1,0:T(8,128)(2,1)}, bf16[128,512]{1,0:T(8,128)(2,1)}, u32[]{:S(2)}, u32[]{:S(2)}) %collective-permute-start.13) | collective-permute-done | bytes 131104 | tf_op jit(solution)/shard_map/ppermute | solution.py:16
  68.9 1.3 fusion.21.refs_0_
  70.1 2.2 %collective-permute-done.11 = bf16[1,256,512]{2,1,0:T(8,128)(2,1)S(1)} collective-permute-done((bf16[1,256,512]{2,1,0:T(8,128)(2,1)S(1)}, bf16[1,256,512]{2,1,0:T(8,128)(2,1)S(1)}, u32[]{:S(2)}, u32[]{:S(2)}) %collective-permute-start.11) | collective-permute-done | bytes 262176 | tf_op jit(solution)/shard_map/ppermute | solution.py:16
  72.6 1.4 add_bitcast_fusion.1
  74.7 0.9 slice_convert_fusion
  75.5 4.0 %collective-permute-start.21 = (bf16[128,512]{1,0:T(8,128)(2,1)S(1)}, bf16[128,512]{1,0:T(8,128)(2,1)S(1)}, u32[]{:S(2)}, u32[]{:S(2)}) collective-permute-start(bf16[128,512]{1,0:T(8,128)(2,1)S(1)} %fusion.21.refs_0_), channel_id=1, source_target_pairs={{0,6},{1,7},{2,4},{3,5},{4,2},{5,3},{6,0},{7,1},{8,14},{9,15},{10,... | collective-permute-start | bytes 393224 | tf_op jit(solution)/shard_map/ppermute | solution.py:16
  80.6 0.9 fusion.27
  81.5 2.5 %collective-permute-done.21.refs_3_ = bf16[128,512]{1,0:T(8,128)(2,1)S(1)} collective-permute-done((bf16[128,512]{1,0:T(8,128)(2,1)S(1)}, bf16[128,512]{1,0:T(8,128)(2,1)S(1)}, u32[]{:S(2)}, u32[]{:S(2)}) %collective-permute-start.21) | collective-permute-done | bytes 131104 | tf_op jit(solution)/shard_map/ppermute | solution.py:16
  84.0 7.4 %collective-permute-done.20.refs_2_ = bf16[128,512]{1,0:T(8,128)(2,1)S(1)} collective-permute-done((bf16[128,512]{1,0:T(8,128)(2,1)S(1)}, bf16[128,512]{1,0:T(8,128)(2,1)S(1)}, u32[]{:S(2)}, u32[]{:S(2)}) %collective-permute-start.20) | collective-permute-done | bytes 131104 | tf_op jit(solution)/shard_map/ppermute | solution.py:16
  91.4 2.3 %dispatch.2 = bf16[4,400,512]{2,1,0:T(8,128)(2,1)} custom-call(s32[3]{0:T(128)S(1)} %pad_add_fusion.position_ref, s32[8,4,128]{2,1,0:T(4,128)S(1)} %bitcast.101, bf16[16,1024]{1,0:T(8,128)(2,1)S(1)} %fusion.30.extra_ref, bf16[128,512]{1,0:T(8,128)(2,1)S(1)} %fusion.21.refs_0_, bf16[128,512]{1,0:T(8,128)(2,1)S(1)} %collective-permute-done.19.refs_1_, ...), custom_call_target="tpu_custom_call" | custom-call | tf_op jit(solution)/shard_map/dispatch/pallas_call | solution.py:527
  93.7 3.6 %all-to-all-start.3 = ((bf16[4,400,512]{2,1,0:T(8,128)(2,1)}), bf16[4,400,512]{2,1,0:T(8,128)(2,1)S(1)}, u32[]{:S(2)}, u32[]{:S(2)}) async-start(bf16[4,400,512]{2,1,0:T(8,128)(2,1)} %dispatch.2), calls=%async_computation.3 | async-start | bytes 3276800 | tf_op jit(solution)/shard_map/all_to_all | solution.py:575
  97.3 2.5 %collective-permute-start.18 = (bf16[128,512]{1,0:T(8,128)(2,1)}, bf16[128,512]{1,0:T(8,128)(2,1)S(1)}, u32[]{:S(2)}, u32[]{:S(2)}) collective-permute-start(bf16[128,512]{1,0:T(8,128)(2,1)} %get-tuple-element.90), channel_id=1, source_target_pairs={{0,6},{1,7},{2,4},{3,5},{4,2},{5,3},{6,0},{7,1},{8,14},{9,15},{10,... | collective-permute-start | bytes 393224 | tf_op jit(solution)/shard_map/ppermute | solution.py:16
  99.8 1.9 %collective-permute-start.16 = (bf16[128,512]{1,0:T(8,128)(2,1)S(1)}, bf16[128,512]{1,0:T(8,128)(2,1)S(1)}, u32[]{:S(2)}, u32[]{:S(2)}) collective-permute-start(bf16[128,512]{1,0:T(8,128)(2,1)S(1)} %get-tuple-element.92), channel_id=1, source_target_pairs={{0,2},{1,3},{2,0},{3,1},{4,6},{5,7},{6,4},{7,5},{8,10},{9,11},{10,... | collective-permute-start | bytes 393224 | tf_op jit(solution)/shard_map/ppermute | solution.py:16
  101.7 4.1 %collective-permute-done.18 = bf16[128,512]{1,0:T(8,128)(2,1)S(1)} collective-permute-done((bf16[128,512]{1,0:T(8,128)(2,1)}, bf16[128,512]{1,0:T(8,128)(2,1)S(1)}, u32[]{:S(2)}, u32[]{:S(2)}) %collective-permute-start.18) | collective-permute-done | bytes 131104 | tf_op jit(solution)/shard_map/ppermute | solution.py:16
  105.8 4.4 %collective-permute-done.17 = bf16[128,512]{1,0:T(8,128)(2,1)S(1)} collective-permute-done((bf16[128,512]{1,0:T(8,128)(2,1)}, bf16[128,512]{1,0:T(8,128)(2,1)S(1)}, u32[]{:S(2)}, u32[]{:S(2)}) %collective-permute-start.17) | collective-permute-done | bytes 131104 | tf_op jit(solution)/shard_map/ppermute | solution.py:16
  110.2 1.0 fusion.16.refs_0_
  111.3 2.4 %collective-permute-start.24 = (bf16[128,512]{1,0:T(8,128)(2,1)S(1)}, bf16[128,512]{1,0:T(8,128)(2,1)S(1)}, u32[]{:S(2)}, u32[]{:S(2)}) collective-permute-start(bf16[128,512]{1,0:T(8,128)(2,1)S(1)} %fusion.16.refs_0_), channel_id=1, source_target_pairs={{0,6},{1,7},{2,4},{3,5},{4,2},{5,3},{6,0},{7,1},{8,14},{9,15},{10,... | collective-permute-start | bytes 393224 | tf_op jit(solution)/shard_map/ppermute | solution.py:16
  113.7 2.1 %collective-permute-start.22 = (bf16[128,512]{1,0:T(8,128)(2,1)S(1)}, bf16[128,512]{1,0:T(8,128)(2,1)S(1)}, u32[]{:S(2)}, u32[]{:S(2)}) collective-permute-start(bf16[128,512]{1,0:T(8,128)(2,1)S(1)} %fusion.16.refs_0_), channel_id=1, source_target_pairs={{0,2},{1,3},{2,0},{3,1},{4,6},{5,7},{6,4},{7,5},{8,10},{9,11},{10,... | collective-permute-start | bytes 393224 | tf_op jit(solution)/shard_map/ppermute | solution.py:16
  115.7 0.8 signs.1
  116.5 1.1 join.1
  117.6 2.0 %collective-permute-done.24.refs_3_ = bf16[128,512]{1,0:T(8,128)(2,1)S(1)} collective-permute-done((bf16[128,512]{1,0:T(8,128)(2,1)S(1)}, bf16[128,512]{1,0:T(8,128)(2,1)S(1)}, u32[]{:S(2)}, u32[]{:S(2)}) %collective-permute-start.24) | collective-permute-done | bytes 131104 | tf_op jit(solution)/shard_map/ppermute | solution.py:16
  119.6 5.1 %collective-permute-done.23.refs_2_ = bf16[128,512]{1,0:T(8,128)(2,1)S(1)} collective-permute-done((bf16[128,512]{1,0:T(8,128)(2,1)S(1)}, bf16[128,512]{1,0:T(8,128)(2,1)S(1)}, u32[]{:S(2)}, u32[]{:S(2)}) %collective-permute-start.23) | collective-permute-done | bytes 131104 | tf_op jit(solution)/shard_map/ppermute | solution.py:16
  124.7 2.3 %dispatch.3 = bf16[4,400,512]{2,1,0:T(8,128)(2,1)} custom-call(s32[3]{0:T(128)S(1)} %pad_add_fusion.position_ref, s32[8,4,128]{2,1,0:T(4,128)S(1)} %bitcast.103, bf16[16,1024]{1,0:T(8,128)(2,1)S(1)} %fusion.30.extra_ref, bf16[128,512]{1,0:T(8,128)(2,1)S(1)} %fusion.16.refs_0_, bf16[128,512]{1,0:T(8,128)(2,1)S(1)} %collective-permute-done.22.refs_1_, ...), custom_call_target="tpu_custom_call" | custom-call | tf_op jit(solution)/shard_map/dispatch/pallas_call | solution.py:527
  127.0 4.6 %all-to-all-start.2 = ((bf16[4,400,512]{2,1,0:T(8,128)(2,1)}), bf16[4,400,512]{2,1,0:T(8,128)(2,1)}, u32[]{:S(2)}, u32[]{:S(2)}) async-start(bf16[4,400,512]{2,1,0:T(8,128)(2,1)} %dispatch.3), calls=%async_computation.2 | async-start | bytes 3276800 | tf_op jit(solution)/shard_map/all_to_all | solution.py:575
  131.6 3.4 %copy-done.2 = bf16[1,4096,1024]{2,1,0:T(8,128)(2,1)S(1)} copy-done((bf16[1,4096,1024]{2,1,0:T(8,128)(2,1)S(1)}, bf16[1,4096,1024]{2,1,0:T(8,128)(2,1)}, u32[]{:S(2)}) %copy-start.2) | copy-done | bytes 8388632
  135.0 12.3 %early.1 = (f32[768,1024]{1,0:T(8,128)S(1)}, f32[768,1024]{1,0:T(8,128)S(1)}, f32[768,16]{1,0:T(8,128)S(1)}, bf16[4,512,768]{2,1,0:T(8,128)(2,1)S(1)}) custom-call(bf16[4,400,512]{2,1,0:T(8,128)(2,1)S(1)} %all-to-all-done.3.own_ref, bf16[4,400,512]{2,1,0:T(8,128)(2,1)} %collective-permute-done.25.other_ref, bf16[4,2,512,1024]{3,2,1,0:T(8,128)(2,1)S(1)} %bitcast.94, ...), custom_call_target="tpu_custom_call" | custom-call | flops 6442450944 | bytes 8388608 | tf_op jit(solution)/shard_map/early/pallas_call | solution.py:588
  147.3 1.7 copy-done.3
  149.0 1.7 copy-done.4
  150.7 1.6 copy-done.5
  153.5 3.3 %collective-permute-done.26.other_ref = bf16[4,400,512]{2,1,0:T(8,128)(2,1)S(1)} collective-permute-done((bf16[4,400,512]{2,1,0:T(8,128)(2,1)}, bf16[4,400,512]{2,1,0:T(8,128)(2,1)S(1)}, u32[]{:S(2)}, u32[]{:S(2)}) %collective-permute-start.26) | collective-permute-done | bytes 1638432 | tf_op jit(solution)/shard_map/ppermute | solution.py:16
  156.9 1.2 copy-done.10
  158.1 32.3 %late.1 = (bf16[4,2,96,1024]{3,2,1,0:T(8,128)(2,1)}, bf16[4,1024,1024]{2,1,0:T(8,128)(2,1)}, bf16[4,1024,1024]{2,1,0:T(8,128)(2,1)}) custom-call(s32[3]{0:T(128)} %copy-done.8, bf16[4,400,512]{2,1,0:T(8,128)(2,1)} %all-to-all-done.2.own_ref, bf16[4,400,512]{2,1,0:T(8,128)(2,1)} %copy-done.10, bf16[4,512,768]{2,1,0:T(8,128)(2,1)} %copy-done.5, ...), custom_call_target="tpu_custom_call" | custom-call | tf_op jit(solution)/shard_map/late/pallas_call | solution.py:627
  (75 shorter events, 6.2 us)
Async XLA Ops:
  0.6 10.5 %all-to-all-start = ((bf16[4,32,1024]{2,1,0:T(8,128)(2,1)}), bf16[4,32,1024]{2,1,0:T(8,128)(2,1)S(1)}, u32[]{:S(2)}, u32[]{:S(2)}) async-start(bf16[4,32,1024]{2,1,0:T(8,128)(2,1)} %bitcast.110), calls=%async_computation | async-start | bytes 524288 | tf_op jit(solution)/shard_map/all_to_all | solution.py:448
  5.9 118.8 %copy-start.8 = (s32[3]{0:T(128)}, s32[3]{0:T(128)S(1)}, u32[]{:S(2)}) copy-start(s32[3]{0:T(128)S(1)} %pad_add_fusion.position_ref) | copy-start | bytes 40
  5.9 2.2 %copy-start = (bf16[1,512,4096]{2,1,0:T(8,128)(2,1)S(1)}, bf16[1,512,4096]{2,1,0:T(8,128)(2,1)}, u32[]{:S(2)}) copy-start(bf16[1,512,4096]{2,1,0:T(8,128)(2,1)} %param.10) | copy-start | bytes 12582916
  8.1 4.9 %copy-start.19 = (s32[128,2]{0,1:T(2,128)S(1)}, s32[128,2]{0,1:T(2,128)}, u32[]{:S(2)}) copy-start(s32[128,2]{0,1:T(2,128)} %param.17) | copy-start | bytes 3076
  8.1 4.9 %copy-start.20 = (s32[128,2]{0,1:T(2,128)S(1)}, s32[128,2]{0,1:T(2,128)}, u32[]{:S(2)}) copy-start(s32[128,2]{0,1:T(2,128)} %param.18) | copy-start | bytes 3076
  11.2 12.3 %collective-permute-start = (bf16[2,256,512]{2,1,0:T(8,128)(2,1)S(1)}, bf16[2,256,512]{2,1,0:T(8,128)(2,1)S(1)}, u32[]{:S(2)}, u32[]{:S(2)}) collective-permute-start(bf16[2,256,512]{2,1,0:T(8,128)(2,1)S(1)} %get-tuple-element.45), channel_id=1, source_target_pairs={{0,8},{8,0},{16,24},{24,16},{1,9},{9,1},{17,25},{25,17},{2,10},{10... | collective-permute-start | bytes 1572872 | tf_op jit(solution)/shard_map/ppermute | solution.py:16
  12.4 12.0 %collective-permute-start.1 = (bf16[2,256,512]{2,1,0:T(8,128)(2,1)S(1)}, bf16[2,256,512]{2,1,0:T(8,128)(2,1)S(1)}, u32[]{:S(2)}, u32[]{:S(2)}) collective-permute-start(bf16[2,256,512]{2,1,0:T(8,128)(2,1)S(1)} %get-tuple-element.46), channel_id=1, source_target_pairs={{0,16},{8,24},{16,0},{24,8},{1,17},{9,25},{17,1},{25,9},{2,18},{10... | collective-permute-start | bytes 1572872 | tf_op jit(solution)/shard_map/ppermute | solution.py:16
  13.8 17.4 %all-to-all-start.1 = ((bf16[8,48,512]{2,1,0:T(8,128)(2,1)}), bf16[8,48,512]{2,1,0:T(8,128)(2,1)S(1)}, u32[]{:S(2)}, u32[]{:S(2)}) async-start(bf16[8,48,512]{2,1,0:T(8,128)(2,1)} %spread.1), calls=%async_computation.1 | async-start | bytes 786432 | tf_op jit(solution)/shard_map/all_to_all | solution.py:464
  23.4 4.7 %copy-start.12 = (bf16[2,256,512]{2,1,0:T(8,128)(2,1)}, bf16[2,256,512]{2,1,0:T(8,128)(2,1)S(1)}, u32[]{:S(2)}) copy-start(bf16[2,256,512]{2,1,0:T(8,128)(2,1)S(1)} %collective-permute-done) | copy-start | bytes 1572868
  24.4 3.7 %copy-start.14 = (bf16[2,256,512]{2,1,0:T(8,128)(2,1)}, bf16[2,256,512]{2,1,0:T(8,128)(2,1)S(1)}, u32[]{:S(2)}) copy-start(bf16[2,256,512]{2,1,0:T(8,128)(2,1)S(1)} %collective-permute-done.1) | copy-start | bytes 1572868
  25.8 6.4 %collective-permute-start.3 = (bf16[1,256,512]{2,1,0:T(8,128)(2,1)S(1)}, bf16[1,256,512]{2,1,0:T(8,128)(2,1)S(1)}, u32[]{:S(2)}, u32[]{:S(2)}) collective-permute-start(bf16[1,256,512]{2,1,0:T(8,128)(2,1)S(1)} %get-tuple-element.88), channel_id=1, source_target_pairs={{0,8},{8,0},{16,24},{24,16},{1,9},{9,1},{17,25},{25,17},{2,10},{10... | collective-permute-start | bytes 786440 | tf_op jit(solution)/shard_map/ppermute | solution.py:16
  26.6 6.4 %collective-permute-start.2 = (bf16[1,256,512]{2,1,0:T(8,128)(2,1)S(1)}, bf16[1,256,512]{2,1,0:T(8,128)(2,1)S(1)}, u32[]{:S(2)}, u32[]{:S(2)}) collective-permute-start(bf16[1,256,512]{2,1,0:T(8,128)(2,1)S(1)} %get-tuple-element.89), channel_id=1, source_target_pairs={{0,16},{8,24},{16,0},{24,8},{1,17},{9,25},{17,1},{25,9},{2,18},{10... | collective-permute-start | bytes 786440 | tf_op jit(solution)/shard_map/ppermute | solution.py:16
  28.1 2.2 %copy-start.1 = (bf16[1,512,4096]{2,1,0:T(8,128)(2,1)S(1)}, bf16[1,512,4096]{2,1,0:T(8,128)(2,1)}, u32[]{:S(2)}) copy-start(bf16[1,512,4096]{2,1,0:T(8,128)(2,1)} %param.10) | copy-start | bytes 12582916
  30.3 6.3 %copy-start.13 = (bf16[2,256,512]{2,1,0:T(8,128)(2,1)S(1)}, bf16[2,256,512]{2,1,0:T(8,128)(2,1)}, u32[]{:S(2)}) copy-start(bf16[2,256,512]{2,1,0:T(8,128)(2,1)} %copy-done.12) | copy-start | bytes 1572868
  31.3 4.5 %copy-start.11 = (bf16[8,48,512]{2,1,0:T(8,128)(2,1)}, bf16[8,48,512]{2,1,0:T(8,128)(2,1)S(1)}, u32[]{:S(2)}) copy-start(bf16[8,48,512]{2,1,0:T(8,128)(2,1)S(1)} %all-to-all-done.1) | copy-start | bytes 1179652
  33.0 2.8 %copy-start.16 = (bf16[1,256,512]{2,1,0:T(8,128)(2,1)}, bf16[1,256,512]{2,1,0:T(8,128)(2,1)S(1)}, u32[]{:S(2)}) copy-start(bf16[1,256,512]{2,1,0:T(8,128)(2,1)S(1)} %collective-permute-done.2) | copy-start | bytes 786436
  33.0 10.0 %collective-permute-start.6 = (bf16[8,32,512]{2,1,0:T(8,128)(2,1)S(1)}, bf16[8,32,512]{2,1,0:T(8,128)(2,1)S(1)}, u32[]{:S(2)}, u32[]{:S(2)}) collective-permute-start(bf16[8,32,512]{2,1,0:T(8,128)(2,1)S(1)} %slice.18), channel_id=1, source_target_pairs={{0,24},{8,16},{16,8},{24,0},{1,25},{9,17},{17,9},{25,1},{2,26},{10... | collective-permute-start | bytes 786440 | tf_op jit(solution)/shard_map/ppermute | solution.py:16
  34.7 11.1 %collective-permute-start.5 = (bf16[8,32,512]{2,1,0:T(8,128)(2,1)S(1)}, bf16[8,32,512]{2,1,0:T(8,128)(2,1)S(1)}, u32[]{:S(2)}, u32[]{:S(2)}) collective-permute-start(bf16[8,32,512]{2,1,0:T(8,128)(2,1)S(1)} %slice.18), channel_id=1, source_target_pairs={{0,16},{8,24},{16,0},{24,8},{1,17},{9,25},{17,1},{25,9},{2,18},{10... | collective-permute-start | bytes 786440 | tf_op jit(solution)/shard_map/ppermute | solution.py:16
  35.8 10.0 %collective-permute-start.4 = (bf16[8,32,512]{2,1,0:T(8,128)(2,1)S(1)}, bf16[8,32,512]{2,1,0:T(8,128)(2,1)S(1)}, u32[]{:S(2)}, u32[]{:S(2)}) collective-permute-start(bf16[8,32,512]{2,1,0:T(8,128)(2,1)S(1)} %slice.18), channel_id=1, source_target_pairs={{0,8},{8,0},{16,24},{24,16},{1,9},{9,1},{17,25},{25,17},{2,10},{10... | collective-permute-start | bytes 786440 | tf_op jit(solution)/shard_map/ppermute | solution.py:16
  46.4 20.3 %copy-start.17 = (bf16[1024]{0:T(1024)(128)(2,1)S(1)}, bf16[1024]{0:T(1024)(128)(2,1)}, u32[]{:S(2)}) copy-start(bf16[1024]{0:T(1024)(128)(2,1)} %param.13) | copy-start | bytes 6148
  46.4 22.4 %copy-start.15 = (bf16[128,1024]{1,0:T(8,128)(2,1)S(1)}, bf16[128,1024]{1,0:T(8,128)(2,1)}, u32[]{:S(2)}) copy-start(bf16[128,1024]{1,0:T(8,128)(2,1)} %param.12) | copy-start | bytes 786436
  47.7 2.2 %collective-permute-start.9 = (bf16[4,128,512]{2,1,0:T(8,128)(2,1)}, bf16[4,128,512]{2,1,0:T(8,128)(2,1)S(1)}, u32[]{:S(2)}, u32[]{:S(2)}) collective-permute-start(bf16[4,128,512]{2,1,0:T(8,128)(2,1)} %convolution_convert_fusion.1), channel_id=1, source_target_pairs={{0,1},{1,0},{2,3},{3,2},{4,5},{5,4},{6,7},{7,6},{8,9},{9,8},{10,11... | collective-permute-start | bytes 1572872 | tf_op jit(solution)/shard_map/ppermute | solution.py:16
  47.7 14.4 %collective-permute-start.7 = (bf16[2,256,512]{2,1,0:T(8,128)(2,1)S(1)}, bf16[2,256,512]{2,1,0:T(8,128)(2,1)}, u32[]{:S(2)}, u32[]{:S(2)}) collective-permute-start(bf16[2,256,512]{2,1,0:T(8,128)(2,1)S(1)} %get-tuple-element.54), channel_id=1, source_target_pairs={{0,8},{8,0},{16,24},{24,16},{1,9},{9,1},{17,25},{25,17},{2,10},{10... | collective-permute-start | bytes 1572872 | tf_op jit(solution)/shard_map/ppermute | solution.py:16
  49.1 14.2 %collective-permute-start.8 = (bf16[2,256,512]{2,1,0:T(8,128)(2,1)S(1)}, bf16[2,256,512]{2,1,0:T(8,128)(2,1)}, u32[]{:S(2)}, u32[]{:S(2)}) collective-permute-start(bf16[2,256,512]{2,1,0:T(8,128)(2,1)S(1)} %get-tuple-element.55), channel_id=1, source_target_pairs={{0,16},{8,24},{16,0},{24,8},{1,17},{9,25},{17,1},{25,9},{2,18},{10... | collective-permute-start | bytes 1572872 | tf_op jit(solution)/shard_map/ppermute | solution.py:16
  53.1 13.6 %collective-permute-start.14 = (bf16[128,512]{1,0:T(8,128)(2,1)}, bf16[128,512]{1,0:T(8,128)(2,1)}, u32[]{:S(2)}, u32[]{:S(2)}) collective-permute-start(bf16[128,512]{1,0:T(8,128)(2,1)} %get-tuple-element.93), channel_id=1, source_target_pairs={{0,6},{1,7},{2,4},{3,5},{4,2},{5,3},{6,0},{7,1},{8,14},{9,15},{10,... | collective-permute-start | bytes 393224 | tf_op jit(solution)/shard_map/ppermute | solution.py:16
  57.0 11.8 %collective-permute-start.13 = (bf16[128,512]{1,0:T(8,128)(2,1)}, bf16[128,512]{1,0:T(8,128)(2,1)}, u32[]{:S(2)}, u32[]{:S(2)}) collective-permute-start(bf16[128,512]{1,0:T(8,128)(2,1)} %get-tuple-element.94), channel_id=1, source_target_pairs={{0,4},{1,5},{2,6},{3,7},{4,0},{5,1},{6,2},{7,3},{8,12},{9,13},{10,... | collective-permute-start | bytes 393224 | tf_op jit(solution)/shard_map/ppermute | solution.py:16
  57.0 11.8 %collective-permute-start.12 = (bf16[128,512]{1,0:T(8,128)(2,1)}, bf16[128,512]{1,0:T(8,128)(2,1)}, u32[]{:S(2)}, u32[]{:S(2)}) collective-permute-start(bf16[128,512]{1,0:T(8,128)(2,1)} %get-tuple-element.95), channel_id=1, source_target_pairs={{0,2},{1,3},{2,0},{3,1},{4,6},{5,7},{6,4},{7,5},{8,10},{9,11},{10,... | collective-permute-start | bytes 393224 | tf_op jit(solution)/shard_map/ppermute | solution.py:16
  64.6 7.7 %collective-permute-start.11 = (bf16[1,256,512]{2,1,0:T(8,128)(2,1)S(1)}, bf16[1,256,512]{2,1,0:T(8,128)(2,1)S(1)}, u32[]{:S(2)}, u32[]{:S(2)}) collective-permute-start(bf16[1,256,512]{2,1,0:T(8,128)(2,1)S(1)} %get-tuple-element.84), channel_id=1, source_target_pairs={{0,8},{8,0},{16,24},{24,16},{1,9},{9,1},{17,25},{25,17},{2,10},{10... | collective-permute-start | bytes 786440 | tf_op jit(solution)/shard_map/ppermute | solution.py:16
  65.3 7.3 %collective-permute-start.10 = (bf16[1,256,512]{2,1,0:T(8,128)(2,1)S(1)}, bf16[1,256,512]{2,1,0:T(8,128)(2,1)S(1)}, u32[]{:S(2)}, u32[]{:S(2)}) collective-permute-start(bf16[1,256,512]{2,1,0:T(8,128)(2,1)S(1)} %get-tuple-element.85), channel_id=1, source_target_pairs={{0,16},{8,24},{16,0},{24,8},{1,17},{9,25},{17,1},{25,9},{2,18},{10... | collective-permute-start | bytes 786440 | tf_op jit(solution)/shard_map/ppermute | solution.py:16
  68.8 5.8 %copy-start.18 = (bf16[1024,4]{0,1:T(4,128)(2,1)S(1)}, bf16[1024,4]{0,1:T(4,128)(2,1)}, u32[]{:S(2)}) copy-start(bf16[1024,4]{0,1:T(4,128)(2,1)} %param.14) | copy-start | bytes 24580
  74.6 5.6 %collective-permute-start.15 = (bf16[4,128,512]{2,1,0:T(8,128)(2,1)S(1)}, bf16[4,128,512]{2,1,0:T(8,128)(2,1)S(1)}, u32[]{:S(2)}, u32[]{:S(2)}) collective-permute-start(bf16[4,128,512]{2,1,0:T(8,128)(2,1)S(1)} %convolution_convert_fusion), channel_id=1, source_target_pairs={{0,1},{1,0},{2,3},{3,2},{4,5},{5,4},{6,7},{7,6},{8,9},{9,8},{10,11... | collective-permute-start | bytes 1572872 | tf_op jit(solution)/shard_map/ppermute | solution.py:16
  75.5 8.4 %collective-permute-start.21 = (bf16[128,512]{1,0:T(8,128)(2,1)S(1)}, bf16[128,512]{1,0:T(8,128)(2,1)S(1)}, u32[]{:S(2)}, u32[]{:S(2)}) collective-permute-start(bf16[128,512]{1,0:T(8,128)(2,1)S(1)} %fusion.21.refs_0_), channel_id=1, source_target_pairs={{0,6},{1,7},{2,4},{3,5},{4,2},{5,3},{6,0},{7,1},{8,14},{9,15},{10,... | collective-permute-start | bytes 393224 | tf_op jit(solution)/shard_map/ppermute | solution.py:16
  79.5 11.9 %collective-permute-start.20 = (bf16[128,512]{1,0:T(8,128)(2,1)S(1)}, bf16[128,512]{1,0:T(8,128)(2,1)S(1)}, u32[]{:S(2)}, u32[]{:S(2)}) collective-permute-start(bf16[128,512]{1,0:T(8,128)(2,1)S(1)} %fusion.21.refs_0_), channel_id=1, source_target_pairs={{0,4},{1,5},{2,6},{3,7},{4,0},{5,1},{6,2},{7,3},{8,12},{9,13},{10,... | collective-permute-start | bytes 393224 | tf_op jit(solution)/shard_map/ppermute | solution.py:16
  79.5 11.9 %collective-permute-start.19 = (bf16[128,512]{1,0:T(8,128)(2,1)S(1)}, bf16[128,512]{1,0:T(8,128)(2,1)S(1)}, u32[]{:S(2)}, u32[]{:S(2)}) collective-permute-start(bf16[128,512]{1,0:T(8,128)(2,1)S(1)} %fusion.21.refs_0_), channel_id=1, source_target_pairs={{0,2},{1,3},{2,0},{3,1},{4,6},{5,7},{6,4},{7,5},{8,10},{9,11},{10,... | collective-permute-start | bytes 393224 | tf_op jit(solution)/shard_map/ppermute | solution.py:16
  80.6 13.1 %copy-start.9 = (f32[4,128,512]{2,1,0:T(8,128)}, f32[4,128,512]{2,1,0:T(8,128)S(1)}, u32[]{:S(2)}) copy-start(f32[4,128,512]{2,1,0:T(8,128)S(1)} %convert_add_fusion) | copy-start | bytes 3145732
  93.7 33.3 %all-to-all-start.3 = ((bf16[4,400,512]{2,1,0:T(8,128)(2,1)}), bf16[4,400,512]{2,1,0:T(8,128)(2,1)S(1)}, u32[]{:S(2)}, u32[]{:S(2)}) async-start(bf16[4,400,512]{2,1,0:T(8,128)(2,1)} %dispatch.2), calls=%async_computation.3 | async-start | bytes 3276800 | tf_op jit(solution)/shard_map/all_to_all | solution.py:575
  97.3 8.5 %collective-permute-start.18 = (bf16[128,512]{1,0:T(8,128)(2,1)}, bf16[128,512]{1,0:T(8,128)(2,1)S(1)}, u32[]{:S(2)}, u32[]{:S(2)}) collective-permute-start(bf16[128,512]{1,0:T(8,128)(2,1)} %get-tuple-element.90), channel_id=1, source_target_pairs={{0,6},{1,7},{2,4},{3,5},{4,2},{5,3},{6,0},{7,1},{8,14},{9,15},{10,... | collective-permute-start | bytes 393224 | tf_op jit(solution)/shard_map/ppermute | solution.py:16
  99.8 10.4 %collective-permute-start.17 = (bf16[128,512]{1,0:T(8,128)(2,1)}, bf16[128,512]{1,0:T(8,128)(2,1)S(1)}, u32[]{:S(2)}, u32[]{:S(2)}) collective-permute-start(bf16[128,512]{1,0:T(8,128)(2,1)} %get-tuple-element.91), channel_id=1, source_target_pairs={{0,4},{1,5},{2,6},{3,7},{4,0},{5,1},{6,2},{7,3},{8,12},{9,13},{10,... | collective-permute-start | bytes 393224 | tf_op jit(solution)/shard_map/ppermute | solution.py:16
  99.8 10.4 %collective-permute-start.16 = (bf16[128,512]{1,0:T(8,128)(2,1)S(1)}, bf16[128,512]{1,0:T(8,128)(2,1)S(1)}, u32[]{:S(2)}, u32[]{:S(2)}) collective-permute-start(bf16[128,512]{1,0:T(8,128)(2,1)S(1)} %get-tuple-element.92), channel_id=1, source_target_pairs={{0,2},{1,3},{2,0},{3,1},{4,6},{5,7},{6,4},{7,5},{8,10},{9,11},{10,... | collective-permute-start | bytes 393224 | tf_op jit(solution)/shard_map/ppermute | solution.py:16
  111.3 8.3 %collective-permute-start.24 = (bf16[128,512]{1,0:T(8,128)(2,1)S(1)}, bf16[128,512]{1,0:T(8,128)(2,1)S(1)}, u32[]{:S(2)}, u32[]{:S(2)}) collective-permute-start(bf16[128,512]{1,0:T(8,128)(2,1)S(1)} %fusion.16.refs_0_), channel_id=1, source_target_pairs={{0,6},{1,7},{2,4},{3,5},{4,2},{5,3},{6,0},{7,1},{8,14},{9,15},{10,... | collective-permute-start | bytes 393224 | tf_op jit(solution)/shard_map/ppermute | solution.py:16
  113.6 11.1 %collective-permute-start.23 = (bf16[128,512]{1,0:T(8,128)(2,1)S(1)}, bf16[128,512]{1,0:T(8,128)(2,1)S(1)}, u32[]{:S(2)}, u32[]{:S(2)}) collective-permute-start(bf16[128,512]{1,0:T(8,128)(2,1)S(1)} %fusion.16.refs_0_), channel_id=1, source_target_pairs={{0,4},{1,5},{2,6},{3,7},{4,0},{5,1},{6,2},{7,3},{8,12},{9,13},{10,... | collective-permute-start | bytes 393224 | tf_op jit(solution)/shard_map/ppermute | solution.py:16
  113.7 11.1 %collective-permute-start.22 = (bf16[128,512]{1,0:T(8,128)(2,1)S(1)}, bf16[128,512]{1,0:T(8,128)(2,1)S(1)}, u32[]{:S(2)}, u32[]{:S(2)}) collective-permute-start(bf16[128,512]{1,0:T(8,128)(2,1)S(1)} %fusion.16.refs_0_), channel_id=1, source_target_pairs={{0,2},{1,3},{2,0},{3,1},{4,6},{5,7},{6,4},{7,5},{8,10},{9,11},{10,... | collective-permute-start | bytes 393224 | tf_op jit(solution)/shard_map/ppermute | solution.py:16
  116.5 1.1 copy-start.6
  127.0 4.6 %collective-permute-start.25 = (bf16[4,400,512]{2,1,0:T(8,128)(2,1)S(1)}, bf16[4,400,512]{2,1,0:T(8,128)(2,1)}, u32[]{:S(2)}, u32[]{:S(2)}) collective-permute-start(bf16[4,400,512]{2,1,0:T(8,128)(2,1)S(1)} %all-to-all-done.3.own_ref), channel_id=1, source_target_pairs={{0,1},{1,0},{2,3},{3,2},{4,5},{5,4},{6,7},{7,6},{8,9},{9,8},{10,11... | collective-permute-start | bytes 4915208 | tf_op jit(solution)/shard_map/ppermute | solution.py:16
  127.0 26.0 %all-to-all-start.2 = ((bf16[4,400,512]{2,1,0:T(8,128)(2,1)}), bf16[4,400,512]{2,1,0:T(8,128)(2,1)}, u32[]{:S(2)}, u32[]{:S(2)}) async-start(bf16[4,400,512]{2,1,0:T(8,128)(2,1)} %dispatch.3), calls=%async_computation.2 | async-start | bytes 3276800 | tf_op jit(solution)/shard_map/all_to_all | solution.py:575
  131.6 3.4 %copy-start.2 = (bf16[1,4096,1024]{2,1,0:T(8,128)(2,1)S(1)}, bf16[1,4096,1024]{2,1,0:T(8,128)(2,1)}, u32[]{:S(2)}) copy-start(bf16[1,4096,1024]{2,1,0:T(8,128)(2,1)} %param.15) | copy-start | bytes 25165828
  147.3 1.7 copy-start.3
  148.9 1.7 copy-start.4
  150.7 1.6 copy-start.5
  152.3 0.7 copy-start.7
  153.0 3.9 %collective-permute-start.26 = (bf16[4,400,512]{2,1,0:T(8,128)(2,1)}, bf16[4,400,512]{2,1,0:T(8,128)(2,1)S(1)}, u32[]{:S(2)}, u32[]{:S(2)}) collective-permute-start(bf16[4,400,512]{2,1,0:T(8,128)(2,1)} %all-to-all-done.2.own_ref), channel_id=1, source_target_pairs={{0,1},{1,0},{2,3},{3,2},{4,5},{5,4},{6,7},{7,6},{8,9},{9,8},{10,11... | collective-permute-start | bytes 4915208 | tf_op jit(solution)/shard_map/ppermute | solution.py:16
  156.9 1.2 copy-start.10
